TPU v7x, 512 devices: a whole 4x4x16 slice. The times are simulated.
512 devices in a mesh: rep: 8 (over x_lo, y), fsdp: 64 (over x_hi, z, core).
Axes of the slice: x: 4 (x_hi: 2, x_lo: 2; x = x_hi * 2 + x_lo), y: 4, z: 16, core: 2. Of those that a mesh axis runs over, the one named last changes fastest.
Arguments:
- hidden: bfloat16 [131072, 5120], P(('rep', 'fsdp')), may hold values from -6 to 6
- weight: bfloat16 [640, 64, 128], P('fsdp'), may hold values from -0.078125 to 0.078125
- momentum: float32 [8, 640, 64, 128], P('rep', 'fsdp'), may hold values from -6 to 6
- gradient: bfloat16 [8, 640, 64, 128], P('rep', 'fsdp'), may hold values from -6 to 6
- indices: int32 [8, 1280, 32], P('rep', 'fsdp'), may hold values from 0 to 4095, as said below
- counts: int32 [8, 1280], P('rep', 'fsdp'), may hold values from 1 to 32, as said below
Outputs:
- key_states: bfloat16 [131072, 1024], P(('rep', 'fsdp'))
- update: bfloat16 [640, 64, 128], P('fsdp', 'rep')
- new_momentum: float32 [8, 640, 64, 128], P('rep', 'fsdp')
Inputs may be any that keep to these rules, and one draw needn't show every extreme that they name: `indices`: the 32 numbers of one replica's block differ from one another. `counts`: some block of every replica keeps all 32.
All inputs are finite; a program needn't handle non-finite values.
Results may differ from a plain program's by a relative error of at most 0.0095.
Values may be sent and summed in bfloat16 or wider, within the bound.
No kernel may reach another device: no remote copies, remote signals or barrier semaphores. Data moves between devices by JAX's collectives and lax.ppermute only.
A program may use at most 128 MiB of HBM per device.

v0:
```python
import jax
import jax.numpy as jnp
from jax import lax
from jax.sharding import PartitionSpec as P

decay_rate = 0.999
step_size = 0.01
tiny_eps = 1e-06
finest_numeric_accuracy = lax.Precision.HIGHEST


def dct_table(length):
    wave_number = jnp.arange(length, dtype=jnp.float32)[:, None]
    position = jnp.arange(length, dtype=jnp.float32)[None, :]
    dct_rows = jnp.cos(jnp.pi * (2.0 * position + 1.0) * wave_number / (2.0 * length)) * jnp.sqrt(
        2.0 / length
    )
    return jnp.where(wave_number == 0.0, dct_rows * jnp.sqrt(0.5), dct_rows)


def make_pair(dct_rows):
    empty_square_tile = jnp.zeros_like(dct_rows)
    upper_half = jnp.concatenate([dct_rows, empty_square_tile], axis=1)
    lower_half = jnp.concatenate([empty_square_tile, dct_rows], axis=1)
    return jnp.concatenate([upper_half, lower_half], axis=0)


def to_spectrum(tile_data, row_basis_operator, paired_cosine_matrix):
    partial_transform = jnp.einsum(
        "ka,tab->tkb", row_basis_operator, tile_data, precision=finest_numeric_accuracy
    )
    return jnp.einsum(
        "tkb,cb->tkc", partial_transform, paired_cosine_matrix, precision=finest_numeric_accuracy
    )


def from_spectrum(tile_frequency_coefficients, row_basis_operator, paired_cosine_matrix):
    partial_transform = jnp.einsum(
        "yh,kyi->khi",
        row_basis_operator,
        tile_frequency_coefficients,
        precision=finest_numeric_accuracy,
    )
    return jnp.einsum(
        "pln,ns->pls", partial_transform, paired_cosine_matrix, precision=finest_numeric_accuracy
    )


def shards(hidden, weight, momentum, gradient, indices, counts):
    tiles_dev, block_side, tile_cols = weight.shape
    kept_count = indices.shape[2]
    replicas = lax.axis_size("rep")
    group_size = lax.axis_size("fsdp")
    all_tiles = tiles_dev * group_size
    width = hidden.shape[1]
    dct_rows = dct_table(block_side)
    paired_cosine_matrix = make_pair(dct_rows)
    moment = decay_rate * momentum[0] + gradient[0].astype(jnp.float32)
    tile_frequency_coefficients = to_spectrum(moment, dct_rows, paired_cosine_matrix)
    span_ids = jnp.arange(2 * tiles_dev, dtype=jnp.int32)[:, None]
    places = (
        span_ids // 2 * (block_side * tile_cols)
        + indices[0] // block_side * tile_cols
        + span_ids % 2 * block_side
        + indices[0] % block_side
    )
    picked = tile_frequency_coefficients.reshape(-1)[places]
    is_live = jnp.arange(kept_count, dtype=jnp.int32)[None, :] < counts[0][:, None]
    kept_values = jnp.where(is_live, picked, jnp.zeros_like(picked))
    flat_size = tiles_dev * block_side * tile_cols
    own_spectra = (
        jnp.zeros((flat_size,), jnp.float32).at[places.reshape(-1)].add(kept_values.reshape(-1))
    )
    own_spectra = own_spectra.reshape(tiles_dev, block_side, tile_cols)
    new_momentum = (moment - from_spectrum(own_spectra, dct_rows, paired_cosine_matrix))[None]
    all_places, all_values = (
        lax.all_gather(places[None], "rep", axis=0, tiled=True),
        lax.all_gather(kept_values[None], "rep", axis=0, tiled=True),
    )
    shared = (
        jnp.zeros((flat_size,), jnp.float32).at[all_places.reshape(-1)].add(all_values.reshape(-1))
    )
    shared = shared.reshape(tiles_dev, block_side, tile_cols) / replicas
    energy = jnp.sum((shared * shared).reshape(tiles_dev, block_side, 2, block_side), axis=(1, 3))
    span_scale = jnp.sqrt(energy / (block_side * block_side) + tiny_eps)
    span_scale = jnp.repeat(span_scale, block_side, axis=1)[:, None, :]
    rows_rep = block_side // replicas
    row_first = lax.axis_index("rep") * rows_rep
    raw_descent_direction = from_spectrum(shared, dct_rows, paired_cosine_matrix)
    update = jnp.tanh(raw_descent_direction / span_scale).astype(jnp.bfloat16)
    revised_parameters = (
        weight.astype(jnp.float32) - step_size * update.astype(jnp.float32)
    ).astype(jnp.bfloat16)
    assembled = lax.all_gather(revised_parameters, "fsdp", axis=0, tiled=True)
    out_update = lax.dynamic_slice_in_dim(update, row_first, rows_rep, 1)
    out_blocks = all_tiles // (width // block_side)
    matrix = assembled.reshape(out_blocks, width // block_side, block_side, tile_cols).transpose(
        1, 2, 0, 3
    )
    matrix = matrix.reshape(width, out_blocks * tile_cols)
    key_states = jnp.dot(hidden, matrix, preferred_element_type=jnp.float32).astype(jnp.bfloat16)
    return (key_states, out_update, new_momentum)


def solution(mesh):
    in_specs = (
        P(("rep", "fsdp"), None),
        P("fsdp", None, None),
        P("rep", "fsdp", None, None),
        P("rep", "fsdp", None, None),
        P("rep", "fsdp", None),
        P("rep", "fsdp"),
    )
    out_specs = (P(("rep", "fsdp"), None), P("fsdp", "rep", None), P("rep", "fsdp", None, None))
    return jax.shard_map(shards, mesh=mesh, in_specs=in_specs, out_specs=out_specs, check_vma=False)
```

profile of v0, /device:TPU:1, one launch (start us, length us, event | category | flops | bytes accessed | tf_op | source)
XLA Modules:
  0.0 328.4 jit_solution(6481195896005296669)
XLA Ops:
  7.3 1.0 fusion.44
  8.3 0.8 fusion.36
  9.1 0.1 multiply_select_fusion
  9.3 1.7 convolution_bitcast_fusion.2
  11.0 0.5 fusion.21
  11.5 3.9 %gather_fusion = f32[640]{0:T(1024)S(1)} fusion(f32[81920]{0:T(1024)S(1)} %bitcast.67, s32[1024]{0:T(1024)S(1)} %pad_clamp_fusion), kind=kCustom, calls=%fused_computation | custom fusion | bytes 7680 | tf_op jit(solution)/shard_map/gather | solution.py:67
  15.4 0.1 fusion.40
  15.5 23.2 %all_gather.10 = f32[8,20,32]{2,1,0:T(8,128)S(1)} all-gather(f32[1,20,32]{2,1,0:T(8,128)S(1)} %fusion.40), channel_id=1, replica_groups=mesh['rep'=8,'fsdp'=64] {'rep'}, dimensions={0}, use_global_device_ids=true | all-gather | bytes 23040 | tf_op jit(solution)/shard_map/all_gather | solution.py:78
  38.7 0.1 reshape.508
  38.8 21.8 %all_gather.9 = s32[8,20,32]{2,1,0:T(8,128)S(1)} all-gather(s32[1,20,32]{2,1,0:T(8,128)S(1)} %fusion.36), channel_id=1, replica_groups=mesh['rep'=8,'fsdp'=64] {'rep'}, dimensions={0}, use_global_device_ids=true | all-gather | bytes 23040 | tf_op jit(solution)/shard_map/all_gather | solution.py:77
  60.6 0.1 reshape.490
  60.7 27.3 %scatter_custom_fusion = f32[81920]{0:T(1024)S(1)} fusion(s32[5120]{0:T(1024)S(1)} %bitcast.72, f32[5120]{0:T(1024)S(1)} %reshape.508, f32[]{:T(128)} %constant.86.clone.1), kind=kCustom, calls=%fused_computation.23 | custom fusion | flops 5120 | bytes 327684 | tf_op jit(solution)/shard_map/scatter-add | solution.py:81
  88.1 0.8 fusion.68
  88.8 1.3 convolution_bitcast_fusion.1
  90.2 1.4 mul.200
  91.5 0.4 reduce_sum.9
  91.9 0.1 broadcast_in_dim.39
  92.0 0.1 div.88
  92.1 2.2 subtract_convert_fusion
  94.4 0.1 fusion.41
  94.5 0.1 reshape.516
  94.6 0.1 add.257
  94.8 0.1 add.260
  94.8 0.1 squeeze.9
  95.0 4.9 %scatter_custom_fusion.1 = f32[81920]{0:T(1024)S(1)} fusion(s32[640]{0:T(1024)S(1)} %fusion.46, f32[640]{0:T(1024)S(1)} %reshape.516, f32[]{:T(128)} %constant.86.clone.1), kind=kCustom, calls=%fused_computation.21 | custom fusion | flops 640 | bytes 327684 | tf_op jit(solution)/shard_map/scatter-add | solution.py:72
  99.9 0.6 constant_dynamic-slice_fusion
  100.5 0.6 convolution_bitcast_fusion
  101.1 2.2 fusion.9
  103.3 180.8 %all-gather.2.cloned.1.call-done = bf16[640,64,128]{2,1,0:T(8,128)(2,1)} async-done(((bf16[10,64,128]{2,1,0:T(8,128)(2,1)}), bf16[640,64,128]{2,1,0:T(8,128)(2,1)}) %all-gather.2.cloned.1.call-update) | async-done | bytes 10485776 | tf_op jit(solution)/shard_map/all_gather | solution.py:94
  284.1 29.1 %copy.35 = bf16[8,80,64,128]{3,0,2,1:T(8,128)(2,1)} copy(bf16[8,80,64,128]{3,2,1,0:T(8,128)(2,1)} %bitcast.68) | data formatting | bytes 20971520 | tf_op jit(solution)/shard_map/reshape | solution.py:97
  313.2 7.3 %fusion.6 = bf16[256,1024]{0,1:T(8,128)(2,1)S(1)} fusion(bf16[256,5120]{1,0:T(8,128)(2,1)S(1)} %copy-done, bf16[640,8,8,128]{3,2,1,0:T(8,128)(2,1)} %bitcast.69), kind=kOutput, calls=%fused_computation.7 | convolution fusion | flops 2684616704 | bytes 13631488 | tf_op jit(solution)/shard_map/dot_general | solution.py:101
  320.5 1.0 copy.37
  (23 shorter events, 0.6 us)
Async XLA Ops:
  7.2 306.0 %copy-start = (bf16[256,5120]{1,0:T(8,128)(2,1)S(1)}, bf16[256,5120]{1,0:T(8,128)(2,1)}, u32[]{:S(2)}) copy-start(bf16[256,5120]{1,0:T(8,128)(2,1)} %param.6) | copy-start | bytes 7864324
  7.2 87.2 %copy-start.2 = (s32[1,20,32]{2,0,1:T(1,128)S(1)}, s32[1,20,32]{2,0,1:T(1,128)}, u32[]{:S(2)}) copy-start(s32[1,20,32]{2,0,1:T(1,128)} %param.10) | copy-start | bytes 7684
  7.2 8.2 %copy-start.3 = (s32[1,20]{1,0:T(1,128)S(1)}, s32[1,20]{1,0:T(1,128)}, u32[]{:S(2)}) copy-start(s32[1,20]{1,0:T(1,128)} %param.11) | copy-start | bytes 244
  7.2 276.9 %all-gather.2.cloned.1.call-start = ((), (), s32[]{:S(2)}) async-start(), calls=%async_computation | async-start | bytes 10649600 | tf_op jit(solution)/shard_map/all_gather | solution.py:94
  9.3 91.8 %copy-start.1 = (bf16[1,10,64,128]{3,2,1,0:T(8,128)(2,1)S(1)}, bf16[1,10,64,128]{3,2,1,0:T(8,128)(2,1)}, u32[]{:S(2)}) copy-start(bf16[1,10,64,128]{3,2,1,0:T(8,128)(2,1)} %param.9) | copy-start | bytes 491524
Sparse Core Ops, SparseCore 0:
  94.4 189.6 all-gather.1
where the time goes:
time: 329 us; the launch traced here: 328 us
  waiting for transfers between devices  181 us (55%)
  blocking collectives  45 us (14%)
  local copies, waits for them, and re-layouts  37 us (11%)
  other arithmetic  35.5 us (11%)
  matrix products  15.8 us (5%)
  between operations  14.2 us (4%)
    all_gather x1, waiting for transfers between devices, shards(): assembled = lax.all_gather(revised_parameters, 'fsdp', axis=0, tiled=True)  181 us
    reshape x1, local copies, waits for them, and re-layouts, shards(): assembled.reshape(out_blocks, width // block_side, block_side, tile_cols)  29.1 us
    scatter-add x1, other arithmetic, shards(): jnp.zeros((flat_size,), jnp.float32).at[all_places.reshape(-1)]  27.3 us
    all_gather x1, blocking collectives, shards(): lax.all_gather(kept_values[None], 'rep', axis=0, tiled=True)  23.2 us
    all_gather x1, blocking collectives, shards(): lax.all_gather(places[None], 'rep', axis=0, tiled=True)  21.8 us
    dot_general x1, matrix products, shards(): jnp.dot(hidden, matrix, preferred_element_type=jnp.float32)  7.31 us
  transfers between devices with their start and end apart: 1, of which 1 were waited for; matrix products, arithmetic and copies ran while one was open for 3% of the time, Pallas kernels for 0%

commit v1 on v0

v1 whole, which is shorter than its diff:
```python
import functools

import jax
import jax.numpy as jnp
import numpy as np
from jax import lax
from jax.experimental import pallas as pl
from jax.experimental.pallas import tpu as pltpu
from jax.sharding import Mesh, PartitionSpec as P

decay_rate = 0.999
step_size = 0.01
tiny_eps = 1e-06
SIDE = 64
exact = lax.Precision.HIGHEST
f32 = jnp.float32
bf16 = jnp.bfloat16
axes = ("xl", "y", "xh", "z", "c")
VMEM_LIMIT = 48 * 1024 * 1024


def tables():
    k = np.arange(SIDE)[:, None]
    n = np.arange(SIDE)[None, :]
    rows = np.cos(np.pi * (2 * n + 1) * k / (2 * SIDE)) * np.sqrt(2.0 / SIDE)
    rows[0] *= np.sqrt(0.5)
    pair = np.zeros((2 * SIDE, 2 * SIDE))
    pair[:SIDE, :SIDE] = rows
    pair[SIDE:, SIDE:] = rows
    ones = np.kron(np.eye(2), np.ones((SIDE, SIDE)))
    return rows.astype(np.float32), pair.astype(np.float32), ones.astype(np.float32)


def dot(a, b, dims=((1,), (0,)), precision=exact):
    return lax.dot_general(a, b, (dims, ((), ())), precision=precision, preferred_element_type=f32)


def one_hots(index_row):
    n = index_row.shape[1]
    lane = lax.broadcasted_iota(jnp.int32, (1, n), 1)
    row = index_row >> 6
    column = (index_row & 63) + jnp.where((lane & 63) >= 32, SIDE, 0)
    row_hot = jnp.where(lax.broadcasted_iota(jnp.int32, (SIDE, n), 0) == row, 1.0, 0.0).astype(f32)
    column_hot = jnp.where(
        lax.broadcasted_iota(jnp.int32, (2 * SIDE, n), 0) == column, 1.0, 0.0
    ).astype(f32)
    return row_hot, column_hot


def split_hidden_kernel(hidden, parts):
    for j in range(8):
        for half in range(2):
            piece = hidden[:, j * 640 + half * 320 : j * 640 + half * 320 + 320]
            for twin in range(2):
                parts[half, twin, :, j * 320 : j * 320 + 320] = piece


def values_kernel(momentum, gradient, indices, live, rows, pair, values):
    tiles = momentum.shape[1]
    table, wide = rows[...], pair[...]
    for t in range(tiles):
        moment = decay_rate * momentum[0, t] + gradient[0, t].astype(f32)
        spectrum = dot(dot(table, moment), wide, ((1,), (1,)))
        row_hot, column_hot = one_hots(indices[t : t + 1, :])
        picked = dot(spectrum, row_hot, ((0,), (0,)))
        value = jnp.sum(picked * column_hot, axis=0, keepdims=True)
        values[t : t + 1, :] = jnp.where(live[t : t + 1, :] > 0, value, 0.0)


def momentum_kernel(momentum, gradient, indices, values, rows, pair, out):
    tiles = momentum.shape[1]
    table, wide = rows[...], pair[...]
    for t in range(tiles):
        moment = decay_rate * momentum[0, t] + gradient[0, t].astype(f32)
        row_hot, column_hot = one_hots(indices[t : t + 1, :])
        spectrum = dot(row_hot * values[t : t + 1, :], column_hot, ((1,), (1,)))
        out[0, t] = moment - dot(dot(table, spectrum, ((0,), (0,))), wide)


def update_kernel(place, got_values, got_indices, weight, rows, pair, ones, update, pieces, raw, tanhs):
    replicas, tiles = got_values.shape[0], got_values.shape[1]
    table, wide = rows[...], pair[...]
    sums = []
    for t in range(tiles):
        index_row = jnp.concatenate([got_indices[r, t : t + 1, :] for r in range(replicas)], axis=1)
        value_row = jnp.concatenate([got_values[r, t : t + 1, :] for r in range(replicas)], axis=1)
        row_hot, column_hot = one_hots(index_row)
        shared = dot(row_hot * value_row, column_hot, ((1,), (1,))) / replicas
        flat = dot(dot(table, shared, ((0,), (0,))), wide)
        raw[t] = flat
        sums.append(jnp.sum(flat * flat, axis=0, keepdims=True))
    energy = dot(jnp.concatenate(sums, axis=0), ones[...])
    scale = jnp.sqrt(energy / (SIDE * SIDE) + tiny_eps)
    for t in range(tiles):
        tanhs[t] = jnp.tanh(raw[t] / scale[t : t + 1, :])
    own_rows = pl.multiple_of(place[0] * 8, 8)
    for t in range(tiles):
        update[t] = tanhs[t, pl.ds(own_rows, 8), :].astype(bf16)
    first_tile = place[1] * (tiles // 2)
    first_row = pl.multiple_of(place[2] * 16, 16)
    for t in range(tiles // 2):
        moved = tanhs[first_tile + t, pl.ds(first_row, 16), :].astype(bf16).astype(f32)
        old = weight[first_tile + t, pl.ds(first_row, 16), :].astype(f32)
        new = (old - step_size * moved).astype(bf16)
        for z in range(pieces.shape[0]):
            pieces[z, t] = new


def project_kernel(place, hidden, own, other, out, matrix):
    @pl.when(pl.program_id(0) == 0)
    def _():
        for source, core in ((own, place[0]), (other, 1 - place[0])):
            for z in range(16):
                start = pl.multiple_of((z % 4 * 2 + core) * 320, 64)
                for t in range(5):
                    for y in range(4):
                        matrix[pl.ds(start + t * 64 + y * 16, 16), z // 4 * 128 : z // 4 * 128 + 128] = source[y, z, t]

    out[0] = jnp.dot(hidden[0], matrix[...], preferred_element_type=f32).astype(bf16)


def call(kernel, out_shape, *args, scratch=(), flops=0, moved=0, **more):
    return pl.pallas_call(
        kernel,
        out_shape=out_shape,
        scratch_shapes=list(scratch),
        compiler_params=pltpu.CompilerParams(vmem_limit_bytes=VMEM_LIMIT),
        cost_estimate=pl.CostEstimate(flops=flops, bytes_accessed=moved, transcendentals=0),
        **more,
    )(*args)


def shards(hidden, weight, momentum, gradient, indices, counts):
    tiles = weight.shape[0]
    kept = indices.shape[2]
    rows, pair, ones = (jnp.asarray(a) for a in tables())
    xl, y, c = lax.axis_index("xl"), lax.axis_index("y"), lax.axis_index("c")
    vm, sm = pl.BlockSpec(memory_space=pltpu.VMEM), pl.BlockSpec(memory_space=pltpu.SMEM)

    with jax.named_scope("hidden_exchange"):
        parts = call(
            split_hidden_kernel,
            jax.ShapeDtypeStruct((2, 2, 256, 2560), bf16),
            hidden,
            moved=8 * 2**20,
            in_specs=[vm],
            out_specs=vm,
        )
        tokens = lax.all_to_all(parts.reshape(4, 256, 2560), ("xl", "xh"), 0, 0)

    with jax.named_scope("own_values"):
        live = (jnp.arange(kept, dtype=jnp.int32)[None, :] < counts[0][:, None]).astype(jnp.int32)
        live = live.reshape(tiles, 2 * kept)
        places = indices[0].reshape(tiles, 2 * kept)
        values = call(
            values_kernel,
            jax.ShapeDtypeStruct((tiles, 2 * kept), f32),
            momentum, gradient, places, live, rows, pair,
            flops=2**28, moved=2**19,
            in_specs=[vm] * 6,
            out_specs=vm,
        )

    with jax.named_scope("replica_exchange"):
        sent = jnp.stack([values, places.astype(f32)])
        got = lax.all_to_all(jnp.broadcast_to(sent, (8,) + sent.shape), ("xl", "y"), 0, 0)

    with jax.named_scope("new_weight"):
        update, pieces = call(
            update_kernel,
            (jax.ShapeDtypeStruct((tiles, 8, 128), bf16), jax.ShapeDtypeStruct((16, tiles // 2, 16, 128), bf16)),
            jnp.stack([xl * 4 + y, xl, y]).astype(jnp.int32),
            got[:, 0], got[:, 1].astype(jnp.int32), weight, rows, pair, ones,
            scratch=[pltpu.VMEM((tiles, SIDE, 128), f32)] * 2,
            flops=2**28, moved=2**19,
            in_specs=[sm] + [vm] * 6,
            out_specs=(vm, vm),
        )

    with jax.named_scope("weight_exchange"):
        along_z = lax.all_to_all(pieces, "z", 0, 0)
        along_y = lax.all_to_all(jnp.broadcast_to(along_z, (4,) + along_z.shape), "y", 0, 0)
        other = lax.ppermute(along_y, "c", [(0, 1), (1, 0)])

    with jax.named_scope("projection"):
        whole = pl.BlockSpec((4, 16, 5, 16, 128), lambda i: (0, 0, 0, 0, 0))
        partial = call(
            project_kernel,
            jax.ShapeDtypeStruct((4, 256, 512), bf16),
            c.reshape(1).astype(jnp.int32), tokens, along_y, other,
            scratch=[pltpu.VMEM((2560, 512), bf16)],
            flops=2 * 1024 * 2560 * 512, moved=10 * 2**20,
            grid=(4,),
            in_specs=[sm, pl.BlockSpec((1, 256, 2560), lambda i: (i, 0, 0)), whole, whole],
            out_specs=pl.BlockSpec((1, 256, 512), lambda i: (i, 0, 0)),
        )

    with jax.named_scope("output_exchange"):
        back = lax.all_to_all(partial, ("xl", "xh"), 0, 0).astype(f32)
        back = back.reshape(2, 2, 256, 512).sum(0).astype(bf16)
        keys = jnp.concatenate([back[0], back[1]], axis=1)

    with jax.named_scope("momentum"):
        new_momentum = call(
            momentum_kernel,
            jax.ShapeDtypeStruct(momentum.shape, f32),
            momentum, gradient, places, values, rows, pair,
            flops=2**28, moved=2**20,
            in_specs=[vm] * 6,
            out_specs=vm,
        )
    return (keys, update, new_momentum)


def solution(mesh):
    fine = Mesh(mesh.devices.reshape(2, 4, 2, 16, 2), axes)
    rep, group = ("xl", "y"), ("xh", "z", "c")
    in_specs = (
        P(axes[:2] + axes[2:], None),
        P(group, None, None),
        P(rep, group, None, None),
        P(rep, group, None, None),
        P(rep, group, None),
        P(rep, group),
    )
    out_specs = (P(axes, None), P(group, rep, None), P(rep, group, None, None))
    return jax.shard_map(shards, mesh=fine, in_specs=in_specs, out_specs=out_specs, check_vma=False)
```

time: 329 us -> 185 us (0.56)
  the two profiles are of different devices: /device:TPU:1 before, /device:TPU:32 now
where the time goes in v1:
time: 185 us; the launch traced here: 184 us
  waiting for transfers between devices  81.2 us (44%)
  blocking collectives  34.4 us (19%)
  Pallas kernels  31.4 us (17%)
  starting transfers between devices  20.4 us (11%)
  local copies, waits for them, and re-layouts  10.6 us (6%)
  other arithmetic  4.99 us (3%)
    all_to_all x1, waiting for transfers between devices, shards(): tokens = lax.all_to_all(parts.reshape(4, 256, 2560), ('xl', 'xh'), 0, 0)  51.2 us
    all_to_all x1, blocking collectives, shards(): along_z = lax.all_to_all(pieces, 'z', 0, 0)  34.4 us
    pallas_call x5, Pallas kernels, call(): pl.pallas_call(kernel, out_shape=out_shape, scratch_shapes=list(scratch),...  31.4 us
    all_to_all x1, waiting for transfers between devices, shards(): lax.all_to_all(jnp.broadcast_to(along_z, (4,) + along_z.shape), 'y', 0, 0)  12.6 us
    unnamed x30, local copies, waits for them, and re-layouts  8.25 us
    all_to_all x1, waiting for transfers between devices, shards(): back = lax.all_to_all(partial, ('xl', 'xh'), 0, 0).astype(f32)  8.05 us
    all_to_all x1, waiting for transfers between devices, shards(): lax.all_to_all(jnp.broadcast_to(sent, (8,) + sent.shape), ('xl', 'y'), 0, 0)  6.21 us
    all_to_all x1, starting transfers between devices, shards(): lax.all_to_all(jnp.broadcast_to(sent, (8,) + sent.shape), ('xl', 'y'), 0, 0)  5.4 us
  transfers between devices with their start and end apart: 5, of which 5 were waited for; matrix products, arithmetic and copies ran while one was open for 0% of the time, Pallas kernels for 5%

profile of v1, /device:TPU:32, one launch (start us, length us, event | category | flops | bytes accessed | tf_op | source)
XLA Modules:
  0.0 183.8 jit_solution(6197499363620240502)
XLA Ops:
  0.6 0.7 convert_reduce_fusion
  1.4 0.7 reduce.1
  2.3 0.5 broadcast.8
  2.8 1.3 reduce.7
  4.4 1.0 copy-done.1
  5.4 0.9 copy-done.4
  6.3 0.8 copy-done.6
  7.2 0.8 copy-done.10
  7.9 6.4 %own_values.1.values = f32[10,64]{1,0:T(8,128)S(1)} custom-call(f32[1,10,64,128]{3,2,1,0:T(8,128)S(1)} %copy-done.1, bf16[1,10,64,128]{3,2,1,0:T(8,128)(2,1)S(1)} %copy-done.4, s32[10,64]{1,0:T(8,128)S(1)} %squeeze.14.indices, s32[10,64]{1,0:T(8,128)S(1)} %compare_convert_fusion.live, f32[64,64]{1,0:T(8,128)S(1)} %copy-done.10, f32[128,128]{1,0:T(8,128)S(1)} %copy-done.6), custom_call_target="tpu_custom_call" | custom-call | flops 268435456 | bytes 524288 | tf_op jit(solution)/shard_map/own_values/pallas_call | solution.py:123
  14.4 0.7 reshape.51
  15.1 5.4 %all-to-all-start.1 = ((f32[8,1,1280]{2,1,0:T(1,128)}), f32[8,1,1280]{2,1,0:T(1,128)S(1)}, u32[]{:S(2)}, u32[]{:S(2)}) async-start(f32[8,1,1280]{2,1,0:T(1,128)} %reshape.51), calls=%async_computation.1 | async-start | bytes 81920 | tf_op jit(solution)/shard_map/replica_exchange/all_to_all | solution.py:166
  20.6 6.2 %all-to-all-done.1 = f32[8,1,1280]{2,1,0:T(1,128)S(1)} async-done(((f32[8,1,1280]{2,1,0:T(1,128)}), f32[8,1,1280]{2,1,0:T(1,128)S(1)}, u32[]{:S(2)}, u32[]{:S(2)}) %all-to-all-start.1) | async-done | bytes 40992 | tf_op jit(solution)/shard_map/replica_exchange/all_to_all | solution.py:166
  27.3 0.7 reduce.8
  28.3 0.9 copy-done.3
  29.2 0.8 copy-done.7
  30.0 0.8 copy-done.9
  30.9 0.8 copy-done.11
  31.6 8.2 %new_weight.1 = (bf16[10,8,128]{2,1,0:T(8,128)(2,1)}, bf16[16,5,16,128]{3,2,1,0:T(8,128)(2,1)S(1)}) custom-call(s32[3]{0:T(128)S(1)} %pad_add_fusion.place, f32[8,10,64]{2,1,0:T(8,128)S(1)} %get-tuple-element.12.got_values, s32[8,10,64]{2,1,0:T(8,128)S(1)} %get-tuple-element.11.got_indices, bf16[10,64,128]{2,1,0:T(8,128)(2,1)S(1)} %copy-done.3, ...), custom_call_target="tpu_custom_call" | custom-call | flops 268435456 | bytes 524288 | tf_op jit(solution)/shard_map/new_weight/pallas_call | solution.py:123
  39.8 34.4 %all_to_all.25 = bf16[16,5,16,128]{3,2,1,0:T(8,128)(2,1)S(1)} all-to-all(bf16[16,5,16,128]{3,2,1,0:T(8,128)(2,1)S(1)} %get-tuple-element.5), channel_id=1, replica_groups=mesh['xl'=2,'y'=4,'xh'=2,'z'=16,'c'=2] {'z'}, dimensions={0} | all-to-all | bytes 655360 | tf_op jit(solution)/shard_map/weight_exchange/all_to_all | solution.py:181
  74.1 1.3 broadcast_in_dim.8
  75.4 4.3 %all-to-all-start.3 = ((bf16[4,16,5,16,128]{4,3,2,1,0:T(8,128)(2,1)}), bf16[4,16,5,16,128]{4,3,2,1,0:T(8,128)(2,1)}, u32[]{:S(2)}, u32[]{:S(2)}) async-start(bf16[4,16,5,16,128]{4,3,2,1,0:T(8,128)(2,1)} %broadcast_in_dim.8), calls=%async_computation.3 | async-start | bytes 2621440 | tf_op jit(solution)/shard_map/weight_exchange/all_to_all | solution.py:182
  79.7 3.1 %hidden_exchange.1 = bf16[2,2,256,2560]{3,2,1,0:T(8,128)(2,1)} custom-call(bf16[256,5120]{1,0:T(8,128)(2,1)S(1)} %copy-done), custom_call_target="tpu_custom_call" | custom-call | bytes 8388608 | tf_op jit(solution)/shard_map/hidden_exchange/pallas_call | solution.py:123
  82.8 12.6 %all-to-all-done.3.own = bf16[4,16,5,16,128]{4,3,2,1,0:T(8,128)(2,1)} async-done(((bf16[4,16,5,16,128]{4,3,2,1,0:T(8,128)(2,1)}), bf16[4,16,5,16,128]{4,3,2,1,0:T(8,128)(2,1)}, u32[]{:S(2)}, u32[]{:S(2)}) %all-to-all-start.3) | async-done | bytes 1310752 | tf_op jit(solution)/shard_map/weight_exchange/all_to_all | solution.py:182
  95.4 5.1 %all-to-all-start = ((bf16[4,256,2560]{2,1,0:T(8,128)(2,1)}), bf16[4,256,2560]{2,1,0:T(8,128)(2,1)}, u32[]{:S(2)}, u32[]{:S(2)}) async-start(bf16[4,256,2560]{2,1,0:T(8,128)(2,1)} %bitcast.19), calls=%async_computation | async-start | bytes 10485760 | tf_op jit(solution)/shard_map/hidden_exchange/all_to_all | solution.py:149
  100.5 1.9 %collective-permute-start = (bf16[4,16,5,16,128]{4,3,2,1,0:T(8,128)(2,1)}, bf16[4,16,5,16,128]{4,3,2,1,0:T(8,128)(2,1)S(1)}, u32[]{:S(2)}, u32[]{:S(2)}) collective-permute-start(bf16[4,16,5,16,128]{4,3,2,1,0:T(8,128)(2,1)} %all-to-all-done.3.own), channel_id=1, source_target_pairs={{0,1},{1,0},{2,3},{3,2},{4,5},{5,4},{6,7},{7,6},{8,9},{9,8},{10,11... | collective-permute-start | bytes 3932168 | tf_op jit(solution)/shard_map/weight_exchange/ppermute | solution.py:183
  102.4 3.2 %collective-permute-done.other = bf16[4,16,5,16,128]{4,3,2,1,0:T(8,128)(2,1)S(1)} collective-permute-done((bf16[4,16,5,16,128]{4,3,2,1,0:T(8,128)(2,1)}, bf16[4,16,5,16,128]{4,3,2,1,0:T(8,128)(2,1)S(1)}, u32[]{:S(2)}, u32[]{:S(2)}) %collective-permute-start) | collective-permute-done | bytes 1310752 | tf_op jit(solution)/shard_map/weight_exchange/ppermute | solution.py:183
  105.6 51.2 %all-to-all-done.hidden = bf16[4,256,2560]{2,1,0:T(8,128)(2,1)} async-done(((bf16[4,256,2560]{2,1,0:T(8,128)(2,1)}), bf16[4,256,2560]{2,1,0:T(8,128)(2,1)}, u32[]{:S(2)}, u32[]{:S(2)}) %all-to-all-start) | async-done | bytes 5242912 | tf_op jit(solution)/shard_map/hidden_exchange/all_to_all | solution.py:149
  156.8 7.1 %projection.1 = bf16[4,256,512]{2,1,0:T(8,128)(2,1)} custom-call(s32[1]{0:T(128)} %bitcast.place, bf16[4,256,2560]{2,1,0:T(8,128)(2,1)} %all-to-all-done.hidden, bf16[4,16,5,16,128]{4,3,2,1,0:T(8,128)(2,1)} %all-to-all-done.3.own, bf16[4,16,5,16,128]{4,3,2,1,0:T(8,128)(2,1)S(1)} %collective-permute-done.other), custom_call_target="tpu_custom_call" | custom-call | flops 2684354560 | bytes 10485760 | tf_op jit(solution)/shard_map/projection/pallas_call | solution.py:123
  164.0 3.7 %all-to-all-start.4 = ((bf16[4,256,512]{2,1,0:T(8,128)(2,1)}), bf16[4,256,512]{2,1,0:T(8,128)(2,1)S(1)}, u32[]{:S(2)}, u32[]{:S(2)}) async-start(bf16[4,256,512]{2,1,0:T(8,128)(2,1)} %projection.1), calls=%async_computation.4 | async-start | bytes 2097152 | tf_op jit(solution)/shard_map/output_exchange/all_to_all | solution.py:199
  167.7 6.6 %momentum.4 = f32[1,10,64,128]{3,2,1,0:T(8,128)} custom-call(f32[1,10,64,128]{3,2,1,0:T(8,128)S(1)} %copy-done.2, bf16[1,10,64,128]{3,2,1,0:T(8,128)(2,1)S(1)} %copy-done.5, s32[10,64]{1,0:T(8,128)S(1)} %squeeze.14.indices, f32[10,64]{1,0:T(8,128)S(1)} %own_values.1.values, f32[64,64]{1,0:T(8,128)S(1)} %copy-done.12, f32[128,128]{1,0:T(8,128)S(1)} %copy-done.8), custom_call_target="tpu_custom_call" | custom-call | flops 268435456 | bytes 1048576 | tf_op jit(solution)/shard_map/momentum/pallas_call | solution.py:123
  174.3 8.1 %all-to-all-done.4 = bf16[4,256,512]{2,1,0:T(8,128)(2,1)S(1)} async-done(((bf16[4,256,512]{2,1,0:T(8,128)(2,1)}), bf16[4,256,512]{2,1,0:T(8,128)(2,1)S(1)}, u32[]{:S(2)}, u32[]{:S(2)}) %all-to-all-start.4) | async-done | bytes 1048608 | tf_op jit(solution)/shard_map/output_exchange/all_to_all | solution.py:199
  182.9 0.9 pad_maximum_fusion
  (36 shorter events, 1.8 us)
Async XLA Ops:
  4.4 1.0 copy-start.1
  5.4 0.9 copy-start.4
  6.3 0.8 copy-start.6
  7.2 0.8 copy-start.10
  15.1 11.7 %all-to-all-start.1 = ((f32[8,1,1280]{2,1,0:T(1,128)}), f32[8,1,1280]{2,1,0:T(1,128)S(1)}, u32[]{:S(2)}, u32[]{:S(2)}) async-start(f32[8,1,1280]{2,1,0:T(1,128)} %reshape.51), calls=%async_computation.1 | async-start | bytes 81920 | tf_op jit(solution)/shard_map/replica_exchange/all_to_all | solution.py:166
  28.3 0.9 copy-start.3
  29.2 0.8 copy-start.7
  30.0 0.8 copy-start.9
  30.9 0.8 copy-start.11
  39.8 39.9 %copy-start = (bf16[256,5120]{1,0:T(8,128)(2,1)S(1)}, bf16[256,5120]{1,0:T(8,128)(2,1)}, u32[]{:S(2)}) copy-start(bf16[256,5120]{1,0:T(8,128)(2,1)} %hidden.1) | copy-start | bytes 7864324
  75.4 20.0 %all-to-all-start.3 = ((bf16[4,16,5,16,128]{4,3,2,1,0:T(8,128)(2,1)}), bf16[4,16,5,16,128]{4,3,2,1,0:T(8,128)(2,1)}, u32[]{:S(2)}, u32[]{:S(2)}) async-start(bf16[4,16,5,16,128]{4,3,2,1,0:T(8,128)(2,1)} %broadcast_in_dim.8), calls=%async_computation.3 | async-start | bytes 2621440 | tf_op jit(solution)/shard_map/weight_exchange/all_to_all | solution.py:182
  95.4 61.4 %all-to-all-start = ((bf16[4,256,2560]{2,1,0:T(8,128)(2,1)}), bf16[4,256,2560]{2,1,0:T(8,128)(2,1)}, u32[]{:S(2)}, u32[]{:S(2)}) async-start(bf16[4,256,2560]{2,1,0:T(8,128)(2,1)} %bitcast.19), calls=%async_computation | async-start | bytes 10485760 | tf_op jit(solution)/shard_map/hidden_exchange/all_to_all | solution.py:149
  100.5 5.1 %collective-permute-start = (bf16[4,16,5,16,128]{4,3,2,1,0:T(8,128)(2,1)}, bf16[4,16,5,16,128]{4,3,2,1,0:T(8,128)(2,1)S(1)}, u32[]{:S(2)}, u32[]{:S(2)}) collective-permute-start(bf16[4,16,5,16,128]{4,3,2,1,0:T(8,128)(2,1)} %all-to-all-done.3.own), channel_id=1, source_target_pairs={{0,1},{1,0},{2,3},{3,2},{4,5},{5,4},{6,7},{7,6},{8,9},{9,8},{10,11... | collective-permute-start | bytes 3932168 | tf_op jit(solution)/shard_map/weight_exchange/ppermute | solution.py:183
  156.8 10.9 %copy-start.2 = (f32[1,10,64,128]{3,2,1,0:T(8,128)S(1)}, f32[1,10,64,128]{3,2,1,0:T(8,128)}, u32[]{:S(2)}) copy-start(f32[1,10,64,128]{3,2,1,0:T(8,128)} %momentum.5) | copy-start | bytes 983044
  156.8 10.9 %copy-start.5 = (bf16[1,10,64,128]{3,2,1,0:T(8,128)(2,1)S(1)}, bf16[1,10,64,128]{3,2,1,0:T(8,128)(2,1)}, u32[]{:S(2)}) copy-start(bf16[1,10,64,128]{3,2,1,0:T(8,128)(2,1)} %gradient.3) | copy-start | bytes 491524
  156.8 10.9 %copy-start.8 = (f32[128,128]{1,0:T(8,128)S(1)}, f32[128,128]{1,0:T(8,128)}, u32[]{:S(2)}) copy-start(f32[128,128]{1,0:T(8,128)} %constant.25.clone.pair) | copy-start | bytes 196612
  156.8 10.9 %copy-start.12 = (f32[64,64]{1,0:T(8,128)S(1)}, f32[64,64]{1,0:T(8,128)}, u32[]{:S(2)}) copy-start(f32[64,64]{1,0:T(8,128)} %constant.24.clone.rows) | copy-start | bytes 49156
  164.0 18.4 %all-to-all-start.4 = ((bf16[4,256,512]{2,1,0:T(8,128)(2,1)}), bf16[4,256,512]{2,1,0:T(8,128)(2,1)S(1)}, u32[]{:S(2)}, u32[]{:S(2)}) async-start(bf16[4,256,512]{2,1,0:T(8,128)(2,1)} %projection.1), calls=%async_computation.4 | async-start | bytes 2097152 | tf_op jit(solution)/shard_map/output_exchange/all_to_all | solution.py:199

commit v2 on v1

v2 whole, which is shorter than its diff:
```python
import jax
import jax.numpy as jnp
import numpy as np
from jax import lax
from jax.experimental import pallas as pl
from jax.experimental.pallas import tpu as pltpu
from jax.sharding import Mesh, PartitionSpec as P

decay_rate = 0.999
step_size = 0.01
tiny_eps = 1e-06
SIDE = 64
PAIR = 128
f32 = jnp.float32
bf16 = jnp.bfloat16
axes = ("xl", "y", "xh", "z", "c")
VMEM_LIMIT = 40 * 1024 * 1024
WIDE_T, WIDE, BLOCK_ONES = 0, 2, 4
HALF = 1280


def split(a):
    high = a.astype(bf16)
    return high, (a - high.astype(f32)).astype(bf16)


def tables():
    k = np.arange(SIDE)[:, None]
    n = np.arange(SIDE)[None, :]
    rows = np.cos(np.pi * (2 * n + 1) * k / (2 * SIDE)) * np.sqrt(2.0 / SIDE)
    rows[0] *= np.sqrt(0.5)
    wide = np.kron(np.eye(2), rows).astype(np.float32)
    parts = []
    for a in (wide.T, wide):
        high = a.astype(bf16)
        parts += [high, (a - high.astype(np.float32)).astype(bf16)]
    parts.append(np.kron(np.eye(2), np.ones((SIDE, SIDE))).astype(bf16))
    return np.stack(parts)


def dot(a, b, dims=((1,), (0,))):
    return lax.dot_general(a, b, (dims, ((), ())), preferred_element_type=f32)


def dot3(a, b, dims=((1,), (0,))):
    return dot(a[0], b[0], dims) + (dot(a[0], b[1], dims) + dot(a[1], b[0], dims))


def one_hots(index_row):
    n = index_row.shape[1]
    lane = lax.broadcasted_iota(jnp.int32, (1, n), 1)
    row = index_row >> 6
    column = (index_row & 63) + jnp.where((lane & 63) >= 32, SIDE, 0)
    return (
        lax.broadcasted_iota(jnp.int32, (SIDE, n), 0) == row,
        lax.broadcasted_iota(jnp.int32, (PAIR, n), 0) == column,
    )


def cosines(index_row, table):
    row_hot, column_hot = (jnp.where(m, 1.0, 0.0).astype(bf16) for m in one_hots(index_row))
    rows = dot(table[WIDE_T, :SIDE, :SIDE], row_hot) + dot(table[WIDE_T + 1, :SIDE, :SIDE], row_hot)
    columns = dot(table[WIDE_T], column_hot) + dot(table[WIDE_T + 1], column_hot)
    return rows, columns


def index_line(indices):
    return jnp.concatenate([indices[b : b + 1, :] for b in range(indices.shape[0])], axis=1)


def split_hidden_kernel(place, hidden_far, after, mine, theirs, hidden, sems):
    even, c = place[0] == 0, place[1]
    copies = fetch(
        [hidden_far.at[:, pl.ds(zl * 1280, 1280)] for zl in range(4)],
        [hidden.at[:, pl.ds(zl * 1280, 1280)] for zl in range(4)],
        sems,
    )
    for zl in range(4):
        copies[zl].wait()
        for turn in range(2):
            core = c if turn == 0 else 1 - c
            both = hidden[:, pl.ds(pl.multiple_of(zl * 1280 + core * 640, 128), 640)]
            left, right = both[:, :320], both[:, 320:]
            start = turn * 1280 + zl * 320
            mine[:, start : start + 320] = jnp.where(even, left, right)
            theirs[:, start : start + 320] = jnp.where(even, right, left)


def fetch(sources, targets, sems):
    copies = [pltpu.make_async_copy(a, b, sems.at[i]) for i, (a, b) in enumerate(zip(sources, targets))]
    for copy in copies:
        copy.start()
    return copies


def values_kernel(momentum_far, gradient_far, indices_far, counts, table_far, sent, momentum, gradient, indices, table, sems):
    copies = fetch(
        (indices_far, table_far, momentum_far, gradient_far), (indices, table, momentum, gradient), sems
    )
    tiles = momentum.shape[1]
    copies[0].wait()
    copies[1].wait()
    line = index_line(indices)
    rows, columns = cosines(line, table)
    high, low = split(columns)
    lane = lax.broadcasted_iota(jnp.int32, (1, SIDE), 1)
    copies[2].wait()
    copies[3].wait()
    out = []
    for t in range(tiles):
        e = slice(t * SIDE, t * SIDE + SIDE)
        moment = decay_rate * momentum[0, t] + gradient[0, t].astype(f32)
        half = dot3(split(moment), (high[:, e], low[:, e]))
        value = jnp.sum(half * rows[:, e], axis=0, keepdims=True)
        live = (lane & 31) < jnp.where(lane < 32, counts[2 * t], counts[2 * t + 1])
        out.append(jnp.concatenate([jnp.where(live, value, 0.0), line[:, e].astype(f32)], axis=1))
    out.append(jnp.zeros((sent.shape[1] - tiles, PAIR), f32))
    out = jnp.concatenate(out, axis=0)
    for r in range(sent.shape[0]):
        sent[r] = out


def momentum_kernel(momentum_far, gradient_far, indices_far, sent, table_far, out, momentum, gradient, indices, table, sems):
    copies = fetch(
        (indices_far, table_far, momentum_far, gradient_far), (indices, table, momentum, gradient), sems
    )
    tiles = momentum.shape[1]
    for copy in copies:
        copy.wait()
    line = index_line(indices)
    rows, columns = cosines(line, table)
    high, low = split(columns)
    for t in range(tiles):
        e = slice(t * SIDE, t * SIDE + SIDE)
        moment = decay_rate * momentum[0, t] + gradient[0, t].astype(f32)
        weighted = rows[:, e] * sent[0, t : t + 1, :SIDE]
        out[0, t] = moment - dot3(split(weighted), (high[:, e], low[:, e]), ((1,), (1,)))


def update_kernel(place, got, weight_far, table_far, update, pieces, tanhs, weight, table, sems):
    copies = fetch((table_far, weight_far), (table, weight), sems)
    replicas, tiles = got.shape[0], weight.shape[0]
    values = jnp.concatenate([got[r, :, :SIDE] for r in range(replicas)], axis=1)
    indices = jnp.concatenate([got[r, :, SIDE:] for r in range(replicas)], axis=1).astype(jnp.int32)
    copies[0].wait()
    wide_t = table[WIDE_T, :SIDE, :SIDE], table[WIDE_T + 1, :SIDE, :SIDE]
    halves = []
    for t in range(tiles):
        row_hot, column_hot = one_hots(indices[t : t + 1, :])
        column_hot = jnp.where(column_hot, 1.0, 0.0).astype(bf16)
        weighted = split(jnp.where(row_hot, values[t : t + 1, :], 0.0))
        nt = ((1,), (1,))
        shared = (dot(weighted[0], column_hot, nt) + dot(weighted[1], column_hot, nt)) / replicas
        halves.append(dot3(wide_t, split(shared)))
    raw = dot3(split(jnp.concatenate(halves, axis=0)), (table[WIDE], table[WIDE + 1]))
    raw = raw.reshape(tiles, SIDE, PAIR)
    energy = jnp.sum(raw * raw, axis=1)
    e0, e1 = split(energy)
    energy = dot(e0, table[BLOCK_ONES]) + dot(e1, table[BLOCK_ONES])
    scale = jnp.sqrt(energy / (SIDE * SIDE) + tiny_eps)
    tanhs[...] = jnp.tanh(raw / scale[:, None, :])
    copies[1].wait()
    own_rows = pl.multiple_of(place[0] * 8, 8)
    for t in range(tiles):
        update[t] = tanhs[t, pl.ds(own_rows, 8), :].astype(bf16)
    first_tile = place[1] * (tiles // 2)
    first_row = pl.multiple_of(place[2] * 16, 16)
    for t in range(tiles // 2):
        moved = tanhs[first_tile + t, pl.ds(first_row, 16), :].astype(bf16).astype(f32)
        old = weight[first_tile + t, pl.ds(first_row, 16), :].astype(f32)
        new = (old - step_size * moved).astype(bf16)
        for z in range(pieces.shape[0]):
            pieces[z, t] = new


def fill(source, matrix):
    for z in range(16):
        for t in range(5):
            for y in range(4):
                row = z % 4 * 320 + t * 64 + y * 16
                matrix[row : row + 16, z // 4 * 128 : z // 4 * 128 + 128] = source[y, z, t]


def project_own_kernel(mine, xh_side, xl_side, across, weights, total, matrix):
    fill(weights, matrix)
    for s, tokens in enumerate((mine, xh_side, xl_side, across)):
        total[s] = jnp.dot(tokens[:, :HALF], matrix[...], preferred_element_type=f32)


def project_rest_kernel(place, mine, xh_side, xl_side, across, weights, total, out, matrix):
    fill(weights, matrix)
    for s, tokens in enumerate((mine, xh_side, xl_side, across)):
        part = jnp.dot(tokens[:, HALF:], matrix[...], preferred_element_type=f32)
        out[(place[0] ^ (s >> 1)) * 2 + (place[1] ^ (s & 1))] = (total[s] + part).astype(bf16)


def call(kernel, out_shape, *args, scratch=(), flops=0, moved=0, **more):
    return pl.pallas_call(
        kernel,
        out_shape=out_shape,
        scratch_shapes=list(scratch),
        compiler_params=pltpu.CompilerParams(vmem_limit_bytes=VMEM_LIMIT),
        cost_estimate=pl.CostEstimate(flops=flops, bytes_accessed=moved, transcendentals=0),
        **more,
    )(*args)


def shards(hidden, weight, momentum, gradient, indices, counts):
    tiles = weight.shape[0]
    table = jnp.asarray(tables())
    xl, y, xh, c = (lax.axis_index(a) for a in ("xl", "y", "xh", "c"))
    vm, sm, far = (pl.BlockSpec(memory_space=m) for m in (pltpu.VMEM, pltpu.SMEM, pltpu.HBM))
    shape = jax.ShapeDtypeStruct
    dmas = pltpu.SemaphoreType.DMA

    def scalars(*a):
        return jnp.stack(a).astype(jnp.int32)

    def room(*arrays):
        return [pltpu.VMEM(a.shape, a.dtype) for a in arrays]

    with jax.named_scope("own_values"):
        sent = call(
            values_kernel,
            shape((8, 16, PAIR), f32),
            momentum, gradient, indices[0], counts[0], table,
            scratch=room(momentum, gradient, indices[0], table) + [dmas((4,))],
            moved=2**19,
            in_specs=[far, far, far, sm, far],
            out_specs=vm,
        )

    with jax.named_scope("hidden_exchange"):
        mine, theirs = call(
            split_hidden_kernel,
            (shape((256, 2 * HALF), bf16),) * 2,
            scalars(xl, c), hidden, sent,
            scratch=room(hidden) + [dmas((4,))],
            moved=5 * 2**20,
            in_specs=[sm, far, far],
            out_specs=(vm, vm),
        )

    with jax.named_scope("replica_exchange"):
        got = lax.all_to_all(sent, ("xl", "y"), 0, 0)
        got, mine, theirs = lax.optimization_barrier((got, mine, theirs))

    with jax.named_scope("hidden_exchange"):
        swap, cross = [(0, 1), (1, 0)], [(0, 3), (1, 2), (2, 1), (3, 0)]
        xl_side = lax.ppermute(theirs, "xl", swap)
        across = lax.ppermute(theirs, ("xl", "xh"), cross)
        mine, xl_side, across = lax.optimization_barrier((mine, xl_side, across))
        xh_side = lax.ppermute(mine, "xh", swap)

    with jax.named_scope("new_weight"):
        update, pieces = call(
            update_kernel,
            (shape((tiles, 8, PAIR), bf16), shape((16, tiles // 2, 16, PAIR), bf16)),
            scalars(xl * 4 + y, xl, y), got, weight, table,
            scratch=[pltpu.VMEM((tiles, SIDE, PAIR), f32)] + room(weight, table) + [dmas((2,))],
            moved=2**19,
            in_specs=[sm, vm, far, far],
            out_specs=(vm, vm),
        )

    with jax.named_scope("weight_exchange"):
        along_z = lax.all_to_all(pieces, "z", 0, 0)
        along_y = lax.all_to_all(jnp.broadcast_to(along_z, (4,) + along_z.shape), "y", 0, 0)
        along_y, xh_side = lax.optimization_barrier((along_y, xh_side))
        other = lax.ppermute(along_y, "c", swap)

    with jax.named_scope("projection"):
        matrix = pltpu.VMEM((HALF, 512), bf16)
        total = call(
            project_own_kernel,
            shape((4, 256, 512), f32),
            mine, xh_side, xl_side, across, along_y,
            scratch=[matrix],
            flops=1024 * 2560 * 512, moved=2**20,
            in_specs=[vm] * 5,
            out_specs=vm,
        )
        partial = call(
            project_rest_kernel,
            shape((4, 256, 512), bf16),
            scalars(xl, xh), mine, xh_side, xl_side, across, other, total,
            scratch=[matrix],
            flops=1024 * 2560 * 512, moved=2**20,
            in_specs=[sm] + [vm] * 6,
            out_specs=vm,
        )

    with jax.named_scope("output_exchange"):
        back = lax.all_to_all(partial, ("xl", "xh"), 0, 0).astype(f32)
        back = back.reshape(2, 2, 256, 512).sum(0).astype(bf16)
        keys = jnp.concatenate([back[0], back[1]], axis=1)

    with jax.named_scope("momentum"):
        new_momentum = call(
            momentum_kernel,
            shape(momentum.shape, f32),
            momentum, gradient, indices[0], sent, table,
            scratch=room(momentum, gradient, indices[0], table) + [dmas((4,))],
            moved=2**20,
            in_specs=[far, far, far, vm, far],
            out_specs=vm,
        )
    return (keys, update, new_momentum)


def solution(mesh):
    fine = Mesh(mesh.devices.reshape(2, 4, 2, 16, 2), axes)
    rep, group = ("xl", "y"), ("xh", "z", "c")
    in_specs = (
        P(axes, None),
        P(group, None, None),
        P(rep, group, None, None),
        P(rep, group, None, None),
        P(rep, group, None),
        P(rep, group),
    )
    out_specs = (P(axes, None), P(group, rep, None), P(rep, group, None, None))
    return jax.shard_map(shards, mesh=fine, in_specs=in_specs, out_specs=out_specs, check_vma=False)
```

time: 185 us -> 119 us (0.64)
  the two profiles are of different devices: /device:TPU:32 before, /device:TPU:256 now
where the time goes in v2:
time: 119 us
  waiting for transfers between devices  34.1 us (29%)
  starting transfers between devices  33.5 us (28%)
  Pallas kernels  20.6 us (17%)
  blocking collectives  20 us (17%)
  local copies, waits for them, and re-layouts  8.15 us (7%)
  other arithmetic  1.58 us (1%)
    pallas_call x6, Pallas kernels, call(): pl.pallas_call(kernel, out_shape=out_shape, scratch_shapes=list(scratch),...  20.6 us
    all_to_all x1, blocking collectives, shards(): lax.all_to_all(jnp.broadcast_to(along_z, (4,) + along_z.shape), 'y', 0, 0)  20 us
    all_to_all x1, waiting for transfers between devices, shards(): back = lax.all_to_all(partial, ('xl', 'xh'), 0, 0).astype(f32)  12.4 us
    all_to_all x1, starting transfers between devices, shards(): along_z = lax.all_to_all(pieces, 'z', 0, 0)  12 us
    ppermute x1, waiting for transfers between devices, shards(): xh_side = lax.ppermute(mine, 'xh', swap)  8.64 us
    unnamed x23, local copies, waits for them, and re-layouts  7.95 us
    ppermute x1, waiting for transfers between devices, shards(): xl_side = lax.ppermute(theirs, 'xl', swap)  7.41 us
    all_to_all x1, starting transfers between devices, shards(): got = lax.all_to_all(sent, ('xl', 'y'), 0, 0)  5.41 us
  transfers between devices with their start and end apart: 7, of which 5 were waited for; matrix products, arithmetic and copies ran while one was open for 0% of the time, Pallas kernels for 12%

profile of v2, /device:TPU:256, one launch (start us, length us, event | category | flops | bytes accessed | tf_op | source)
XLA Modules:
  0.0 118.8 jit_solution(2780759840193016770)
XLA Ops:
  0.6 0.7 copy.12
  1.3 0.9 copy-done.2
  2.3 1.0 copy-done.4
  3.2 0.9 copy-done.6
  4.1 0.7 copy-done.9
  4.8 2.6 %own_values.1.after.sent = f32[8,16,128]{2,1,0:T(8,128)} custom-call(f32[1,10,64,128]{3,2,1,0:T(8,128)S(1)} %copy-done.4, bf16[1,10,64,128]{3,2,1,0:T(8,128)(2,1)S(1)} %copy-done.6, s32[20,32]{1,0:T(8,128)S(1)} %bitcast.14, s32[20]{0:T(128)S(1)} %bitcast.16, bf16[5,128,128]{2,1,0:T(8,128)(2,1)S(1)} %copy-done.2), custom_call_target="tpu_custom_call" | custom-call | bytes 524288 | tf_op jit(solution)/shard_map/own_values/pallas_call | solution.py:198
  7.4 5.4 %all-to-all-start = ((f32[8,16,128]{2,1,0:T(8,128)}), f32[8,16,128]{2,1,0:T(8,128)S(1)}, u32[]{:S(2)}, u32[]{:S(2)}) async-start(f32[8,16,128]{2,1,0:T(8,128)} %own_values.1.after.sent), calls=%async_computation | async-start | bytes 131072 | tf_op jit(solution)/shard_map/replica_exchange/all_to_all | solution.py:245
  12.9 1.7 %copy-done.1 = bf16[256,5120]{1,0:T(8,128)(2,1)S(1)} copy-done((bf16[256,5120]{1,0:T(8,128)(2,1)S(1)}, bf16[256,5120]{1,0:T(8,128)(2,1)}, u32[]{:S(2)}) %copy-start.1) | copy-done | bytes 2621464
  14.6 2.6 %hidden_exchange.1 = (bf16[256,2560]{1,0:T(8,128)(2,1)S(1)}, bf16[256,2560]{1,0:T(8,128)(2,1)S(1)}) custom-call(s32[2]{0:T(128)S(1)} %pad_add_fusion.1.place, bf16[256,5120]{1,0:T(8,128)(2,1)S(1)} %copy-done.1, f32[8,16,128]{2,1,0:T(8,128)} %own_values.1.after.sent), custom_call_target="tpu_custom_call" | custom-call | bytes 5242880 | tf_op jit(solution)/shard_map/hidden_exchange/pallas_call | solution.py:198
  17.2 1.0 copy-done.10
  18.2 0.9 all-to-all-done.got
  19.1 3.0 %collective-permute-start = (bf16[256,2560]{1,0:T(8,128)(2,1)}, bf16[256,2560]{1,0:T(8,128)(2,1)S(1)}, u32[]{:S(2)}, u32[]{:S(2)}) collective-permute-start(bf16[256,2560]{1,0:T(8,128)(2,1)} %copy-done.10), channel_id=1, source_target_pairs={{0,256},{256,0},{1,257},{257,1},{2,258},{258,2},{3,259},{259,3},{4... | collective-permute-start | bytes 3932168 | tf_op jit(solution)/shard_map/hidden_exchange/ppermute | solution.py:250
  22.2 4.1 %collective-permute-start.1 = (bf16[256,2560]{1,0:T(8,128)(2,1)}, bf16[256,2560]{1,0:T(8,128)(2,1)}, u32[]{:S(2)}, u32[]{:S(2)}) collective-permute-start(bf16[256,2560]{1,0:T(8,128)(2,1)} %copy-done.10), channel_id=1, source_target_pairs={{0,288},{32,256},{256,32},{288,0},{1,289},{33,257},{257,33},{289,1... | collective-permute-start | bytes 3932168 | tf_op jit(solution)/shard_map/hidden_exchange/ppermute | solution.py:251
  26.2 0.1 pad_add_fusion.2.place
  26.3 4.8 %new_weight.1 = (bf16[10,8,128]{2,1,0:T(8,128)(2,1)}, bf16[16,5,16,128]{3,2,1,0:T(8,128)(2,1)}) custom-call(s32[3]{0:T(128)S(1)} %pad_add_fusion.2.place, f32[8,16,128]{2,1,0:T(8,128)S(1)} %all-to-all-done.got, bf16[10,64,128]{2,1,0:T(8,128)(2,1)S(1)} %copy-done.8, bf16[5,128,128]{2,1,0:T(8,128)(2,1)S(1)} %copy-done.3), custom_call_target="tpu_custom_call" | custom-call | bytes 524288 | tf_op jit(solution)/shard_map/new_weight/pallas_call | solution.py:198
  31.1 12.0 %all-to-all-start.1 = ((bf16[16,5,16,128]{3,2,1,0:T(8,128)(2,1)}), bf16[16,5,16,128]{3,2,1,0:T(8,128)(2,1)S(1)}, u32[]{:S(2)}, u32[]{:S(2)}) async-start(bf16[16,5,16,128]{3,2,1,0:T(8,128)(2,1)} %get-tuple-element.21), calls=%async_computation.1 | async-start | bytes 655360 | tf_op jit(solution)/shard_map/weight_exchange/all_to_all | solution.py:267
  43.2 7.4 %collective-permute-done.xl_side = bf16[256,2560]{1,0:T(8,128)(2,1)S(1)} collective-permute-done((bf16[256,2560]{1,0:T(8,128)(2,1)}, bf16[256,2560]{1,0:T(8,128)(2,1)S(1)}, u32[]{:S(2)}, u32[]{:S(2)}) %collective-permute-start) | collective-permute-done | bytes 1310752 | tf_op jit(solution)/shard_map/hidden_exchange/ppermute | solution.py:250
  50.6 4.7 %collective-permute-done.1.across = bf16[256,2560]{1,0:T(8,128)(2,1)} collective-permute-done((bf16[256,2560]{1,0:T(8,128)(2,1)}, bf16[256,2560]{1,0:T(8,128)(2,1)}, u32[]{:S(2)}, u32[]{:S(2)}) %collective-permute-start.1) | collective-permute-done | bytes 1310752 | tf_op jit(solution)/shard_map/hidden_exchange/ppermute | solution.py:251
  55.3 3.4 %collective-permute-start.2 = (bf16[256,2560]{1,0:T(8,128)(2,1)S(1)}, bf16[256,2560]{1,0:T(8,128)(2,1)}, u32[]{:S(2)}, u32[]{:S(2)}) collective-permute-start(bf16[256,2560]{1,0:T(8,128)(2,1)S(1)} %get-tuple-element.19.mine), channel_id=1, source_target_pairs={{0,32},{32,0},{1,33},{33,1},{2,34},{34,2},{3,35},{35,3},{4,36},{36... | collective-permute-start | bytes 3932168 | tf_op jit(solution)/shard_map/hidden_exchange/ppermute | solution.py:253
  58.7 0.2 broadcast_in_dim.3
  58.9 20.0 %all_to_all.20.weights = bf16[4,16,5,16,128]{4,3,2,1,0:T(8,128)(2,1)} all-to-all(bf16[4,16,5,16,128]{4,3,2,1,0:T(8,128)(2,1)S(1)} %broadcast_in_dim.3), channel_id=1, replica_groups=mesh['xl'=2,'y'=4,'xh'=2,'z'=16,'c'=2] {'y'}, dimensions={0} | all-to-all | bytes 2621440 | tf_op jit(solution)/shard_map/weight_exchange/all_to_all | solution.py:268
  78.9 8.6 %collective-permute-done.2.xh_side = bf16[256,2560]{1,0:T(8,128)(2,1)} collective-permute-done((bf16[256,2560]{1,0:T(8,128)(2,1)S(1)}, bf16[256,2560]{1,0:T(8,128)(2,1)}, u32[]{:S(2)}, u32[]{:S(2)}) %collective-permute-start.2) | collective-permute-done | bytes 1310752 | tf_op jit(solution)/shard_map/hidden_exchange/ppermute | solution.py:253
  87.5 1.9 %collective-permute-start.3 = (bf16[4,16,5,16,128]{4,3,2,1,0:T(8,128)(2,1)}, bf16[4,16,5,16,128]{4,3,2,1,0:T(8,128)(2,1)}, u32[]{:S(2)}, u32[]{:S(2)}) collective-permute-start(bf16[4,16,5,16,128]{4,3,2,1,0:T(8,128)(2,1)} %all_to_all.20.weights), channel_id=1, source_target_pairs={{0,1},{1,0},{2,3},{3,2},{4,5},{5,4},{6,7},{7,6},{8,9},{9,8},{10,11... | collective-permute-start | bytes 3932168 | tf_op jit(solution)/shard_map/weight_exchange/ppermute | solution.py:270
  89.5 0.1 pad_add_fusion.place
  89.5 3.7 %projection.2.total = f32[4,256,512]{2,1,0:T(8,128)S(1)} custom-call(bf16[256,2560]{1,0:T(8,128)(2,1)S(1)} %get-tuple-element.19.mine, bf16[256,2560]{1,0:T(8,128)(2,1)} %collective-permute-done.2.xh_side, bf16[256,2560]{1,0:T(8,128)(2,1)S(1)} %collective-permute-done.xl_side, bf16[256,2560]{1,0:T(8,128)(2,1)} %collective-permute-done.1.across, ...), custom_call_target="tpu_custom_call" | custom-call | flops 1342177280 | bytes 1048576 | tf_op jit(solution)/shard_map/projection/pallas_call | solution.py:198
  93.3 3.7 %projection.3 = bf16[4,256,512]{2,1,0:T(8,128)(2,1)S(1)} custom-call(s32[2]{0:T(128)S(1)} %pad_add_fusion.place, bf16[256,2560]{1,0:T(8,128)(2,1)S(1)} %get-tuple-element.19.mine, bf16[256,2560]{1,0:T(8,128)(2,1)} %collective-permute-done.2.xh_side, bf16[256,2560]{1,0:T(8,128)(2,1)S(1)} %collective-permute-done.xl_side, ...), custom_call_target="tpu_custom_call" | custom-call | flops 1342177280 | bytes 1048576 | tf_op jit(solution)/shard_map/projection/pallas_call | solution.py:198
  97.0 1.0 copy-done
  98.0 3.6 %all-to-all-start.3 = ((bf16[4,256,512]{2,1,0:T(8,128)(2,1)}), bf16[4,256,512]{2,1,0:T(8,128)(2,1)S(1)}, u32[]{:S(2)}, u32[]{:S(2)}) async-start(bf16[4,256,512]{2,1,0:T(8,128)(2,1)} %copy-done), calls=%async_computation.3 | async-start | bytes 2097152 | tf_op jit(solution)/shard_map/output_exchange/all_to_all | solution.py:294
  101.7 3.2 %momentum.1 = f32[1,10,64,128]{3,2,1,0:T(8,128)} custom-call(f32[1,10,64,128]{3,2,1,0:T(8,128)S(1)} %copy-done.5, bf16[1,10,64,128]{3,2,1,0:T(8,128)(2,1)S(1)} %copy-done.7, s32[20,32]{1,0:T(8,128)S(1)} %bitcast.15, f32[8,16,128]{2,1,0:T(8,128)} %own_values.1.after.sent, bf16[5,128,128]{2,1,0:T(8,128)(2,1)S(1)} %copy-done.3), custom_call_target="tpu_custom_call" | custom-call | bytes 1048576 | tf_op jit(solution)/shard_map/momentum/pallas_call | solution.py:198
  104.9 12.4 %all-to-all-done.3 = bf16[4,256,512]{2,1,0:T(8,128)(2,1)S(1)} async-done(((bf16[4,256,512]{2,1,0:T(8,128)(2,1)}), bf16[4,256,512]{2,1,0:T(8,128)(2,1)S(1)}, u32[]{:S(2)}, u32[]{:S(2)}) %all-to-all-start.3) | async-done | bytes 1048608 | tf_op jit(solution)/shard_map/output_exchange/all_to_all | solution.py:294
  117.4 0.5 reduce
  117.9 0.9 pad_maximum_fusion
  (19 shorter events, 0.1 us)
Async XLA Ops:
  1.3 0.9 copy-start.2
  2.3 1.0 copy-start.4
  3.2 0.9 copy-start.6
  4.1 0.7 copy-start.9
  7.4 11.8 %all-to-all-start = ((f32[8,16,128]{2,1,0:T(8,128)}), f32[8,16,128]{2,1,0:T(8,128)S(1)}, u32[]{:S(2)}, u32[]{:S(2)}) async-start(f32[8,16,128]{2,1,0:T(8,128)} %own_values.1.after.sent), calls=%async_computation | async-start | bytes 131072 | tf_op jit(solution)/shard_map/replica_exchange/all_to_all | solution.py:245
  12.8 1.7 %copy-start.1 = (bf16[256,5120]{1,0:T(8,128)(2,1)S(1)}, bf16[256,5120]{1,0:T(8,128)(2,1)}, u32[]{:S(2)}) copy-start(bf16[256,5120]{1,0:T(8,128)(2,1)} %hidden_far.1) | copy-start | bytes 7864324
  14.6 11.7 %copy-start.3 = (bf16[5,128,128]{2,1,0:T(8,128)(2,1)S(1)}, bf16[5,128,128]{2,1,0:T(8,128)(2,1)}, u32[]{:S(2)}) copy-start(bf16[5,128,128]{2,1,0:T(8,128)(2,1)} %constant.24.clone.table_far) | copy-start | bytes 491524
  14.6 11.7 %copy-start.8 = (bf16[10,64,128]{2,1,0:T(8,128)(2,1)S(1)}, bf16[10,64,128]{2,1,0:T(8,128)(2,1)}, u32[]{:S(2)}) copy-start(bf16[10,64,128]{2,1,0:T(8,128)(2,1)} %weight_far.1) | copy-start | bytes 491524
  17.2 1.1 copy-start.10
  19.1 31.5 %collective-permute-start = (bf16[256,2560]{1,0:T(8,128)(2,1)}, bf16[256,2560]{1,0:T(8,128)(2,1)S(1)}, u32[]{:S(2)}, u32[]{:S(2)}) collective-permute-start(bf16[256,2560]{1,0:T(8,128)(2,1)} %copy-done.10), channel_id=1, source_target_pairs={{0,256},{256,0},{1,257},{257,1},{2,258},{258,2},{3,259},{259,3},{4... | collective-permute-start | bytes 3932168 | tf_op jit(solution)/shard_map/hidden_exchange/ppermute | solution.py:250
  22.2 33.1 %collective-permute-start.1 = (bf16[256,2560]{1,0:T(8,128)(2,1)}, bf16[256,2560]{1,0:T(8,128)(2,1)}, u32[]{:S(2)}, u32[]{:S(2)}) collective-permute-start(bf16[256,2560]{1,0:T(8,128)(2,1)} %copy-done.10), channel_id=1, source_target_pairs={{0,288},{32,256},{256,32},{288,0},{1,289},{33,257},{257,33},{289,1... | collective-permute-start | bytes 3932168 | tf_op jit(solution)/shard_map/hidden_exchange/ppermute | solution.py:251
  31.1 27.6 %all-to-all-start.1 = ((bf16[16,5,16,128]{3,2,1,0:T(8,128)(2,1)}), bf16[16,5,16,128]{3,2,1,0:T(8,128)(2,1)S(1)}, u32[]{:S(2)}, u32[]{:S(2)}) async-start(bf16[16,5,16,128]{3,2,1,0:T(8,128)(2,1)} %get-tuple-element.21), calls=%async_computation.1 | async-start | bytes 655360 | tf_op jit(solution)/shard_map/weight_exchange/all_to_all | solution.py:267
  55.3 32.3 %collective-permute-start.2 = (bf16[256,2560]{1,0:T(8,128)(2,1)S(1)}, bf16[256,2560]{1,0:T(8,128)(2,1)}, u32[]{:S(2)}, u32[]{:S(2)}) collective-permute-start(bf16[256,2560]{1,0:T(8,128)(2,1)S(1)} %get-tuple-element.19.mine), channel_id=1, source_target_pairs={{0,32},{32,0},{1,33},{33,1},{2,34},{34,2},{3,35},{35,3},{4,36},{36... | collective-permute-start | bytes 3932168 | tf_op jit(solution)/shard_map/hidden_exchange/ppermute | solution.py:253
  87.5 5.7 %collective-permute-start.3 = (bf16[4,16,5,16,128]{4,3,2,1,0:T(8,128)(2,1)}, bf16[4,16,5,16,128]{4,3,2,1,0:T(8,128)(2,1)}, u32[]{:S(2)}, u32[]{:S(2)}) collective-permute-start(bf16[4,16,5,16,128]{4,3,2,1,0:T(8,128)(2,1)} %all_to_all.20.weights), channel_id=1, source_target_pairs={{0,1},{1,0},{2,3},{3,2},{4,5},{5,4},{6,7},{7,6},{8,9},{9,8},{10,11... | collective-permute-start | bytes 3932168 | tf_op jit(solution)/shard_map/weight_exchange/ppermute | solution.py:270
  97.0 1.0 copy-start
  98.0 3.7 %copy-start.5 = (f32[1,10,64,128]{3,2,1,0:T(8,128)S(1)}, f32[1,10,64,128]{3,2,1,0:T(8,128)}, u32[]{:S(2)}) copy-start(f32[1,10,64,128]{3,2,1,0:T(8,128)} %momentum_far.3) | copy-start | bytes 983044
  98.0 3.7 %copy-start.7 = (bf16[1,10,64,128]{3,2,1,0:T(8,128)(2,1)S(1)}, bf16[1,10,64,128]{3,2,1,0:T(8,128)(2,1)}, u32[]{:S(2)}) copy-start(bf16[1,10,64,128]{3,2,1,0:T(8,128)(2,1)} %gradient_far.3) | copy-start | bytes 491524
  98.0 19.4 %all-to-all-start.3 = ((bf16[4,256,512]{2,1,0:T(8,128)(2,1)}), bf16[4,256,512]{2,1,0:T(8,128)(2,1)S(1)}, u32[]{:S(2)}, u32[]{:S(2)}) async-start(bf16[4,256,512]{2,1,0:T(8,128)(2,1)} %copy-done), calls=%async_computation.3 | async-start | bytes 2097152 | tf_op jit(solution)/shard_map/output_exchange/all_to_all | solution.py:294

commit v3 on v2

v3 whole, which is shorter than its diff:
```python
import jax
import jax.numpy as jnp
import numpy as np
from jax import lax
from jax.experimental import pallas as pl
from jax.experimental.pallas import tpu as pltpu
from jax.sharding import Mesh, PartitionSpec as P

decay_rate = 0.999
step_size = 0.01
tiny_eps = 1e-06
SIDE = 64
PAIR = 128
f32 = jnp.float32
bf16 = jnp.bfloat16
axes = ("xl", "y", "xh", "z", "c")
VMEM_LIMIT = 16 * 2**20
MOST = 60 * 2**20
WIDE_T, WIDE, BLOCK_ONES = 0, 2, 4
HALF = 1280
OWN_FLOPS = 100 * 10**9
BAND = 64


def split(a):
    high = a.astype(bf16)
    return high, (a - high.astype(f32)).astype(bf16)


def tables():
    k = np.arange(SIDE)[:, None]
    n = np.arange(SIDE)[None, :]
    rows = np.cos(np.pi * (2 * n + 1) * k / (2 * SIDE)) * np.sqrt(2.0 / SIDE)
    rows[0] *= np.sqrt(0.5)
    wide = np.kron(np.eye(2), rows).astype(np.float32)
    parts = []
    for a in (wide.T, wide):
        high = a.astype(bf16)
        parts += [high, (a - high.astype(np.float32)).astype(bf16)]
    parts.append(np.kron(np.eye(2), np.ones((SIDE, SIDE))).astype(bf16))
    return np.stack(parts)


def dot(a, b, dims=((1,), (0,))):
    return lax.dot_general(a, b, (dims, ((), ())), preferred_element_type=f32)


def dot3(a, b, dims=((1,), (0,))):
    return dot(a[0], b[0], dims) + (dot(a[0], b[1], dims) + dot(a[1], b[0], dims))


def one_hots(index_row):
    n = index_row.shape[1]
    lane = lax.broadcasted_iota(jnp.int32, (1, n), 1)
    row = index_row >> 6
    column = (index_row & 63) + jnp.where((lane & 63) >= 32, SIDE, 0)
    return (
        lax.broadcasted_iota(jnp.int32, (SIDE, n), 0) == row,
        lax.broadcasted_iota(jnp.int32, (PAIR, n), 0) == column,
    )


def cosines(index_row, table):
    row_hot, column_hot = (jnp.where(m, 1.0, 0.0).astype(bf16) for m in one_hots(index_row))
    rows = dot(table[WIDE_T, :SIDE, :SIDE], row_hot) + dot(table[WIDE_T + 1, :SIDE, :SIDE], row_hot)
    columns = dot(table[WIDE_T], column_hot) + dot(table[WIDE_T + 1], column_hot)
    return rows, columns


def index_line(indices):
    return jnp.concatenate([indices[b] for b in range(indices.shape[0])], axis=1)


def split_hidden_kernel(hidden_far, after, mine_far, theirs_far, hidden, mine, theirs, sems):
    xl, c = lax.axis_index("xl"), lax.axis_index("c")
    bands = [pl.ds(i * BAND, BAND) for i in range(256 // BAND)]
    copies = fetch([hidden_far.at[k] for k in bands], [hidden.at[k] for k in bands], sems)
    left = lax.broadcasted_iota(jnp.int32, (BAND, 128), 1) < 64
    leaving = []
    for i, band in enumerate(bands):
        copies[i].wait()
        for turn in range(2):
            core = c if turn == 0 else 1 - c
            corners = []
            for zl in range(4):
                first = zl * 1280 + core * 640
                for out, half in ((theirs, 1 - xl), (mine, xl)):
                    start = turn * HALF + zl * 256
                    out[band, start : start + 256] = hidden[band, pl.ds(pl.multiple_of(first + half * 384, 128), 256)]
                corners.append(hidden[band, pl.ds(pl.multiple_of(first + 256, 128), 128)].astype(f32))
            for pair in range(2):
                a, b = corners[2 * pair : 2 * pair + 2]
                lows = jnp.where(left, a, pltpu.roll(b, 64, 1)).astype(bf16)
                highs = jnp.where(left, pltpu.roll(a, 64, 1), b).astype(bf16)
                start = turn * HALF + 1024 + pair * 128
                mine[band, start : start + 128] = jnp.where(xl == 0, lows, highs)
                theirs[band, start : start + 128] = jnp.where(xl == 0, highs, lows)
        leaving += fetch(
            (theirs.at[band], mine.at[band]),
            (theirs_far.at[band], mine_far.at[band]),
            [sems.at[len(bands) + 2 * i + j] for j in range(2)],
        )
    for copy in leaving:
        copy.wait()


def fetch(sources, targets, sems):
    sems = sems if isinstance(sems, list) else [sems.at[i] for i in range(len(sources))]
    copies = [pltpu.make_async_copy(*each) for each in zip(sources, targets, sems)]
    for copy in copies:
        copy.start()
    return copies


def values_kernel(momentum_far, gradient_far, indices_far, counts_far, table_far, sent, momentum, gradient, indices, counts, table, sems):
    copies = fetch(
        (indices_far, table_far, momentum_far, gradient_far, counts_far), (indices, table, momentum, gradient, counts), sems
    )
    tiles = momentum.shape[1]
    copies[0].wait()
    copies[1].wait()
    line = index_line(indices)
    rows, columns = cosines(line, table)
    high, low = split(columns)
    lane = lax.broadcasted_iota(jnp.int32, (1, SIDE), 1)
    for copy in copies[2:]:
        copy.wait()
    out = []
    for t in range(tiles):
        e = slice(t * SIDE, t * SIDE + SIDE)
        moment = decay_rate * momentum[0, t] + gradient[0, t].astype(f32)
        half = dot3(split(moment), (high[:, e], low[:, e]))
        value = jnp.sum(half * rows[:, e], axis=0, keepdims=True)
        live = (lane & 31) < jnp.where(lane < 32, counts[2 * t], counts[2 * t + 1])
        out.append(jnp.concatenate([jnp.where(live, value, 0.0), line[:, e].astype(f32)], axis=1))
    out.append(jnp.zeros((sent.shape[1] - tiles, PAIR), f32))
    out = jnp.concatenate(out, axis=0)
    for r in range(sent.shape[0]):
        sent[r] = out


def momentum_kernel(momentum, gradient, indices, sent, table, out):
    tiles = momentum.shape[1]
    line = index_line(indices)
    rows, columns = cosines(line, table)
    high, low = split(columns)
    for t in range(tiles):
        e = slice(t * SIDE, t * SIDE + SIDE)
        moment = decay_rate * momentum[0, t] + gradient[0, t].astype(f32)
        weighted = rows[:, e] * sent[0, t : t + 1, :SIDE]
        out[0, t] = moment - dot3(split(weighted), (high[:, e], low[:, e]), ((1,), (1,)))


def shared_directions(got, tiles, first_row, rows, table):
    replicas, nt = got.shape[0], ((1,), (1,))
    wide_t = [table[i, pl.ds(first_row, rows), :SIDE] for i in (WIDE_T, WIDE_T + 1)]
    halves, sums = [], []
    for t in tiles:
        lines = [got[r, pl.ds(t, 1), :] for r in range(replicas)]
        values = jnp.concatenate([line[:, :SIDE] for line in lines], axis=1)
        indices = jnp.concatenate([line[:, SIDE:] for line in lines], axis=1).astype(jnp.int32)
        row_hot, column_hot = one_hots(indices)
        column_hot = jnp.where(column_hot, 1.0, 0.0).astype(bf16)
        weighted = split(jnp.where(row_hot, values, 0.0))
        shared = (dot(weighted[0], column_hot, nt) + dot(weighted[1], column_hot, nt)) / replicas
        sums.append(jnp.sum(shared * shared, axis=0, keepdims=True))
        halves.append(dot3(wide_t, split(shared)))
    raw = dot3(split(jnp.concatenate(halves, axis=0)), (table[WIDE], table[WIDE + 1]))
    high, low = split(jnp.concatenate(sums, axis=0))
    energy = dot(high, table[BLOCK_ONES]) + dot(low, table[BLOCK_ONES])
    scale = jnp.sqrt(energy / (SIDE * SIDE) + tiny_eps)
    return jnp.tanh(raw.reshape(len(tiles), rows, PAIR) / scale[:, None, :])


def new_weight_kernel(got, weight, table, pieces):
    count = pieces.shape[1]
    first_tile = lax.axis_index("xl") * count
    first_row = pl.multiple_of(lax.axis_index("y") * 16, 16)
    tiles = [first_tile + t for t in range(count)]
    moved = shared_directions(got, tiles, first_row, 16, table).astype(bf16).astype(f32)
    for t in range(count):
        old = weight[tiles[t], pl.ds(first_row, 16), :].astype(f32)
        new = (old - step_size * moved[t]).astype(bf16)
        for z in range(pieces.shape[0]):
            pieces[z, t] = new


def update_kernel(got, table, update):
    first_row = pl.multiple_of((lax.axis_index("xl") * 4 + lax.axis_index("y")) * 8, 8)
    rows = pl.multiple_of(first_row // 16 * 16, 16)
    tanhs = shared_directions(got, list(range(update.shape[0])), rows, 16, table)
    upper = first_row == rows
    update[...] = jnp.where(upper, tanhs[:, :8], tanhs[:, 8:]).astype(bf16)


def fill_kernel(source, matrix):
    xl = lax.axis_index("xl")
    for z in range(16):
        for t in range(5):
            start = z % 4 * 256 + t * 64 if t < 4 else 1024 + z % 4 * 64
            tile = t + xl if t < 4 else 4 - 4 * xl
            for y in range(4):
                row = start + y * 16
                matrix[row : row + 16, z // 4 * 128 : z // 4 * 128 + 128] = source[y, z, tile]


def fetch_rows(tokens, start, rows, sems):
    return fetch([t.at[:, pl.ds(start, HALF)] for t in tokens], [rows.at[s] for s in range(4)], sems)


def project_own_kernel(mine, xh_side, xl_side, across, matrix, total, rows, sems):
    copies = fetch_rows((mine, xh_side, xl_side, across), 0, rows, sems)
    for s in range(4):
        copies[s].wait()
        total[s] = jnp.dot(rows[s], matrix[...], preferred_element_type=f32)


def project_rest_kernel(mine, xh_side, xl_side, across, matrix, total, out, rows, block, sems, out_sems):
    copies = fetch_rows((mine, xh_side, xl_side, across), HALF, rows, sems)
    xl, xh = lax.axis_index("xl"), lax.axis_index("xh")
    slots = xl * 2 + xh, xl * 2 + 1 - xh, (1 - xl) * 2 + xh, (1 - xl) * 2 + 1 - xh
    leaving = []
    for s in range(4):
        copies[s].wait()
        whole = total[s] + jnp.dot(rows[s], matrix[...], preferred_element_type=f32)
        block[s] = whole.astype(bf16)
        leaving += fetch([block.at[s]], [out.at[slots[s]]], [out_sems.at[s]])
    for copy in leaving:
        copy.wait()


def combine_kernel(back, keys):
    for xh in range(2):
        whole = back[xh].astype(f32) + back[2 + xh].astype(f32)
        keys[:, xh * 512 : xh * 512 + 512] = whole.astype(bf16)


def call(kernel, out_shape, *args, scratch=(), flops=0, moved=0, limit=VMEM_LIMIT, **more):
    return pl.pallas_call(
        kernel,
        out_shape=out_shape,
        scratch_shapes=list(scratch),
        compiler_params=pltpu.CompilerParams(vmem_limit_bytes=limit),
        cost_estimate=pl.CostEstimate(flops=flops, bytes_accessed=moved, transcendentals=0),
        **more,
    )(*args)


def shards(hidden, weight, momentum, gradient, indices, counts):
    tiles = weight.shape[0]
    table = jnp.asarray(tables())
    vm, far = (pl.BlockSpec(memory_space=m) for m in (pltpu.VMEM, pltpu.HBM))
    shape = jax.ShapeDtypeStruct
    dmas = pltpu.SemaphoreType.DMA

    def room(*arrays):
        return [pltpu.VMEM(a.shape, a.dtype) for a in arrays]

    lines = indices.reshape(2 * tiles, 1, indices.shape[2])
    with jax.named_scope("own_values"):
        sent = call(
            values_kernel,
            shape((8, 16, PAIR), f32),
            momentum, gradient, lines, counts[0], table,
            scratch=room(momentum, gradient, lines) + [pltpu.SMEM((2 * tiles,), jnp.int32)] + room(table) + [dmas((5,))],
            moved=2**19,
            limit=MOST,
            in_specs=[far] * 5,
            out_specs=vm,
        )

    with jax.named_scope("hidden_exchange"):
        mine, theirs = call(
            split_hidden_kernel,
            (shape((256, 2 * HALF), bf16),) * 2,
            hidden, sent,
            scratch=room(hidden) + [pltpu.VMEM((256, 2 * HALF), bf16)] * 2 + [dmas((12,))],
            moved=5 * 2**20,
            limit=MOST,
            in_specs=[far, pl.BlockSpec(memory_space=pl.ANY)],
            out_specs=(far, far),
        )

    with jax.named_scope("replica_exchange"):
        got = lax.all_to_all(sent, ("xl", "y"), 0, 0)
        got, mine, theirs = lax.optimization_barrier((got, mine, theirs))

    with jax.named_scope("hidden_exchange"):
        swap, cross = [(0, 1), (1, 0)], [(0, 3), (1, 2), (2, 1), (3, 0)]
        xh_side = lax.ppermute(mine, "xh", swap)
        theirs, xh_side = lax.optimization_barrier((theirs, xh_side))
        xl_side = lax.ppermute(theirs, "xl", swap)
        across = lax.ppermute(theirs, ("xl", "xh"), cross)

    with jax.named_scope("new_weight"):
        pieces = call(
            new_weight_kernel,
            shape((16, tiles // 2, 16, PAIR), bf16),
            got, weight, table,
            moved=2**19,
            in_specs=[vm] * 3,
            out_specs=vm,
        )
        update = call(
            update_kernel,
            shape((tiles, 8, PAIR), bf16),
            got, table,
            moved=2**19,
            in_specs=[vm] * 2,
            out_specs=vm,
        )

    with jax.named_scope("weight_exchange"):
        along_z = lax.all_to_all(pieces, "z", 0, 0)
        along_y = lax.all_to_all(jnp.broadcast_to(along_z, (4,) + along_z.shape), "y", 0, 0)
        matrix = shape((HALF, 512), bf16)
        own = call(fill_kernel, matrix, along_y, in_specs=[vm], out_specs=vm)
        other = lax.ppermute(own, "c", swap)

    with jax.named_scope("projection"):
        rows, anywhere = pltpu.VMEM((4, 256, HALF), bf16), pl.BlockSpec(memory_space=pl.ANY)
        total = call(
            project_own_kernel,
            shape((4, 256, 512), f32),
            mine, xh_side, xl_side, across, own,
            scratch=[rows, dmas((4,))],
            flops=OWN_FLOPS,
            in_specs=[anywhere] * 4 + [vm],
            out_specs=vm,
        )
        partial = call(
            project_rest_kernel,
            shape((4, 256, 512), bf16),
            mine, xh_side, xl_side, across, other, total,
            scratch=[rows, pltpu.VMEM((4, 256, 512), bf16), dmas((4,)), dmas((4,))],
            in_specs=[anywhere] * 4 + [vm, vm],
            out_specs=far,
        )

    with jax.named_scope("output_exchange"):
        back = lax.all_to_all(partial, ("xl", "xh"), 0, 0)
        keys = call(combine_kernel, shape((256, 1024), bf16), back, in_specs=[vm], out_specs=vm)

    with jax.named_scope("momentum"):
        new_momentum = call(
            momentum_kernel,
            shape(momentum.shape, f32),
            momentum, gradient, lines, sent, table,
            moved=2**20,
            in_specs=[vm] * 5,
            out_specs=vm,
        )
    return (keys, update, new_momentum)


def solution(mesh):
    fine = Mesh(mesh.devices.reshape(2, 4, 2, 16, 2), axes)
    rep, group = ("xl", "y"), ("xh", "z", "c")
    in_specs = (
        P(axes, None),
        P(group, None, None),
        P(rep, group, None, None),
        P(rep, group, None, None),
        P(rep, group, None),
        P(rep, group),
    )
    out_specs = (P(axes, None), P(group, rep, None), P(rep, group, None, None))
    return jax.shard_map(shards, mesh=fine, in_specs=in_specs, out_specs=out_specs, check_vma=False)
```

time: 119 us -> 103 us (0.87)
  local copies, waits for them, and re-layouts: 8.15 us -> 0.21 us
  waiting for transfers between devices: 34.1 us -> 29.3 us
  blocking collectives: 20 us -> 17.7 us
  starting transfers between devices: 33.5 us -> 35.3 us
  other arithmetic: 1.58 us -> 0 us
  Pallas kernels: 20.6 us -> 19.3 us
    unnamed x23 -> x16, local copies, waits for them, and re-layouts: 7.95 us -> 0.04 us
    all_to_all x1, waiting for transfers between devices: 12.4 us -> 6.05 us  [shards(): back = lax.all_to_all(partial, ('xl', 'xh'), 0, 0)]
    ppermute x1, waiting for transfers between devices: 8.64 us -> 13.5 us  [shards(): xh_side = lax.ppermute(mine, 'xh', swap)]
    ppermute x1, waiting for transfers between devices: 7.41 us -> 2.85 us  [shards(): xl_side = lax.ppermute(theirs, 'xl', swap)]
    all_to_all x1, waiting for transfers between devices: 0.88 us -> 3.38 us  [shards(): got = lax.all_to_all(sent, ('xl', 'y'), 0, 0)]
    all_to_all x1, blocking collectives: 20 us -> 17.7 us  [shards(): lax.all_to_all(jnp.broadcast_to(along_z, (4,) + along_z.shape), 'y', 0, 0)]
    pallas_call x6 -> x9, Pallas kernels: 20.6 us -> 19.3 us  [call(): pl.pallas_call(kernel, out_shape=out_shape, scratch_shapes=list(scratch),...]
    ppermute x1, starting transfers between devices: 3.41 us -> 4.63 us  [shards(): xh_side = lax.ppermute(mine, 'xh', swap)]
  transfers between devices with their start and end apart: 7 -> 7, of which waited for: 5 -> 5; matrix products, arithmetic and copies ran while one was open for 0% -> 0% of each run, Pallas kernels for 12% -> 13%
where the time goes in v3:
time: 103 us
  starting transfers between devices  35.3 us (34%)
  waiting for transfers between devices  29.3 us (28%)
  Pallas kernels  19.3 us (19%)
  blocking collectives  17.7 us (17%)
    pallas_call x9, Pallas kernels, call(): pl.pallas_call(kernel, out_shape=out_shape, scratch_shapes=list(scratch),...  19.3 us
    all_to_all x1, blocking collectives, shards(): lax.all_to_all(jnp.broadcast_to(along_z, (4,) + along_z.shape), 'y', 0, 0)  17.7 us
    ppermute x1, waiting for transfers between devices, shards(): xh_side = lax.ppermute(mine, 'xh', swap)  13.5 us
    all_to_all x1, starting transfers between devices, shards(): along_z = lax.all_to_all(pieces, 'z', 0, 0)  12 us
    all_to_all x1, waiting for transfers between devices, shards(): back = lax.all_to_all(partial, ('xl', 'xh'), 0, 0)  6.05 us
    all_to_all x1, starting transfers between devices, shards(): got = lax.all_to_all(sent, ('xl', 'y'), 0, 0)  5.41 us
    ppermute x1, starting transfers between devices, shards(): xh_side = lax.ppermute(mine, 'xh', swap)  4.63 us
    ppermute x1, starting transfers between devices, shards(): across = lax.ppermute(theirs, ('xl', 'xh'), cross)  4.55 us
  transfers between devices with their start and end apart: 7, of which 5 were waited for; matrix products, arithmetic and copies ran while one was open for 0% of the time, Pallas kernels for 13%

profile of v3, /device:TPU:256, one launch (start us, length us, event | category | flops | bytes accessed | tf_op | source)
XLA Modules:
  0.0 102.7 jit_solution(11210426930387162085)
XLA Ops:
  0.6 2.4 %own_values.1.after.sent = f32[8,16,128]{2,1,0:T(8,128)} custom-call(f32[1,10,64,128]{3,2,1,0:T(8,128)} %momentum.3, bf16[1,10,64,128]{3,2,1,0:T(8,128)(2,1)} %gradient.1, s32[20,1,32]{2,1,0:T(1,128)} %bitcast.2, s32[20]{0:T(128)} %bitcast.4, bf16[5,128,128]{2,1,0:T(8,128)(2,1)} %constant.2.clone.table_far.table), custom_call_target="tpu_custom_call" | custom-call | bytes 524288 | tf_op jit(solution)/shard_map/own_values/pallas_call | solution.py:239
  3.1 5.4 %all-to-all-start = ((f32[8,16,128]{2,1,0:T(8,128)}), f32[8,16,128]{2,1,0:T(8,128)S(1)}, u32[]{:S(2)}, u32[]{:S(2)}) async-start(f32[8,16,128]{2,1,0:T(8,128)} %own_values.1.after.sent), calls=%async_computation | async-start | bytes 131072 | tf_op jit(solution)/shard_map/replica_exchange/all_to_all | solution.py:285
  8.5 0.0 copy-start.5
  8.5 2.9 %hidden_exchange.1 = (bf16[256,2560]{1,0:T(8,128)(2,1)}, bf16[256,2560]{1,0:T(8,128)(2,1)}) custom-call(bf16[256,5120]{1,0:T(8,128)(2,1)} %hidden_far.1, f32[8,16,128]{2,1,0:T(8,128)} %own_values.1.after.sent), custom_call_target="tpu_custom_call" | custom-call | bytes 5242880 | tf_op jit(solution)/shard_map/hidden_exchange/pallas_call | solution.py:239
  11.4 0.0 copy-start.7
  11.4 3.4 %all-to-all-done.got = f32[8,16,128]{2,1,0:T(8,128)S(1)} async-done(((f32[8,16,128]{2,1,0:T(8,128)}), f32[8,16,128]{2,1,0:T(8,128)S(1)}, u32[]{:S(2)}, u32[]{:S(2)}) %all-to-all-start) | async-done | bytes 65568 | tf_op jit(solution)/shard_map/replica_exchange/all_to_all | solution.py:285
  14.8 4.6 %collective-permute-start = (bf16[256,2560]{1,0:T(8,128)(2,1)}, bf16[256,2560]{1,0:T(8,128)(2,1)S(1)}, u32[]{:S(2)}, u32[]{:S(2)}) collective-permute-start(bf16[256,2560]{1,0:T(8,128)(2,1)} %get-tuple-element.12.mine), channel_id=1, source_target_pairs={{0,32},{32,0},{1,33},{33,1},{2,34},{34,2},{3,35},{35,3},{4,36},{36... | collective-permute-start | bytes 3932168 | tf_op jit(solution)/shard_map/hidden_exchange/ppermute | solution.py:290
  19.5 2.5 %new_weight.2 = bf16[16,5,16,128]{3,2,1,0:T(8,128)(2,1)} custom-call(f32[8,16,128]{2,1,0:T(8,128)S(1)} %all-to-all-done.got, bf16[10,64,128]{2,1,0:T(8,128)(2,1)S(1)} %copy-done.5, bf16[5,128,128]{2,1,0:T(8,128)(2,1)S(1)} %copy-done), custom_call_target="tpu_custom_call" | custom-call | bytes 524288 | tf_op jit(solution)/shard_map/new_weight/pallas_call | solution.py:239
  22.0 12.0 %all-to-all-start.1 = ((bf16[16,5,16,128]{3,2,1,0:T(8,128)(2,1)}), bf16[16,5,16,128]{3,2,1,0:T(8,128)(2,1)S(1)}, u32[]{:S(2)}, u32[]{:S(2)}) async-start(bf16[16,5,16,128]{3,2,1,0:T(8,128)(2,1)} %new_weight.2), calls=%async_computation.1 | async-start | bytes 655360 | tf_op jit(solution)/shard_map/weight_exchange/all_to_all | solution.py:314
  34.0 13.5 %collective-permute-done.xh_side = bf16[256,2560]{1,0:T(8,128)(2,1)S(1)} collective-permute-done((bf16[256,2560]{1,0:T(8,128)(2,1)}, bf16[256,2560]{1,0:T(8,128)(2,1)S(1)}, u32[]{:S(2)}, u32[]{:S(2)}) %collective-permute-start) | collective-permute-done | bytes 1310752 | tf_op jit(solution)/shard_map/hidden_exchange/ppermute | solution.py:290
  47.5 2.6 %collective-permute-start.1 = (bf16[256,2560]{1,0:T(8,128)(2,1)S(1)}, bf16[256,2560]{1,0:T(8,128)(2,1)}, u32[]{:S(2)}, u32[]{:S(2)}) collective-permute-start(bf16[256,2560]{1,0:T(8,128)(2,1)S(1)} %copy-done.7), channel_id=1, source_target_pairs={{0,256},{256,0},{1,257},{257,1},{2,258},{258,2},{3,259},{259,3},{4... | collective-permute-start | bytes 3932168 | tf_op jit(solution)/shard_map/hidden_exchange/ppermute | solution.py:292
  50.1 4.6 %collective-permute-start.2 = (bf16[256,2560]{1,0:T(8,128)(2,1)S(1)}, bf16[256,2560]{1,0:T(8,128)(2,1)}, u32[]{:S(2)}, u32[]{:S(2)}) collective-permute-start(bf16[256,2560]{1,0:T(8,128)(2,1)S(1)} %copy-done.7), channel_id=1, source_target_pairs={{0,288},{32,256},{256,32},{288,0},{1,289},{33,257},{257,33},{289,1... | collective-permute-start | bytes 3932168 | tf_op jit(solution)/shard_map/hidden_exchange/ppermute | solution.py:293
  54.6 0.0 all-to-all-done.1
  54.7 0.2 broadcast_in_dim.3
  54.8 17.7 %all_to_all.20.source = bf16[4,16,5,16,128]{4,3,2,1,0:T(8,128)(2,1)S(1)} all-to-all(bf16[4,16,5,16,128]{4,3,2,1,0:T(8,128)(2,1)S(1)} %broadcast_in_dim.3), channel_id=1, replica_groups=mesh['xl'=2,'y'=4,'xh'=2,'z'=16,'c'=2] {'y'}, dimensions={0} | all-to-all | bytes 2621440 | tf_op jit(solution)/shard_map/weight_exchange/all_to_all | solution.py:315
  72.5 0.2 weight_exchange.1.matrix
  72.8 2.1 %collective-permute-start.3 = (bf16[1280,512]{1,0:T(8,128)(2,1)S(1)}, bf16[1280,512]{1,0:T(8,128)(2,1)S(1)}, u32[]{:S(2)}, u32[]{:S(2)}) collective-permute-start(bf16[1280,512]{1,0:T(8,128)(2,1)S(1)} %weight_exchange.1.matrix), channel_id=1, source_target_pairs={{0,1},{1,0},{2,3},{3,2},{4,5},{5,4},{6,7},{7,6},{8,9},{9,8},{10,11... | collective-permute-start | bytes 3932168 | tf_op jit(solution)/shard_map/weight_exchange/ppermute | solution.py:318
  74.8 2.8 %collective-permute-done.1.xl_side = bf16[256,2560]{1,0:T(8,128)(2,1)} collective-permute-done((bf16[256,2560]{1,0:T(8,128)(2,1)S(1)}, bf16[256,2560]{1,0:T(8,128)(2,1)}, u32[]{:S(2)}, u32[]{:S(2)}) %collective-permute-start.1) | collective-permute-done | bytes 1310752 | tf_op jit(solution)/shard_map/hidden_exchange/ppermute | solution.py:292
  77.7 3.5 %collective-permute-done.2.across = bf16[256,2560]{1,0:T(8,128)(2,1)} collective-permute-done((bf16[256,2560]{1,0:T(8,128)(2,1)S(1)}, bf16[256,2560]{1,0:T(8,128)(2,1)}, u32[]{:S(2)}, u32[]{:S(2)}) %collective-permute-start.2) | collective-permute-done | bytes 1310752 | tf_op jit(solution)/shard_map/hidden_exchange/ppermute | solution.py:293
  81.2 2.2 %projection.2.total = f32[4,256,512]{2,1,0:T(8,128)S(1)} custom-call(bf16[256,2560]{1,0:T(8,128)(2,1)S(1)} %copy-done.1, bf16[256,2560]{1,0:T(8,128)(2,1)S(1)} %collective-permute-done.xh_side, bf16[256,2560]{1,0:T(8,128)(2,1)} %collective-permute-done.1.xl_side, bf16[256,2560]{1,0:T(8,128)(2,1)} %collective-permute-done.2.across, ...), custom_call_target="tpu_custom_call" | custom-call | flops 99999997952 | tf_op jit(solution)/shard_map/projection/pallas_call | solution.py:239
  83.4 0.0 collective-permute-done.3.matrix
  83.4 3.0 %projection.3 = bf16[4,256,512]{2,1,0:T(8,128)(2,1)} custom-call(bf16[256,2560]{1,0:T(8,128)(2,1)S(1)} %copy-done.1, bf16[256,2560]{1,0:T(8,128)(2,1)S(1)} %collective-permute-done.xh_side, bf16[256,2560]{1,0:T(8,128)(2,1)} %collective-permute-done.1.xl_side, bf16[256,2560]{1,0:T(8,128)(2,1)} %collective-permute-done.2.across, ...), custom_call_target="tpu_custom_call" | custom-call | tf_op jit(solution)/shard_map/projection/pallas_call | solution.py:239
  86.4 0.0 copy-start.2
  86.4 0.0 copy-start.3
  86.4 0.0 copy-start.4
  86.4 0.0 copy-start.6
  86.4 4.1 %all-to-all-start.3 = ((bf16[4,256,512]{2,1,0:T(8,128)(2,1)}), bf16[4,256,512]{2,1,0:T(8,128)(2,1)S(1)}, u32[]{:S(2)}, u32[]{:S(2)}) async-start(bf16[4,256,512]{2,1,0:T(8,128)(2,1)} %projection.3), calls=%async_computation.3 | async-start | bytes 2097152 | tf_op jit(solution)/shard_map/output_exchange/all_to_all | solution.py:341
  90.5 0.0 copy-done.4
  90.5 1.9 %momentum.2 = f32[1,10,64,128]{3,2,1,0:T(8,128)} custom-call(f32[1,10,64,128]{3,2,1,0:T(8,128)S(1)} %copy-done.2, bf16[1,10,64,128]{3,2,1,0:T(8,128)(2,1)S(1)} %copy-done.4, s32[20,1,32]{2,1,0:T(1,128)S(1)} %bitcast.3, f32[8,16,128]{2,1,0:T(8,128)S(1)} %copy-done.3, bf16[5,128,128]{2,1,0:T(8,128)(2,1)S(1)} %copy-done), custom_call_target="tpu_custom_call" | custom-call | bytes 1048576 | tf_op jit(solution)/shard_map/momentum/pallas_call | solution.py:239
  92.4 3.3 %new_weight.3 = bf16[10,8,128]{2,1,0:T(8,128)(2,1)} custom-call(f32[8,16,128]{2,1,0:T(8,128)S(1)} %all-to-all-done.got, bf16[5,128,128]{2,1,0:T(8,128)(2,1)S(1)} %copy-done), custom_call_target="tpu_custom_call" | custom-call | bytes 524288 | tf_op jit(solution)/shard_map/new_weight/pallas_call | solution.py:239
  95.7 6.1 %all-to-all-done.3.back = bf16[4,256,512]{2,1,0:T(8,128)(2,1)S(1)} async-done(((bf16[4,256,512]{2,1,0:T(8,128)(2,1)}), bf16[4,256,512]{2,1,0:T(8,128)(2,1)S(1)}, u32[]{:S(2)}, u32[]{:S(2)}) %all-to-all-start.3) | async-done | bytes 1048608 | tf_op jit(solution)/shard_map/output_exchange/all_to_all | solution.py:341
  101.7 0.9 output_exchange.1
  (9 shorter events, 0.0 us)
Async XLA Ops:
  3.1 11.8 %all-to-all-start = ((f32[8,16,128]{2,1,0:T(8,128)}), f32[8,16,128]{2,1,0:T(8,128)S(1)}, u32[]{:S(2)}, u32[]{:S(2)}) async-start(f32[8,16,128]{2,1,0:T(8,128)} %own_values.1.after.sent), calls=%async_computation | async-start | bytes 131072 | tf_op jit(solution)/shard_map/replica_exchange/all_to_all | solution.py:285
  8.5 11.0 %copy-start = (bf16[5,128,128]{2,1,0:T(8,128)(2,1)S(1)}, bf16[5,128,128]{2,1,0:T(8,128)(2,1)}, u32[]{:S(2)}) copy-start(bf16[5,128,128]{2,1,0:T(8,128)(2,1)} %constant.2.clone.table_far.table) | copy-start | bytes 491524
  8.5 11.0 %copy-start.5 = (bf16[10,64,128]{2,1,0:T(8,128)(2,1)S(1)}, bf16[10,64,128]{2,1,0:T(8,128)(2,1)}, u32[]{:S(2)}) copy-start(bf16[10,64,128]{2,1,0:T(8,128)(2,1)} %weight.1) | copy-start | bytes 491524
  11.4 36.1 %copy-start.7 = (bf16[256,2560]{1,0:T(8,128)(2,1)S(1)}, bf16[256,2560]{1,0:T(8,128)(2,1)}, u32[]{:S(2)}) copy-start(bf16[256,2560]{1,0:T(8,128)(2,1)} %get-tuple-element.15) | copy-start | bytes 3932164
  14.8 32.7 %collective-permute-start = (bf16[256,2560]{1,0:T(8,128)(2,1)}, bf16[256,2560]{1,0:T(8,128)(2,1)S(1)}, u32[]{:S(2)}, u32[]{:S(2)}) collective-permute-start(bf16[256,2560]{1,0:T(8,128)(2,1)} %get-tuple-element.12.mine), channel_id=1, source_target_pairs={{0,32},{32,0},{1,33},{33,1},{2,34},{34,2},{3,35},{35,3},{4,36},{36... | collective-permute-start | bytes 3932168 | tf_op jit(solution)/shard_map/hidden_exchange/ppermute | solution.py:290
  22.0 32.7 %all-to-all-start.1 = ((bf16[16,5,16,128]{3,2,1,0:T(8,128)(2,1)}), bf16[16,5,16,128]{3,2,1,0:T(8,128)(2,1)S(1)}, u32[]{:S(2)}, u32[]{:S(2)}) async-start(bf16[16,5,16,128]{3,2,1,0:T(8,128)(2,1)} %new_weight.2), calls=%async_computation.1 | async-start | bytes 655360 | tf_op jit(solution)/shard_map/weight_exchange/all_to_all | solution.py:314
  47.5 30.2 %collective-permute-start.1 = (bf16[256,2560]{1,0:T(8,128)(2,1)S(1)}, bf16[256,2560]{1,0:T(8,128)(2,1)}, u32[]{:S(2)}, u32[]{:S(2)}) collective-permute-start(bf16[256,2560]{1,0:T(8,128)(2,1)S(1)} %copy-done.7), channel_id=1, source_target_pairs={{0,256},{256,0},{1,257},{257,1},{2,258},{258,2},{3,259},{259,3},{4... | collective-permute-start | bytes 3932168 | tf_op jit(solution)/shard_map/hidden_exchange/ppermute | solution.py:292
  50.1 31.1 %collective-permute-start.2 = (bf16[256,2560]{1,0:T(8,128)(2,1)S(1)}, bf16[256,2560]{1,0:T(8,128)(2,1)}, u32[]{:S(2)}, u32[]{:S(2)}) collective-permute-start(bf16[256,2560]{1,0:T(8,128)(2,1)S(1)} %copy-done.7), channel_id=1, source_target_pairs={{0,288},{32,256},{256,32},{288,0},{1,289},{33,257},{257,33},{289,1... | collective-permute-start | bytes 3932168 | tf_op jit(solution)/shard_map/hidden_exchange/ppermute | solution.py:293
  72.5 8.6 %copy-start.1 = (bf16[256,2560]{1,0:T(8,128)(2,1)S(1)}, bf16[256,2560]{1,0:T(8,128)(2,1)}, u32[]{:S(2)}) copy-start(bf16[256,2560]{1,0:T(8,128)(2,1)} %get-tuple-element.12.mine) | copy-start | bytes 3932164
  72.8 10.6 %collective-permute-start.3 = (bf16[1280,512]{1,0:T(8,128)(2,1)S(1)}, bf16[1280,512]{1,0:T(8,128)(2,1)S(1)}, u32[]{:S(2)}, u32[]{:S(2)}) collective-permute-start(bf16[1280,512]{1,0:T(8,128)(2,1)S(1)} %weight_exchange.1.matrix), channel_id=1, source_target_pairs={{0,1},{1,0},{2,3},{3,2},{4,5},{5,4},{6,7},{7,6},{8,9},{9,8},{10,11... | collective-permute-start | bytes 3932168 | tf_op jit(solution)/shard_map/weight_exchange/ppermute | solution.py:318
  86.4 4.1 %copy-start.2 = (f32[1,10,64,128]{3,2,1,0:T(8,128)S(1)}, f32[1,10,64,128]{3,2,1,0:T(8,128)}, u32[]{:S(2)}) copy-start(f32[1,10,64,128]{3,2,1,0:T(8,128)} %momentum.3) | copy-start | bytes 983044
  86.4 4.1 %copy-start.3 = (f32[8,16,128]{2,1,0:T(8,128)S(1)}, f32[8,16,128]{2,1,0:T(8,128)}, u32[]{:S(2)}) copy-start(f32[8,16,128]{2,1,0:T(8,128)} %own_values.1.after.sent) | copy-start | bytes 196612
  86.4 4.1 %copy-start.4 = (bf16[1,10,64,128]{3,2,1,0:T(8,128)(2,1)S(1)}, bf16[1,10,64,128]{3,2,1,0:T(8,128)(2,1)}, u32[]{:S(2)}) copy-start(bf16[1,10,64,128]{3,2,1,0:T(8,128)(2,1)} %gradient.1) | copy-start | bytes 491524
  86.4 4.1 %copy-start.6 = (s32[1,20,32]{2,0,1:T(1,128)S(1)}, s32[1,20,32]{2,0,1:T(1,128)}, u32[]{:S(2)}) copy-start(s32[1,20,32]{2,0,1:T(1,128)} %param.11) | copy-start | bytes 7684
  86.4 15.3 %all-to-all-start.3 = ((bf16[4,256,512]{2,1,0:T(8,128)(2,1)}), bf16[4,256,512]{2,1,0:T(8,128)(2,1)S(1)}, u32[]{:S(2)}, u32[]{:S(2)}) async-start(bf16[4,256,512]{2,1,0:T(8,128)(2,1)} %projection.3), calls=%async_computation.3 | async-start | bytes 2097152 | tf_op jit(solution)/shard_map/output_exchange/all_to_all | solution.py:341

commit v4 on v3

--- a/solution.py
+++ b/solution.py
@@ -1,3 +1,5 @@
+import functools
+
 import jax
 import jax.numpy as jnp
 import numpy as np
@@ -19,7 +21,6 @@
 WIDE_T, WIDE, BLOCK_ONES = 0, 2, 4
 HALF = 1280
 OWN_FLOPS = 100 * 10**9
-BAND = 64
 
 
 def split(a):
@@ -71,36 +72,33 @@
     return jnp.concatenate([indices[b] for b in range(indices.shape[0])], axis=1)
 
 
-def split_hidden_kernel(hidden_far, after, mine_far, theirs_far, hidden, mine, theirs, sems):
-    xl, c = lax.axis_index("xl"), lax.axis_index("c")
-    bands = [pl.ds(i * BAND, BAND) for i in range(256 // BAND)]
-    copies = fetch([hidden_far.at[k] for k in bands], [hidden.at[k] for k in bands], sems)
-    left = lax.broadcasted_iota(jnp.int32, (BAND, 128), 1) < 64
-    leaving = []
-    for i, band in enumerate(bands):
-        copies[i].wait()
-        for turn in range(2):
-            core = c if turn == 0 else 1 - c
-            corners = []
-            for zl in range(4):
-                first = zl * 1280 + core * 640
-                for out, half in ((theirs, 1 - xl), (mine, xl)):
-                    start = turn * HALF + zl * 256
-                    out[band, start : start + 256] = hidden[band, pl.ds(pl.multiple_of(first + half * 384, 128), 256)]
-                corners.append(hidden[band, pl.ds(pl.multiple_of(first + 256, 128), 128)].astype(f32))
-            for pair in range(2):
-                a, b = corners[2 * pair : 2 * pair + 2]
-                lows = jnp.where(left, a, pltpu.roll(b, 64, 1)).astype(bf16)
-                highs = jnp.where(left, pltpu.roll(a, 64, 1), b).astype(bf16)
-                start = turn * HALF + 1024 + pair * 128
-                mine[band, start : start + 128] = jnp.where(xl == 0, lows, highs)
-                theirs[band, start : start + 128] = jnp.where(xl == 0, highs, lows)
-        leaving += fetch(
-            (theirs.at[band], mine.at[band]),
-            (theirs_far.at[band], mine_far.at[band]),
-            [sems.at[len(bands) + 2 * i + j] for j in range(2)],
-        )
-    for copy in leaving:
+def pack_hidden_kernel(keep, hidden_far, after, out_far, parts, out, sems):
+    half = lax.axis_index("xl") if keep else 1 - lax.axis_index("xl")
+    c = lax.axis_index("c")
+    sources = []
+    for turn in range(2):
+        core = c if turn == 0 else 1 - c
+        for zl in range(4):
+            start = pl.multiple_of(zl * 1280 + core * 640 + half * 256, 128)
+            sources.append(hidden_far.at[:, pl.ds(start, 384)])
+    copies = fetch(sources, [parts.at[i] for i in range(8)], sems)
+    left = lax.broadcasted_iota(jnp.int32, (256, 128), 1) < 64
+    corner, body = pl.multiple_of(256 - half * 256, 128), pl.multiple_of(half * 128, 128)
+    for turn in range(2):
+        for zl in range(4):
+            i = turn * 4 + zl
+            copies[i].wait()
+            start = turn * HALF + zl * 256
+            out[:, start : start + 256] = parts[i, :, pl.ds(body, 256)]
+            if zl % 2 == 1:
+                a = parts[i - 1, :, pl.ds(corner, 128)].astype(f32)
+                b = parts[i, :, pl.ds(corner, 128)].astype(f32)
+                lows = jnp.where(left, a, pltpu.roll(b, 64, 1))
+                highs = jnp.where(left, pltpu.roll(a, 64, 1), b)
+                start = turn * HALF + 1024 + zl // 2 * 128
+                out[:, start : start + 128] = jnp.where(half == 0, lows, highs).astype(bf16)
+    bands = [pl.ds(i * 64, 64) for i in range(4)]
+    for copy in fetch([out.at[k] for k in bands], [out_far.at[k] for k in bands], sems):
         copy.wait()
 
 
@@ -270,25 +268,27 @@
         )
 
     with jax.named_scope("hidden_exchange"):
-        mine, theirs = call(
-            split_hidden_kernel,
-            (shape((256, 2 * HALF), bf16),) * 2,
-            hidden, sent,
-            scratch=room(hidden) + [pltpu.VMEM((256, 2 * HALF), bf16)] * 2 + [dmas((12,))],
-            moved=5 * 2**20,
-            limit=MOST,
-            in_specs=[far, pl.BlockSpec(memory_space=pl.ANY)],
-            out_specs=(far, far),
-        )
+        def pack(keep, after):
+            return call(
+                functools.partial(pack_hidden_kernel, keep),
+                shape((256, 2 * HALF), bf16),
+                hidden, after,
+                scratch=[pltpu.VMEM((8, 256, 384), bf16), pltpu.VMEM((256, 2 * HALF), bf16), dmas((8,))],
+                moved=2**22,
+                limit=MOST,
+                in_specs=[far, pl.BlockSpec(memory_space=pl.ANY)],
+                out_specs=far,
+            )
+
+        mine = pack(True, sent)
 
     with jax.named_scope("replica_exchange"):
         got = lax.all_to_all(sent, ("xl", "y"), 0, 0)
-        got, mine, theirs = lax.optimization_barrier((got, mine, theirs))
 
     with jax.named_scope("hidden_exchange"):
         swap, cross = [(0, 1), (1, 0)], [(0, 3), (1, 2), (2, 1), (3, 0)]
         xh_side = lax.ppermute(mine, "xh", swap)
-        theirs, xh_side = lax.optimization_barrier((theirs, xh_side))
+        theirs = pack(False, got)
         xl_side = lax.ppermute(theirs, "xl", swap)
         across = lax.ppermute(theirs, ("xl", "xh"), cross)
 
@@ -297,7 +297,7 @@
             new_weight_kernel,
             shape((16, tiles // 2, 16, PAIR), bf16),
             got, weight, table,
-            moved=2**19,
+            flops=OWN_FLOPS,
             in_specs=[vm] * 3,
             out_specs=vm,
         )
@@ -312,6 +312,7 @@
 
     with jax.named_scope("weight_exchange"):
         along_z = lax.all_to_all(pieces, "z", 0, 0)
+        along_z, xh_side = lax.optimization_barrier((along_z, xh_side))
         along_y = lax.all_to_all(jnp.broadcast_to(along_z, (4,) + along_z.shape), "y", 0, 0)
         matrix = shape((HALF, 512), bf16)
         own = call(fill_kernel, matrix, along_y, in_specs=[vm], out_specs=vm)

time: 103 us -> 102 us (level)
  the two profiles are of different devices: /device:TPU:256 before, /device:TPU:32 now
where the time goes in v4:
time: 102 us; the launch traced here: 101 us
  starting transfers between devices  36.9 us (36%)
  Pallas kernels  21.9 us (21%)
  waiting for transfers between devices  21.4 us (21%)
  blocking collectives  20 us (20%)
    pallas_call x10, Pallas kernels, call(): pl.pallas_call(kernel, out_shape=out_shape, scratch_shapes=list(scratch),...  21.9 us
    all_to_all x1, blocking collectives, shards(): lax.all_to_all(jnp.broadcast_to(along_z, (4,) + along_z.shape), 'y', 0, 0)  20 us
    all_to_all x1, starting transfers between devices, shards(): along_z = lax.all_to_all(pieces, 'z', 0, 0)  15.2 us
    all_to_all x1, waiting for transfers between devices, shards(): along_z = lax.all_to_all(pieces, 'z', 0, 0)  10.5 us
    all_to_all x1, waiting for transfers between devices, shards(): back = lax.all_to_all(partial, ('xl', 'xh'), 0, 0)  10.1 us
    all_to_all x1, starting transfers between devices, shards(): got = lax.all_to_all(sent, ('xl', 'y'), 0, 0)  5.41 us
    ppermute x1, starting transfers between devices, shards(): xh_side = lax.ppermute(mine, 'xh', swap)  4.64 us
    all_to_all x1, starting transfers between devices, shards(): back = lax.all_to_all(partial, ('xl', 'xh'), 0, 0)  3.66 us
  transfers between devices with their start and end apart: 7, of which 3 were waited for; matrix products, arithmetic and copies ran while one was open for 0% of the time, Pallas kernels for 15%

profile of v4, /device:TPU:32, one launch (start us, length us, event | category | flops | bytes accessed | tf_op | source)
XLA Modules:
  0.0 101.3 jit_solution(14924904001898157778)
XLA Ops:
  0.6 2.4 %own_values.1.after.sent = f32[8,16,128]{2,1,0:T(8,128)} custom-call(f32[1,10,64,128]{3,2,1,0:T(8,128)} %momentum.3, bf16[1,10,64,128]{3,2,1,0:T(8,128)(2,1)} %gradient.1, s32[20,1,32]{2,1,0:T(1,128)} %bitcast.2, s32[20]{0:T(128)} %bitcast.4, bf16[5,128,128]{2,1,0:T(8,128)(2,1)} %constant.2.clone.table_far.table), custom_call_target="tpu_custom_call" | custom-call | bytes 524288 | tf_op jit(solution)/shard_map/own_values/pallas_call | solution.py:237
  3.1 5.4 %all-to-all-start = ((f32[8,16,128]{2,1,0:T(8,128)}), f32[8,16,128]{2,1,0:T(8,128)S(1)}, u32[]{:S(2)}, u32[]{:S(2)}) async-start(f32[8,16,128]{2,1,0:T(8,128)} %own_values.1.after.sent), calls=%async_computation | async-start | bytes 131072 | tf_op jit(solution)/shard_map/replica_exchange/all_to_all | solution.py:286
  8.5 0.0 copy-start.8
  8.5 2.8 %hidden_exchange.2.mine = bf16[256,2560]{1,0:T(8,128)(2,1)} custom-call(bf16[256,5120]{1,0:T(8,128)(2,1)} %hidden_far.3, f32[8,16,128]{2,1,0:T(8,128)} %own_values.1.after.sent), custom_call_target="tpu_custom_call" | custom-call | bytes 4194304 | tf_op jit(solution)/shard_map/hidden_exchange/pallas_call | solution.py:237
  11.3 4.6 %collective-permute-start = (bf16[256,2560]{1,0:T(8,128)(2,1)}, bf16[256,2560]{1,0:T(8,128)(2,1)S(1)}, u32[]{:S(2)}, u32[]{:S(2)}) collective-permute-start(bf16[256,2560]{1,0:T(8,128)(2,1)} %hidden_exchange.2.mine), channel_id=1, source_target_pairs={{0,32},{32,0},{1,33},{33,1},{2,34},{34,2},{3,35},{35,3},{4,36},{36... | collective-permute-start | bytes 3932168 | tf_op jit(solution)/shard_map/hidden_exchange/ppermute | solution.py:290
  15.9 0.0 all-to-all-done.got.after
  16.0 0.0 copy-done.1
  16.0 2.5 %new_weight.2 = bf16[16,5,16,128]{3,2,1,0:T(8,128)(2,1)} custom-call(f32[8,16,128]{2,1,0:T(8,128)S(1)} %all-to-all-done.got.after, bf16[10,64,128]{2,1,0:T(8,128)(2,1)S(1)} %copy-done.8, bf16[5,128,128]{2,1,0:T(8,128)(2,1)S(1)} %copy-done.1), custom_call_target="tpu_custom_call" | custom-call | flops 99999997952 | tf_op jit(solution)/shard_map/new_weight/pallas_call | solution.py:237
  18.5 15.2 %all-to-all-start.1 = ((bf16[16,5,16,128]{3,2,1,0:T(8,128)(2,1)}), bf16[16,5,16,128]{3,2,1,0:T(8,128)(2,1)S(1)}, u32[]{:S(2)}, u32[]{:S(2)}) async-start(bf16[16,5,16,128]{3,2,1,0:T(8,128)(2,1)} %new_weight.2), calls=%async_computation.1 | async-start | bytes 655360 | tf_op jit(solution)/shard_map/weight_exchange/all_to_all | solution.py:314
  33.7 2.7 %hidden_exchange.3 = bf16[256,2560]{1,0:T(8,128)(2,1)} custom-call(bf16[256,5120]{1,0:T(8,128)(2,1)} %hidden_far.3, f32[8,16,128]{2,1,0:T(8,128)} %copy-done.5), custom_call_target="tpu_custom_call" | custom-call | bytes 4194304 | tf_op jit(solution)/shard_map/hidden_exchange/pallas_call | solution.py:237
  36.4 3.3 %collective-permute-start.1 = (bf16[256,2560]{1,0:T(8,128)(2,1)}, bf16[256,2560]{1,0:T(8,128)(2,1)}, u32[]{:S(2)}, u32[]{:S(2)}) collective-permute-start(bf16[256,2560]{1,0:T(8,128)(2,1)} %hidden_exchange.3), channel_id=1, source_target_pairs={{0,256},{256,0},{1,257},{257,1},{2,258},{258,2},{3,259},{259,3},{4... | collective-permute-start | bytes 3932168 | tf_op jit(solution)/shard_map/hidden_exchange/ppermute | solution.py:292
  39.7 2.6 %collective-permute-start.2 = (bf16[256,2560]{1,0:T(8,128)(2,1)}, bf16[256,2560]{1,0:T(8,128)(2,1)}, u32[]{:S(2)}, u32[]{:S(2)}) collective-permute-start(bf16[256,2560]{1,0:T(8,128)(2,1)} %hidden_exchange.3), channel_id=1, source_target_pairs={{0,288},{32,256},{256,32},{288,0},{1,289},{33,257},{257,33},{289,1... | collective-permute-start | bytes 3932168 | tf_op jit(solution)/shard_map/hidden_exchange/ppermute | solution.py:293
  42.4 10.5 %all-to-all-done.1 = bf16[16,5,16,128]{3,2,1,0:T(8,128)(2,1)S(1)} async-done(((bf16[16,5,16,128]{3,2,1,0:T(8,128)(2,1)}), bf16[16,5,16,128]{3,2,1,0:T(8,128)(2,1)S(1)}, u32[]{:S(2)}, u32[]{:S(2)}) %all-to-all-start.1) | async-done | bytes 327712 | tf_op jit(solution)/shard_map/weight_exchange/all_to_all | solution.py:314
  52.9 0.0 collective-permute-done.xh_side
  52.9 0.2 broadcast_in_dim.3
  53.1 20.0 %all_to_all.20.source = bf16[4,16,5,16,128]{4,3,2,1,0:T(8,128)(2,1)S(1)} all-to-all(bf16[4,16,5,16,128]{4,3,2,1,0:T(8,128)(2,1)S(1)} %broadcast_in_dim.3), channel_id=1, replica_groups=mesh['xl'=2,'y'=4,'xh'=2,'z'=16,'c'=2] {'y'}, dimensions={0} | all-to-all | bytes 2621440 | tf_op jit(solution)/shard_map/weight_exchange/all_to_all | solution.py:316
  73.1 0.2 weight_exchange.1.matrix
  73.3 2.1 %collective-permute-start.3 = (bf16[1280,512]{1,0:T(8,128)(2,1)S(1)}, bf16[1280,512]{1,0:T(8,128)(2,1)S(1)}, u32[]{:S(2)}, u32[]{:S(2)}) collective-permute-start(bf16[1280,512]{1,0:T(8,128)(2,1)S(1)} %weight_exchange.1.matrix), channel_id=1, source_target_pairs={{0,1},{1,0},{2,3},{3,2},{4,5},{5,4},{6,7},{7,6},{8,9},{9,8},{10,11... | collective-permute-start | bytes 3932168 | tf_op jit(solution)/shard_map/weight_exchange/ppermute | solution.py:319
  75.4 0.0 collective-permute-done.1.xl_side
  75.4 0.0 collective-permute-done.2.across
  75.4 2.2 %projection.2.total = f32[4,256,512]{2,1,0:T(8,128)S(1)} custom-call(bf16[256,2560]{1,0:T(8,128)(2,1)S(1)} %copy-done, bf16[256,2560]{1,0:T(8,128)(2,1)S(1)} %collective-permute-done.xh_side, bf16[256,2560]{1,0:T(8,128)(2,1)} %collective-permute-done.1.xl_side, bf16[256,2560]{1,0:T(8,128)(2,1)} %collective-permute-done.2.across, ...), custom_call_target="tpu_custom_call" | custom-call | flops 99999997952 | tf_op jit(solution)/shard_map/projection/pallas_call | solution.py:237
  77.6 0.7 collective-permute-done.3.matrix
  78.4 3.0 %projection.3 = bf16[4,256,512]{2,1,0:T(8,128)(2,1)} custom-call(bf16[256,2560]{1,0:T(8,128)(2,1)S(1)} %copy-done, bf16[256,2560]{1,0:T(8,128)(2,1)S(1)} %collective-permute-done.xh_side, bf16[256,2560]{1,0:T(8,128)(2,1)} %collective-permute-done.1.xl_side, bf16[256,2560]{1,0:T(8,128)(2,1)} %collective-permute-done.2.across, ...), custom_call_target="tpu_custom_call" | custom-call | tf_op jit(solution)/shard_map/projection/pallas_call | solution.py:237
  81.3 0.0 copy-start.2
  81.4 0.0 copy-start.3
  81.4 0.0 copy-start.4
  81.4 0.0 copy-start.7
  81.4 3.7 %all-to-all-start.3 = ((bf16[4,256,512]{2,1,0:T(8,128)(2,1)}), bf16[4,256,512]{2,1,0:T(8,128)(2,1)S(1)}, u32[]{:S(2)}, u32[]{:S(2)}) async-start(bf16[4,256,512]{2,1,0:T(8,128)(2,1)} %projection.3), calls=%async_computation.3 | async-start | bytes 2097152 | tf_op jit(solution)/shard_map/output_exchange/all_to_all | solution.py:342
  85.1 1.9 %momentum.2 = f32[1,10,64,128]{3,2,1,0:T(8,128)} custom-call(f32[1,10,64,128]{3,2,1,0:T(8,128)S(1)} %copy-done.2, bf16[1,10,64,128]{3,2,1,0:T(8,128)(2,1)S(1)} %copy-done.4, s32[20,1,32]{2,1,0:T(1,128)S(1)} %bitcast.3, f32[8,16,128]{2,1,0:T(8,128)S(1)} %copy-done.3, bf16[5,128,128]{2,1,0:T(8,128)(2,1)S(1)} %copy-done.1), custom_call_target="tpu_custom_call" | custom-call | bytes 1048576 | tf_op jit(solution)/shard_map/momentum/pallas_call | solution.py:237
  87.0 3.3 %new_weight.3 = bf16[10,8,128]{2,1,0:T(8,128)(2,1)} custom-call(f32[8,16,128]{2,1,0:T(8,128)S(1)} %copy-done.6, bf16[5,128,128]{2,1,0:T(8,128)(2,1)S(1)} %copy-done.1), custom_call_target="tpu_custom_call" | custom-call | bytes 524288 | tf_op jit(solution)/shard_map/new_weight/pallas_call | solution.py:237
  90.3 10.1 %all-to-all-done.3.back = bf16[4,256,512]{2,1,0:T(8,128)(2,1)S(1)} async-done(((bf16[4,256,512]{2,1,0:T(8,128)(2,1)}), bf16[4,256,512]{2,1,0:T(8,128)(2,1)S(1)}, u32[]{:S(2)}, u32[]{:S(2)}) %all-to-all-start.3) | async-done | bytes 1048608 | tf_op jit(solution)/shard_map/output_exchange/all_to_all | solution.py:342
  100.4 0.9 output_exchange.1
  (12 shorter events, 0.0 us)
Async XLA Ops:
  3.1 12.9 %all-to-all-start = ((f32[8,16,128]{2,1,0:T(8,128)}), f32[8,16,128]{2,1,0:T(8,128)S(1)}, u32[]{:S(2)}, u32[]{:S(2)}) async-start(f32[8,16,128]{2,1,0:T(8,128)} %own_values.1.after.sent), calls=%async_computation | async-start | bytes 131072 | tf_op jit(solution)/shard_map/replica_exchange/all_to_all | solution.py:286
  8.5 7.5 %copy-start.1 = (bf16[5,128,128]{2,1,0:T(8,128)(2,1)S(1)}, bf16[5,128,128]{2,1,0:T(8,128)(2,1)}, u32[]{:S(2)}) copy-start(bf16[5,128,128]{2,1,0:T(8,128)(2,1)} %constant.2.clone.table_far.table) | copy-start | bytes 491524
  8.5 7.5 %copy-start.8 = (bf16[10,64,128]{2,1,0:T(8,128)(2,1)S(1)}, bf16[10,64,128]{2,1,0:T(8,128)(2,1)}, u32[]{:S(2)}) copy-start(bf16[10,64,128]{2,1,0:T(8,128)(2,1)} %weight.1) | copy-start | bytes 491524
  11.3 41.6 %collective-permute-start = (bf16[256,2560]{1,0:T(8,128)(2,1)}, bf16[256,2560]{1,0:T(8,128)(2,1)S(1)}, u32[]{:S(2)}, u32[]{:S(2)}) collective-permute-start(bf16[256,2560]{1,0:T(8,128)(2,1)} %hidden_exchange.2.mine), channel_id=1, source_target_pairs={{0,32},{32,0},{1,33},{33,1},{2,34},{34,2},{3,35},{35,3},{4,36},{36... | collective-permute-start | bytes 3932168 | tf_op jit(solution)/shard_map/hidden_exchange/ppermute | solution.py:290
  16.0 2.5 %copy-start.5 = (f32[8,16,128]{2,1,0:T(8,128)}, f32[8,16,128]{2,1,0:T(8,128)S(1)}, u32[]{:S(2)}) copy-start(f32[8,16,128]{2,1,0:T(8,128)S(1)} %all-to-all-done.got.after) | copy-start | bytes 196612
  18.5 34.5 %all-to-all-start.1 = ((bf16[16,5,16,128]{3,2,1,0:T(8,128)(2,1)}), bf16[16,5,16,128]{3,2,1,0:T(8,128)(2,1)S(1)}, u32[]{:S(2)}, u32[]{:S(2)}) async-start(bf16[16,5,16,128]{3,2,1,0:T(8,128)(2,1)} %new_weight.2), calls=%async_computation.1 | async-start | bytes 655360 | tf_op jit(solution)/shard_map/weight_exchange/all_to_all | solution.py:314
  36.4 39.0 %collective-permute-start.1 = (bf16[256,2560]{1,0:T(8,128)(2,1)}, bf16[256,2560]{1,0:T(8,128)(2,1)}, u32[]{:S(2)}, u32[]{:S(2)}) collective-permute-start(bf16[256,2560]{1,0:T(8,128)(2,1)} %hidden_exchange.3), channel_id=1, source_target_pairs={{0,256},{256,0},{1,257},{257,1},{2,258},{258,2},{3,259},{259,3},{4... | collective-permute-start | bytes 3932168 | tf_op jit(solution)/shard_map/hidden_exchange/ppermute | solution.py:292
  39.7 35.7 %collective-permute-start.2 = (bf16[256,2560]{1,0:T(8,128)(2,1)}, bf16[256,2560]{1,0:T(8,128)(2,1)}, u32[]{:S(2)}, u32[]{:S(2)}) collective-permute-start(bf16[256,2560]{1,0:T(8,128)(2,1)} %hidden_exchange.3), channel_id=1, source_target_pairs={{0,288},{32,256},{256,32},{288,0},{1,289},{33,257},{257,33},{289,1... | collective-permute-start | bytes 3932168 | tf_op jit(solution)/shard_map/hidden_exchange/ppermute | solution.py:293
  73.1 2.3 %copy-start = (bf16[256,2560]{1,0:T(8,128)(2,1)S(1)}, bf16[256,2560]{1,0:T(8,128)(2,1)}, u32[]{:S(2)}) copy-start(bf16[256,2560]{1,0:T(8,128)(2,1)} %hidden_exchange.2.mine) | copy-start | bytes 3932164
  73.3 5.1 %collective-permute-start.3 = (bf16[1280,512]{1,0:T(8,128)(2,1)S(1)}, bf16[1280,512]{1,0:T(8,128)(2,1)S(1)}, u32[]{:S(2)}, u32[]{:S(2)}) collective-permute-start(bf16[1280,512]{1,0:T(8,128)(2,1)S(1)} %weight_exchange.1.matrix), channel_id=1, source_target_pairs={{0,1},{1,0},{2,3},{3,2},{4,5},{5,4},{6,7},{7,6},{8,9},{9,8},{10,11... | collective-permute-start | bytes 3932168 | tf_op jit(solution)/shard_map/weight_exchange/ppermute | solution.py:319
  81.3 3.7 %copy-start.2 = (f32[1,10,64,128]{3,2,1,0:T(8,128)S(1)}, f32[1,10,64,128]{3,2,1,0:T(8,128)}, u32[]{:S(2)}) copy-start(f32[1,10,64,128]{3,2,1,0:T(8,128)} %momentum.3) | copy-start | bytes 983044
  81.4 3.7 %copy-start.3 = (f32[8,16,128]{2,1,0:T(8,128)S(1)}, f32[8,16,128]{2,1,0:T(8,128)}, u32[]{:S(2)}) copy-start(f32[8,16,128]{2,1,0:T(8,128)} %own_values.1.after.sent) | copy-start | bytes 196612
  81.4 3.7 %copy-start.4 = (bf16[1,10,64,128]{3,2,1,0:T(8,128)(2,1)S(1)}, bf16[1,10,64,128]{3,2,1,0:T(8,128)(2,1)}, u32[]{:S(2)}) copy-start(bf16[1,10,64,128]{3,2,1,0:T(8,128)(2,1)} %gradient.1) | copy-start | bytes 491524
  81.4 3.7 %copy-start.7 = (s32[1,20,32]{2,0,1:T(1,128)S(1)}, s32[1,20,32]{2,0,1:T(1,128)}, u32[]{:S(2)}) copy-start(s32[1,20,32]{2,0,1:T(1,128)} %param.11) | copy-start | bytes 7684
  81.4 5.6 %copy-start.6 = (f32[8,16,128]{2,1,0:T(8,128)S(1)}, f32[8,16,128]{2,1,0:T(8,128)}, u32[]{:S(2)}) copy-start(f32[8,16,128]{2,1,0:T(8,128)} %copy-done.5) | copy-start | bytes 196612
  81.4 19.0 %all-to-all-start.3 = ((bf16[4,256,512]{2,1,0:T(8,128)(2,1)}), bf16[4,256,512]{2,1,0:T(8,128)(2,1)S(1)}, u32[]{:S(2)}, u32[]{:S(2)}) async-start(bf16[4,256,512]{2,1,0:T(8,128)(2,1)} %projection.3), calls=%async_computation.3 | async-start | bytes 2097152 | tf_op jit(solution)/shard_map/output_exchange/all_to_all | solution.py:342

commit v5 on v4

--- a/solution.py
+++ b/solution.py
@@ -1,5 +1,3 @@
-import functools
-
 import jax
 import jax.numpy as jnp
 import numpy as np
@@ -20,6 +18,7 @@
 MOST = 60 * 2**20
 WIDE_T, WIDE, BLOCK_ONES = 0, 2, 4
 HALF = 1280
+BAND = 64
 OWN_FLOPS = 100 * 10**9
 
 
@@ -72,36 +71,6 @@
     return jnp.concatenate([indices[b] for b in range(indices.shape[0])], axis=1)
 
 
-def pack_hidden_kernel(keep, hidden_far, after, out_far, parts, out, sems):
-    half = lax.axis_index("xl") if keep else 1 - lax.axis_index("xl")
-    c = lax.axis_index("c")
-    sources = []
-    for turn in range(2):
-        core = c if turn == 0 else 1 - c
-        for zl in range(4):
-            start = pl.multiple_of(zl * 1280 + core * 640 + half * 256, 128)
-            sources.append(hidden_far.at[:, pl.ds(start, 384)])
-    copies = fetch(sources, [parts.at[i] for i in range(8)], sems)
-    left = lax.broadcasted_iota(jnp.int32, (256, 128), 1) < 64
-    corner, body = pl.multiple_of(256 - half * 256, 128), pl.multiple_of(half * 128, 128)
-    for turn in range(2):
-        for zl in range(4):
-            i = turn * 4 + zl
-            copies[i].wait()
-            start = turn * HALF + zl * 256
-            out[:, start : start + 256] = parts[i, :, pl.ds(body, 256)]
-            if zl % 2 == 1:
-                a = parts[i - 1, :, pl.ds(corner, 128)].astype(f32)
-                b = parts[i, :, pl.ds(corner, 128)].astype(f32)
-                lows = jnp.where(left, a, pltpu.roll(b, 64, 1))
-                highs = jnp.where(left, pltpu.roll(a, 64, 1), b)
-                start = turn * HALF + 1024 + zl // 2 * 128
-                out[:, start : start + 128] = jnp.where(half == 0, lows, highs).astype(bf16)
-    bands = [pl.ds(i * 64, 64) for i in range(4)]
-    for copy in fetch([out.at[k] for k in bands], [out_far.at[k] for k in bands], sems):
-        copy.wait()
-
-
 def fetch(sources, targets, sems):
     sems = sems if isinstance(sems, list) else [sems.at[i] for i in range(len(sources))]
     copies = [pltpu.make_async_copy(*each) for each in zip(sources, targets, sems)]
@@ -110,10 +79,51 @@
     return copies
 
 
-def values_kernel(momentum_far, gradient_far, indices_far, counts_far, table_far, sent, momentum, gradient, indices, counts, table, sems):
+def start_hidden(hidden_far, hidden, sems):
+    bands = [pl.ds(i * BAND, BAND) for i in range(256 // BAND)]
+    return fetch([hidden_far.at[k] for k in bands], [hidden.at[k] for k in bands], sems)
+
+
+def pack_hidden(half, copies, hidden, out, out_far, sems):
+    c = lax.axis_index("c")
+    left = lax.broadcasted_iota(jnp.int32, (BAND, 128), 1) < 64
+    leaving = []
+    for i, copy in enumerate(copies):
+        copy.wait()
+        band = pl.ds(i * BAND, BAND)
+        for turn in range(2):
+            core = c if turn == 0 else 1 - c
+            corners = []
+            for zl in range(4):
+                first = zl * 1280 + core * 640
+                start = turn * HALF + zl * 256
+                out[band, start : start + 256] = hidden[band, pl.ds(pl.multiple_of(first + half * 384, 128), 256)]
+                corners.append(hidden[band, pl.ds(pl.multiple_of(first + 256, 128), 128)].astype(f32))
+            for pair in range(2):
+                a, b = corners[2 * pair : 2 * pair + 2]
+                lows = jnp.where(left, a, pltpu.roll(b, 64, 1))
+                highs = jnp.where(left, pltpu.roll(a, 64, 1), b)
+                start = turn * HALF + 1024 + pair * 128
+                out[band, start : start + 128] = jnp.where(half == 0, lows, highs).astype(bf16)
+        leaving += fetch([out.at[band]], [out_far.at[band]], [sems.at[len(copies) + i]])
+    for copy in leaving:
+        copy.wait()
+
+
+def pack_theirs_kernel(hidden_far, after, out_far, parts, out, sems):
+    half = 1 - lax.axis_index("xl")
+    pack_hidden(half, start_hidden(hidden_far, parts, sems), parts, out, out_far, sems)
+
+
+def values_kernel(
+    momentum_far, gradient_far, indices_far, counts_far, table_far, hidden_far, sent, mine_far,
+    momentum, gradient, indices, counts, table, parts, mine, sems, hidden_sems,
+):
     copies = fetch(
         (indices_far, table_far, momentum_far, gradient_far, counts_far), (indices, table, momentum, gradient, counts), sems
     )
+    half = lax.axis_index("xl")
+    hidden_copies = start_hidden(hidden_far, parts, hidden_sems)
     tiles = momentum.shape[1]
     copies[0].wait()
     copies[1].wait()
@@ -127,14 +137,15 @@
     for t in range(tiles):
         e = slice(t * SIDE, t * SIDE + SIDE)
         moment = decay_rate * momentum[0, t] + gradient[0, t].astype(f32)
-        half = dot3(split(moment), (high[:, e], low[:, e]))
-        value = jnp.sum(half * rows[:, e], axis=0, keepdims=True)
+        mixed = dot3(split(moment), (high[:, e], low[:, e]))
+        value = jnp.sum(mixed * rows[:, e], axis=0, keepdims=True)
         live = (lane & 31) < jnp.where(lane < 32, counts[2 * t], counts[2 * t + 1])
         out.append(jnp.concatenate([jnp.where(live, value, 0.0), line[:, e].astype(f32)], axis=1))
     out.append(jnp.zeros((sent.shape[1] - tiles, PAIR), f32))
     out = jnp.concatenate(out, axis=0)
     for r in range(sent.shape[0]):
         sent[r] = out
+    pack_hidden(half, hidden_copies, parts, mine, mine_far, hidden_sems)
 
 
 def momentum_kernel(momentum, gradient, indices, sent, table, out):
@@ -256,31 +267,17 @@
 
     lines = indices.reshape(2 * tiles, 1, indices.shape[2])
     with jax.named_scope("own_values"):
-        sent = call(
+        packing = room(hidden) + [pltpu.VMEM((256, 2 * HALF), bf16)]
+        sent, mine = call(
             values_kernel,
-            shape((8, 16, PAIR), f32),
-            momentum, gradient, lines, counts[0], table,
-            scratch=room(momentum, gradient, lines) + [pltpu.SMEM((2 * tiles,), jnp.int32)] + room(table) + [dmas((5,))],
+            (shape((8, 16, PAIR), f32), shape((256, 2 * HALF), bf16)),
+            momentum, gradient, lines, counts[0], table, hidden,
+            scratch=room(momentum, gradient, lines) + [pltpu.SMEM((2 * tiles,), jnp.int32)] + room(table) + packing + [dmas((5,)), dmas((8,))],
             moved=2**19,
             limit=MOST,
-            in_specs=[far] * 5,
-            out_specs=vm,
-        )
-
-    with jax.named_scope("hidden_exchange"):
-        def pack(keep, after):
-            return call(
-                functools.partial(pack_hidden_kernel, keep),
-                shape((256, 2 * HALF), bf16),
-                hidden, after,
-                scratch=[pltpu.VMEM((8, 256, 384), bf16), pltpu.VMEM((256, 2 * HALF), bf16), dmas((8,))],
-                moved=2**22,
-                limit=MOST,
-                in_specs=[far, pl.BlockSpec(memory_space=pl.ANY)],
-                out_specs=far,
-            )
-
-        mine = pack(True, sent)
+            in_specs=[far] * 6,
+            out_specs=(vm, far),
+        )
 
     with jax.named_scope("replica_exchange"):
         got = lax.all_to_all(sent, ("xl", "y"), 0, 0)
@@ -288,7 +285,16 @@
     with jax.named_scope("hidden_exchange"):
         swap, cross = [(0, 1), (1, 0)], [(0, 3), (1, 2), (2, 1), (3, 0)]
         xh_side = lax.ppermute(mine, "xh", swap)
-        theirs = pack(False, got)
+        theirs = call(
+            pack_theirs_kernel,
+            shape((256, 2 * HALF), bf16),
+            hidden, got,
+            scratch=packing + [dmas((8,))],
+            moved=2**22,
+            limit=MOST,
+            in_specs=[far, pl.BlockSpec(memory_space=pl.ANY)],
+            out_specs=far,
+        )
         xl_side = lax.ppermute(theirs, "xl", swap)
         across = lax.ppermute(theirs, ("xl", "xh"), cross)
 

time: 102 us -> 101 us (level)
  blocking collectives: 20 us -> 18.5 us
  Pallas kernels: 21.9 us -> 20.5 us
  starting transfers between devices: 36.9 us -> 38.2 us
    ppermute x1, starting transfers between devices: 2.65 us -> 4.55 us  [shards(): across = lax.ppermute(theirs, ('xl', 'xh'), cross)]
    all_to_all x1, waiting for transfers between devices: 0.01 us -> 1.71 us  [shards(): got = lax.all_to_all(sent, ('xl', 'y'), 0, 0)]
    all_to_all x1, blocking collectives: 20 us -> 18.5 us  [shards(): lax.all_to_all(jnp.broadcast_to(along_z, (4,) + along_z.shape), 'y', 0, 0)]
    pallas_call x10 -> x9, Pallas kernels: 21.9 us -> 20.5 us  [call(): pl.pallas_call(kernel, out_shape=out_shape, scratch_shapes=list(scratch),...]
    all_to_all x1, waiting for transfers between devices: 10.5 us -> 9.37 us  [shards(): along_z = lax.all_to_all(pieces, 'z', 0, 0)]
  transfers between devices with their start and end apart: 7 -> 7, of which waited for: 3 -> 4; matrix products, arithmetic and copies ran while one was open for 0% -> 0% of each run, Pallas kernels for 15% -> 13%
where the time goes in v5:
time: 101 us; the launch traced here: 100 us
  starting transfers between devices  38.2 us (38%)
  waiting for transfers between devices  21.9 us (22%)
  Pallas kernels  20.5 us (20%)
  blocking collectives  18.5 us (18%)
    pallas_call x9, Pallas kernels, call(): pl.pallas_call(kernel, out_shape=out_shape, scratch_shapes=list(scratch),...  20.5 us
    all_to_all x1, blocking collectives, shards(): lax.all_to_all(jnp.broadcast_to(along_z, (4,) + along_z.shape), 'y', 0, 0)  18.5 us
    all_to_all x1, starting transfers between devices, shards(): along_z = lax.all_to_all(pieces, 'z', 0, 0)  15.2 us
    all_to_all x1, waiting for transfers between devices, shards(): back = lax.all_to_all(partial, ('xl', 'xh'), 0, 0)  10.1 us
    all_to_all x1, waiting for transfers between devices, shards(): along_z = lax.all_to_all(pieces, 'z', 0, 0)  9.37 us
    all_to_all x1, starting transfers between devices, shards(): got = lax.all_to_all(sent, ('xl', 'y'), 0, 0)  5.41 us
    ppermute x1, starting transfers between devices, shards(): xh_side = lax.ppermute(mine, 'xh', swap)  4.63 us
    ppermute x1, starting transfers between devices, shards(): across = lax.ppermute(theirs, ('xl', 'xh'), cross)  4.55 us
  transfers between devices with their start and end apart: 7, of which 4 were waited for; matrix products, arithmetic and copies ran while one was open for 0% of the time, Pallas kernels for 13%

profile of v5, /device:TPU:32, one launch (start us, length us, event | category | flops | bytes accessed | tf_op | source)
XLA Modules:
  0.0 100.1 jit_solution(8108564353602850645)
XLA Ops:
  0.6 0.0 copy-start
  0.7 4.0 %own_values.1 = (f32[8,16,128]{2,1,0:T(8,128)}, bf16[256,2560]{1,0:T(8,128)(2,1)}) custom-call(f32[1,10,64,128]{3,2,1,0:T(8,128)} %momentum.3, bf16[1,10,64,128]{3,2,1,0:T(8,128)(2,1)} %gradient.1, s32[20,1,32]{2,1,0:T(1,128)} %bitcast.2, s32[20]{0:T(128)} %bitcast.4, bf16[5,128,128]{2,1,0:T(8,128)(2,1)} %constant.2.clone.table_far.table, ...), custom_call_target="tpu_custom_call" | custom-call | bytes 524288 | tf_op jit(solution)/shard_map/own_values/pallas_call | solution.py:248
  4.7 5.4 %all-to-all-start = ((f32[8,16,128]{2,1,0:T(8,128)}), f32[8,16,128]{2,1,0:T(8,128)S(1)}, u32[]{:S(2)}, u32[]{:S(2)}) async-start(f32[8,16,128]{2,1,0:T(8,128)} %get-tuple-element.8.sent), calls=%async_computation | async-start | bytes 131072 | tf_op jit(solution)/shard_map/replica_exchange/all_to_all | solution.py:283
  10.1 4.6 %collective-permute-start = (bf16[256,2560]{1,0:T(8,128)(2,1)}, bf16[256,2560]{1,0:T(8,128)(2,1)S(1)}, u32[]{:S(2)}, u32[]{:S(2)}) collective-permute-start(bf16[256,2560]{1,0:T(8,128)(2,1)} %get-tuple-element.7.mine), channel_id=1, source_target_pairs={{0,32},{32,0},{1,33},{33,1},{2,34},{34,2},{3,35},{35,3},{4,36},{36... | collective-permute-start | bytes 3932168 | tf_op jit(solution)/shard_map/hidden_exchange/ppermute | solution.py:287
  14.7 1.7 %all-to-all-done.got.after = f32[8,16,128]{2,1,0:T(8,128)S(1)} async-done(((f32[8,16,128]{2,1,0:T(8,128)}), f32[8,16,128]{2,1,0:T(8,128)S(1)}, u32[]{:S(2)}, u32[]{:S(2)}) %all-to-all-start) | async-done | bytes 65568 | tf_op jit(solution)/shard_map/replica_exchange/all_to_all | solution.py:283
  16.4 0.0 copy-done.8
  16.4 2.5 %new_weight.2 = bf16[16,5,16,128]{3,2,1,0:T(8,128)(2,1)} custom-call(f32[8,16,128]{2,1,0:T(8,128)S(1)} %all-to-all-done.got.after, bf16[10,64,128]{2,1,0:T(8,128)(2,1)S(1)} %copy-done.8, bf16[5,128,128]{2,1,0:T(8,128)(2,1)S(1)} %copy-done), custom_call_target="tpu_custom_call" | custom-call | flops 99999997952 | tf_op jit(solution)/shard_map/new_weight/pallas_call | solution.py:248
  18.9 15.2 %all-to-all-start.1 = ((bf16[16,5,16,128]{3,2,1,0:T(8,128)(2,1)}), bf16[16,5,16,128]{3,2,1,0:T(8,128)(2,1)S(1)}, u32[]{:S(2)}, u32[]{:S(2)}) async-start(bf16[16,5,16,128]{3,2,1,0:T(8,128)(2,1)} %new_weight.2), calls=%async_computation.1 | async-start | bytes 655360 | tf_op jit(solution)/shard_map/weight_exchange/all_to_all | solution.py:320
  34.1 2.6 %hidden_exchange.1 = bf16[256,2560]{1,0:T(8,128)(2,1)} custom-call(bf16[256,5120]{1,0:T(8,128)(2,1)} %hidden_far.3, f32[8,16,128]{2,1,0:T(8,128)} %copy-done.4), custom_call_target="tpu_custom_call" | custom-call | bytes 4194304 | tf_op jit(solution)/shard_map/hidden_exchange/pallas_call | solution.py:248
  36.7 2.6 %collective-permute-start.1 = (bf16[256,2560]{1,0:T(8,128)(2,1)}, bf16[256,2560]{1,0:T(8,128)(2,1)}, u32[]{:S(2)}, u32[]{:S(2)}) collective-permute-start(bf16[256,2560]{1,0:T(8,128)(2,1)} %hidden_exchange.1), channel_id=1, source_target_pairs={{0,256},{256,0},{1,257},{257,1},{2,258},{258,2},{3,259},{259,3},{4... | collective-permute-start | bytes 3932168 | tf_op jit(solution)/shard_map/hidden_exchange/ppermute | solution.py:298
  39.3 4.5 %collective-permute-start.2 = (bf16[256,2560]{1,0:T(8,128)(2,1)}, bf16[256,2560]{1,0:T(8,128)(2,1)}, u32[]{:S(2)}, u32[]{:S(2)}) collective-permute-start(bf16[256,2560]{1,0:T(8,128)(2,1)} %hidden_exchange.1), channel_id=1, source_target_pairs={{0,288},{32,256},{256,32},{288,0},{1,289},{33,257},{257,33},{289,1... | collective-permute-start | bytes 3932168 | tf_op jit(solution)/shard_map/hidden_exchange/ppermute | solution.py:299
  43.8 9.4 %all-to-all-done.1 = bf16[16,5,16,128]{3,2,1,0:T(8,128)(2,1)S(1)} async-done(((bf16[16,5,16,128]{3,2,1,0:T(8,128)(2,1)}), bf16[16,5,16,128]{3,2,1,0:T(8,128)(2,1)S(1)}, u32[]{:S(2)}, u32[]{:S(2)}) %all-to-all-start.1) | async-done | bytes 327712 | tf_op jit(solution)/shard_map/weight_exchange/all_to_all | solution.py:320
  53.2 0.0 collective-permute-done.xh_side
  53.2 0.2 broadcast_in_dim.3
  53.4 18.5 %all_to_all.20.source = bf16[4,16,5,16,128]{4,3,2,1,0:T(8,128)(2,1)S(1)} all-to-all(bf16[4,16,5,16,128]{4,3,2,1,0:T(8,128)(2,1)S(1)} %broadcast_in_dim.3), channel_id=1, replica_groups=mesh['xl'=2,'y'=4,'xh'=2,'z'=16,'c'=2] {'y'}, dimensions={0} | all-to-all | bytes 2621440 | tf_op jit(solution)/shard_map/weight_exchange/all_to_all | solution.py:322
  71.8 0.2 weight_exchange.1.matrix
  72.1 2.1 %collective-permute-start.3 = (bf16[1280,512]{1,0:T(8,128)(2,1)S(1)}, bf16[1280,512]{1,0:T(8,128)(2,1)S(1)}, u32[]{:S(2)}, u32[]{:S(2)}) collective-permute-start(bf16[1280,512]{1,0:T(8,128)(2,1)S(1)} %weight_exchange.1.matrix), channel_id=1, source_target_pairs={{0,1},{1,0},{2,3},{3,2},{4,5},{5,4},{6,7},{7,6},{8,9},{9,8},{10,11... | collective-permute-start | bytes 3932168 | tf_op jit(solution)/shard_map/weight_exchange/ppermute | solution.py:325
  74.1 0.0 collective-permute-done.1.xl_side
  74.1 0.0 collective-permute-done.2.across
  74.2 2.2 %projection.2.total = f32[4,256,512]{2,1,0:T(8,128)S(1)} custom-call(bf16[256,2560]{1,0:T(8,128)(2,1)S(1)} %copy-done.1, bf16[256,2560]{1,0:T(8,128)(2,1)S(1)} %collective-permute-done.xh_side, bf16[256,2560]{1,0:T(8,128)(2,1)} %collective-permute-done.1.xl_side, bf16[256,2560]{1,0:T(8,128)(2,1)} %collective-permute-done.2.across, ...), custom_call_target="tpu_custom_call" | custom-call | flops 99999997952 | tf_op jit(solution)/shard_map/projection/pallas_call | solution.py:248
  76.4 0.7 collective-permute-done.3.matrix
  77.1 3.0 %projection.3 = bf16[4,256,512]{2,1,0:T(8,128)(2,1)} custom-call(bf16[256,2560]{1,0:T(8,128)(2,1)S(1)} %copy-done.1, bf16[256,2560]{1,0:T(8,128)(2,1)S(1)} %collective-permute-done.xh_side, bf16[256,2560]{1,0:T(8,128)(2,1)} %collective-permute-done.1.xl_side, bf16[256,2560]{1,0:T(8,128)(2,1)} %collective-permute-done.2.across, ...), custom_call_target="tpu_custom_call" | custom-call | tf_op jit(solution)/shard_map/projection/pallas_call | solution.py:248
  80.1 0.0 copy-start.2
  80.1 0.0 copy-start.3
  80.1 0.0 copy-start.6
  80.1 0.0 copy-start.7
  80.1 3.8 %all-to-all-start.3 = ((bf16[4,256,512]{2,1,0:T(8,128)(2,1)}), bf16[4,256,512]{2,1,0:T(8,128)(2,1)S(1)}, u32[]{:S(2)}, u32[]{:S(2)}) async-start(bf16[4,256,512]{2,1,0:T(8,128)(2,1)} %projection.3), calls=%async_computation.3 | async-start | bytes 2097152 | tf_op jit(solution)/shard_map/output_exchange/all_to_all | solution.py:348
  83.9 1.9 %momentum.2 = f32[1,10,64,128]{3,2,1,0:T(8,128)} custom-call(f32[1,10,64,128]{3,2,1,0:T(8,128)S(1)} %copy-done.2, bf16[1,10,64,128]{3,2,1,0:T(8,128)(2,1)S(1)} %copy-done.3, s32[20,1,32]{2,1,0:T(1,128)S(1)} %bitcast.3, f32[8,16,128]{2,1,0:T(8,128)S(1)} %copy-done.6, bf16[5,128,128]{2,1,0:T(8,128)(2,1)S(1)} %copy-done), custom_call_target="tpu_custom_call" | custom-call | bytes 1048576 | tf_op jit(solution)/shard_map/momentum/pallas_call | solution.py:248
  85.8 0.0 copy-done.5
  85.8 3.3 %new_weight.3 = bf16[10,8,128]{2,1,0:T(8,128)(2,1)} custom-call(f32[8,16,128]{2,1,0:T(8,128)S(1)} %copy-done.5, bf16[5,128,128]{2,1,0:T(8,128)(2,1)S(1)} %copy-done), custom_call_target="tpu_custom_call" | custom-call | bytes 524288 | tf_op jit(solution)/shard_map/new_weight/pallas_call | solution.py:248
  89.1 10.1 %all-to-all-done.3.back = bf16[4,256,512]{2,1,0:T(8,128)(2,1)S(1)} async-done(((bf16[4,256,512]{2,1,0:T(8,128)(2,1)}), bf16[4,256,512]{2,1,0:T(8,128)(2,1)S(1)}, u32[]{:S(2)}, u32[]{:S(2)}) %all-to-all-start.3) | async-done | bytes 1048608 | tf_op jit(solution)/shard_map/output_exchange/all_to_all | solution.py:348
  99.2 0.9 output_exchange.1
  (11 shorter events, 0.0 us)
Async XLA Ops:
  0.6 15.8 %copy-start = (bf16[5,128,128]{2,1,0:T(8,128)(2,1)S(1)}, bf16[5,128,128]{2,1,0:T(8,128)(2,1)}, u32[]{:S(2)}) copy-start(bf16[5,128,128]{2,1,0:T(8,128)(2,1)} %constant.2.clone.table_far.table) | copy-start | bytes 491524
  0.6 15.8 %copy-start.8 = (bf16[10,64,128]{2,1,0:T(8,128)(2,1)S(1)}, bf16[10,64,128]{2,1,0:T(8,128)(2,1)}, u32[]{:S(2)}) copy-start(bf16[10,64,128]{2,1,0:T(8,128)(2,1)} %weight.1) | copy-start | bytes 491524
  4.7 11.8 %all-to-all-start = ((f32[8,16,128]{2,1,0:T(8,128)}), f32[8,16,128]{2,1,0:T(8,128)S(1)}, u32[]{:S(2)}, u32[]{:S(2)}) async-start(f32[8,16,128]{2,1,0:T(8,128)} %get-tuple-element.8.sent), calls=%async_computation | async-start | bytes 131072 | tf_op jit(solution)/shard_map/replica_exchange/all_to_all | solution.py:283
  10.1 43.1 %collective-permute-start = (bf16[256,2560]{1,0:T(8,128)(2,1)}, bf16[256,2560]{1,0:T(8,128)(2,1)S(1)}, u32[]{:S(2)}, u32[]{:S(2)}) collective-permute-start(bf16[256,2560]{1,0:T(8,128)(2,1)} %get-tuple-element.7.mine), channel_id=1, source_target_pairs={{0,32},{32,0},{1,33},{33,1},{2,34},{34,2},{3,35},{35,3},{4,36},{36... | collective-permute-start | bytes 3932168 | tf_op jit(solution)/shard_map/hidden_exchange/ppermute | solution.py:287
  16.4 2.5 %copy-start.4 = (f32[8,16,128]{2,1,0:T(8,128)}, f32[8,16,128]{2,1,0:T(8,128)S(1)}, u32[]{:S(2)}) copy-start(f32[8,16,128]{2,1,0:T(8,128)S(1)} %all-to-all-done.got.after) | copy-start | bytes 196612
  18.9 34.3 %all-to-all-start.1 = ((bf16[16,5,16,128]{3,2,1,0:T(8,128)(2,1)}), bf16[16,5,16,128]{3,2,1,0:T(8,128)(2,1)S(1)}, u32[]{:S(2)}, u32[]{:S(2)}) async-start(bf16[16,5,16,128]{3,2,1,0:T(8,128)(2,1)} %new_weight.2), calls=%async_computation.1 | async-start | bytes 655360 | tf_op jit(solution)/shard_map/weight_exchange/all_to_all | solution.py:320
  36.7 37.4 %collective-permute-start.1 = (bf16[256,2560]{1,0:T(8,128)(2,1)}, bf16[256,2560]{1,0:T(8,128)(2,1)}, u32[]{:S(2)}, u32[]{:S(2)}) collective-permute-start(bf16[256,2560]{1,0:T(8,128)(2,1)} %hidden_exchange.1), channel_id=1, source_target_pairs={{0,256},{256,0},{1,257},{257,1},{2,258},{258,2},{3,259},{259,3},{4... | collective-permute-start | bytes 3932168 | tf_op jit(solution)/shard_map/hidden_exchange/ppermute | solution.py:298
  39.3 34.9 %collective-permute-start.2 = (bf16[256,2560]{1,0:T(8,128)(2,1)}, bf16[256,2560]{1,0:T(8,128)(2,1)}, u32[]{:S(2)}, u32[]{:S(2)}) collective-permute-start(bf16[256,2560]{1,0:T(8,128)(2,1)} %hidden_exchange.1), channel_id=1, source_target_pairs={{0,288},{32,256},{256,32},{288,0},{1,289},{33,257},{257,33},{289,1... | collective-permute-start | bytes 3932168 | tf_op jit(solution)/shard_map/hidden_exchange/ppermute | solution.py:299
  71.8 2.3 %copy-start.1 = (bf16[256,2560]{1,0:T(8,128)(2,1)S(1)}, bf16[256,2560]{1,0:T(8,128)(2,1)}, u32[]{:S(2)}) copy-start(bf16[256,2560]{1,0:T(8,128)(2,1)} %get-tuple-element.7.mine) | copy-start | bytes 3932164
  72.1 5.1 %collective-permute-start.3 = (bf16[1280,512]{1,0:T(8,128)(2,1)S(1)}, bf16[1280,512]{1,0:T(8,128)(2,1)S(1)}, u32[]{:S(2)}, u32[]{:S(2)}) collective-permute-start(bf16[1280,512]{1,0:T(8,128)(2,1)S(1)} %weight_exchange.1.matrix), channel_id=1, source_target_pairs={{0,1},{1,0},{2,3},{3,2},{4,5},{5,4},{6,7},{7,6},{8,9},{9,8},{10,11... | collective-permute-start | bytes 3932168 | tf_op jit(solution)/shard_map/weight_exchange/ppermute | solution.py:325
  80.1 3.8 %copy-start.2 = (f32[1,10,64,128]{3,2,1,0:T(8,128)S(1)}, f32[1,10,64,128]{3,2,1,0:T(8,128)}, u32[]{:S(2)}) copy-start(f32[1,10,64,128]{3,2,1,0:T(8,128)} %momentum.3) | copy-start | bytes 983044
  80.1 3.8 %copy-start.3 = (bf16[1,10,64,128]{3,2,1,0:T(8,128)(2,1)S(1)}, bf16[1,10,64,128]{3,2,1,0:T(8,128)(2,1)}, u32[]{:S(2)}) copy-start(bf16[1,10,64,128]{3,2,1,0:T(8,128)(2,1)} %gradient.1) | copy-start | bytes 491524
  80.1 3.8 %copy-start.6 = (f32[8,16,128]{2,1,0:T(8,128)S(1)}, f32[8,16,128]{2,1,0:T(8,128)}, u32[]{:S(2)}) copy-start(f32[8,16,128]{2,1,0:T(8,128)} %get-tuple-element.8.sent) | copy-start | bytes 196612
  80.1 3.8 %copy-start.7 = (s32[1,20,32]{2,0,1:T(1,128)S(1)}, s32[1,20,32]{2,0,1:T(1,128)}, u32[]{:S(2)}) copy-start(s32[1,20,32]{2,0,1:T(1,128)} %param.11) | copy-start | bytes 7684
  80.1 5.6 %copy-start.5 = (f32[8,16,128]{2,1,0:T(8,128)S(1)}, f32[8,16,128]{2,1,0:T(8,128)}, u32[]{:S(2)}) copy-start(f32[8,16,128]{2,1,0:T(8,128)} %copy-done.4) | copy-start | bytes 196612
  80.1 19.0 %all-to-all-start.3 = ((bf16[4,256,512]{2,1,0:T(8,128)(2,1)}), bf16[4,256,512]{2,1,0:T(8,128)(2,1)S(1)}, u32[]{:S(2)}, u32[]{:S(2)}) async-start(bf16[4,256,512]{2,1,0:T(8,128)(2,1)} %projection.3), calls=%async_computation.3 | async-start | bytes 2097152 | tf_op jit(solution)/shard_map/output_exchange/all_to_all | solution.py:348

commit v6 on v5

--- a/solution.py
+++ b/solution.py
@@ -217,20 +217,22 @@
     return fetch([t.at[:, pl.ds(start, HALF)] for t in tokens], [rows.at[s] for s in range(4)], sems)
 
 
-def project_own_kernel(mine, xh_side, xl_side, across, matrix, total, rows, sems):
-    copies = fetch_rows((mine, xh_side, xl_side, across), 0, rows, sems)
+def project_own_kernel(mine, xh_side, xl_side, across, matrix, total, later, rows, sems):
+    tokens = mine, xh_side, xl_side, across
+    copies = fetch_rows(tokens, 0, rows, sems)
+    rest = fetch_rows(tokens, HALF, later, [sems.at[4 + s] for s in range(4)])
     for s in range(4):
         copies[s].wait()
         total[s] = jnp.dot(rows[s], matrix[...], preferred_element_type=f32)
-
-
-def project_rest_kernel(mine, xh_side, xl_side, across, matrix, total, out, rows, block, sems, out_sems):
-    copies = fetch_rows((mine, xh_side, xl_side, across), HALF, rows, sems)
+    for copy in rest:
+        copy.wait()
+
+
+def project_rest_kernel(rows, matrix, total, out, block, out_sems):
     xl, xh = lax.axis_index("xl"), lax.axis_index("xh")
     slots = xl * 2 + xh, xl * 2 + 1 - xh, (1 - xl) * 2 + xh, (1 - xl) * 2 + 1 - xh
     leaving = []
     for s in range(4):
-        copies[s].wait()
         whole = total[s] + jnp.dot(rows[s], matrix[...], preferred_element_type=f32)
         block[s] = whole.astype(bf16)
         leaving += fetch([block.at[s]], [out.at[slots[s]]], [out_sems.at[s]])
@@ -325,22 +327,22 @@
         other = lax.ppermute(own, "c", swap)
 
     with jax.named_scope("projection"):
-        rows, anywhere = pltpu.VMEM((4, 256, HALF), bf16), pl.BlockSpec(memory_space=pl.ANY)
-        total = call(
+        anywhere, half_rows = pl.BlockSpec(memory_space=pl.ANY), (4, 256, HALF)
+        total, later = call(
             project_own_kernel,
-            shape((4, 256, 512), f32),
+            (shape((4, 256, 512), f32), shape(half_rows, bf16)),
             mine, xh_side, xl_side, across, own,
-            scratch=[rows, dmas((4,))],
+            scratch=[pltpu.VMEM(half_rows, bf16), dmas((8,))],
             flops=OWN_FLOPS,
             in_specs=[anywhere] * 4 + [vm],
-            out_specs=vm,
+            out_specs=(vm, vm),
         )
         partial = call(
             project_rest_kernel,
             shape((4, 256, 512), bf16),
-            mine, xh_side, xl_side, across, other, total,
-            scratch=[rows, pltpu.VMEM((4, 256, 512), bf16), dmas((4,)), dmas((4,))],
-            in_specs=[anywhere] * 4 + [vm, vm],
+            later, other, total,
+            scratch=[pltpu.VMEM((4, 256, 512), bf16), dmas((4,))],
+            in_specs=[vm] * 3,
             out_specs=far,
         )
 

time: 101 us -> 99.9 us (0.989)
  no operation moved by 1% of the time
where the time goes in v6:
time: 99.9 us; the launch traced here: 99.4 us
  starting transfers between devices  38.2 us (38%)
  waiting for transfers between devices  21.7 us (22%)
  Pallas kernels  20 us (20%)
  blocking collectives  18.5 us (19%)
    pallas_call x9, Pallas kernels, call(): pl.pallas_call(kernel, out_shape=out_shape, scratch_shapes=list(scratch),...  20 us
    all_to_all x1, blocking collectives, shards(): lax.all_to_all(jnp.broadcast_to(along_z, (4,) + along_z.shape), 'y', 0, 0)  18.5 us
    all_to_all x1, starting transfers between devices, shards(): along_z = lax.all_to_all(pieces, 'z', 0, 0)  15.2 us
    all_to_all x1, waiting for transfers between devices, shards(): back = lax.all_to_all(partial, ('xl', 'xh'), 0, 0)  10.1 us
    all_to_all x1, waiting for transfers between devices, shards(): along_z = lax.all_to_all(pieces, 'z', 0, 0)  9.38 us
    all_to_all x1, starting transfers between devices, shards(): got = lax.all_to_all(sent, ('xl', 'y'), 0, 0)  5.41 us
    ppermute x1, starting transfers between devices, shards(): xh_side = lax.ppermute(mine, 'xh', swap)  4.63 us
    ppermute x1, starting transfers between devices, shards(): across = lax.ppermute(theirs, ('xl', 'xh'), cross)  4.55 us
  transfers between devices with their start and end apart: 7, of which 4 were waited for; matrix products, arithmetic and copies ran while one was open for 0% of the time, Pallas kernels for 13%

profile of v6, /device:TPU:32, one launch (start us, length us, event | category | flops | bytes accessed | tf_op | source)
XLA Modules:
  0.0 99.4 jit_solution(18370342266770432276)
XLA Ops:
  0.6 0.0 copy-start
  0.7 4.0 %own_values.1 = (f32[8,16,128]{2,1,0:T(8,128)}, bf16[256,2560]{1,0:T(8,128)(2,1)}) custom-call(f32[1,10,64,128]{3,2,1,0:T(8,128)} %momentum.3, bf16[1,10,64,128]{3,2,1,0:T(8,128)(2,1)} %gradient.1, s32[20,1,32]{2,1,0:T(1,128)} %bitcast.2, s32[20]{0:T(128)} %bitcast.4, bf16[5,128,128]{2,1,0:T(8,128)(2,1)} %constant.2.clone.table_far.table, ...), custom_call_target="tpu_custom_call" | custom-call | bytes 524288 | tf_op jit(solution)/shard_map/own_values/pallas_call | solution.py:250
  4.6 5.4 %all-to-all-start = ((f32[8,16,128]{2,1,0:T(8,128)}), f32[8,16,128]{2,1,0:T(8,128)S(1)}, u32[]{:S(2)}, u32[]{:S(2)}) async-start(f32[8,16,128]{2,1,0:T(8,128)} %get-tuple-element.10.sent), calls=%async_computation | async-start | bytes 131072 | tf_op jit(solution)/shard_map/replica_exchange/all_to_all | solution.py:285
  10.1 4.6 %collective-permute-start = (bf16[256,2560]{1,0:T(8,128)(2,1)}, bf16[256,2560]{1,0:T(8,128)(2,1)S(1)}, u32[]{:S(2)}, u32[]{:S(2)}) collective-permute-start(bf16[256,2560]{1,0:T(8,128)(2,1)} %get-tuple-element.9.mine), channel_id=1, source_target_pairs={{0,32},{32,0},{1,33},{33,1},{2,34},{34,2},{3,35},{35,3},{4,36},{36... | collective-permute-start | bytes 3932168 | tf_op jit(solution)/shard_map/hidden_exchange/ppermute | solution.py:289
  14.7 1.7 %all-to-all-done.got.after = f32[8,16,128]{2,1,0:T(8,128)S(1)} async-done(((f32[8,16,128]{2,1,0:T(8,128)}), f32[8,16,128]{2,1,0:T(8,128)S(1)}, u32[]{:S(2)}, u32[]{:S(2)}) %all-to-all-start) | async-done | bytes 65568 | tf_op jit(solution)/shard_map/replica_exchange/all_to_all | solution.py:285
  16.4 2.5 %new_weight.2 = bf16[16,5,16,128]{3,2,1,0:T(8,128)(2,1)} custom-call(f32[8,16,128]{2,1,0:T(8,128)S(1)} %all-to-all-done.got.after, bf16[10,64,128]{2,1,0:T(8,128)(2,1)S(1)} %copy-done.8, bf16[5,128,128]{2,1,0:T(8,128)(2,1)S(1)} %copy-done), custom_call_target="tpu_custom_call" | custom-call | flops 99999997952 | tf_op jit(solution)/shard_map/new_weight/pallas_call | solution.py:250
  18.9 15.2 %all-to-all-start.1 = ((bf16[16,5,16,128]{3,2,1,0:T(8,128)(2,1)}), bf16[16,5,16,128]{3,2,1,0:T(8,128)(2,1)S(1)}, u32[]{:S(2)}, u32[]{:S(2)}) async-start(bf16[16,5,16,128]{3,2,1,0:T(8,128)(2,1)} %new_weight.2), calls=%async_computation.1 | async-start | bytes 655360 | tf_op jit(solution)/shard_map/weight_exchange/all_to_all | solution.py:322
  34.1 2.6 %hidden_exchange.1 = bf16[256,2560]{1,0:T(8,128)(2,1)} custom-call(bf16[256,5120]{1,0:T(8,128)(2,1)} %hidden_far.3, f32[8,16,128]{2,1,0:T(8,128)} %copy-done.3), custom_call_target="tpu_custom_call" | custom-call | bytes 4194304 | tf_op jit(solution)/shard_map/hidden_exchange/pallas_call | solution.py:250
  36.7 2.6 %collective-permute-start.1 = (bf16[256,2560]{1,0:T(8,128)(2,1)}, bf16[256,2560]{1,0:T(8,128)(2,1)S(1)}, u32[]{:S(2)}, u32[]{:S(2)}) collective-permute-start(bf16[256,2560]{1,0:T(8,128)(2,1)} %hidden_exchange.1), channel_id=1, source_target_pairs={{0,256},{256,0},{1,257},{257,1},{2,258},{258,2},{3,259},{259,3},{4... | collective-permute-start | bytes 3932168 | tf_op jit(solution)/shard_map/hidden_exchange/ppermute | solution.py:300
  39.2 4.6 %collective-permute-start.2 = (bf16[256,2560]{1,0:T(8,128)(2,1)}, bf16[256,2560]{1,0:T(8,128)(2,1)}, u32[]{:S(2)}, u32[]{:S(2)}) collective-permute-start(bf16[256,2560]{1,0:T(8,128)(2,1)} %hidden_exchange.1), channel_id=1, source_target_pairs={{0,288},{32,256},{256,32},{288,0},{1,289},{33,257},{257,33},{289,1... | collective-permute-start | bytes 3932168 | tf_op jit(solution)/shard_map/hidden_exchange/ppermute | solution.py:301
  43.8 9.4 %all-to-all-done.1 = bf16[16,5,16,128]{3,2,1,0:T(8,128)(2,1)S(1)} async-done(((bf16[16,5,16,128]{3,2,1,0:T(8,128)(2,1)}), bf16[16,5,16,128]{3,2,1,0:T(8,128)(2,1)S(1)}, u32[]{:S(2)}, u32[]{:S(2)}) %all-to-all-start.1) | async-done | bytes 327712 | tf_op jit(solution)/shard_map/weight_exchange/all_to_all | solution.py:322
  53.2 0.0 collective-permute-done.xh_side
  53.2 0.2 broadcast_in_dim.3
  53.4 18.5 %all_to_all.20.source = bf16[4,16,5,16,128]{4,3,2,1,0:T(8,128)(2,1)S(1)} all-to-all(bf16[4,16,5,16,128]{4,3,2,1,0:T(8,128)(2,1)S(1)} %broadcast_in_dim.3), channel_id=1, replica_groups=mesh['xl'=2,'y'=4,'xh'=2,'z'=16,'c'=2] {'y'}, dimensions={0} | all-to-all | bytes 2621440 | tf_op jit(solution)/shard_map/weight_exchange/all_to_all | solution.py:324
  71.8 0.2 weight_exchange.1.matrix
  72.1 2.1 %collective-permute-start.3 = (bf16[1280,512]{1,0:T(8,128)(2,1)S(1)}, bf16[1280,512]{1,0:T(8,128)(2,1)S(1)}, u32[]{:S(2)}, u32[]{:S(2)}) collective-permute-start(bf16[1280,512]{1,0:T(8,128)(2,1)S(1)} %weight_exchange.1.matrix), channel_id=1, source_target_pairs={{0,1},{1,0},{2,3},{3,2},{4,5},{5,4},{6,7},{7,6},{8,9},{9,8},{10,11... | collective-permute-start | bytes 3932168 | tf_op jit(solution)/shard_map/weight_exchange/ppermute | solution.py:327
  74.1 0.0 collective-permute-done.1.xl_side
  74.1 0.0 collective-permute-done.2.across
  74.1 0.0 copy-done.7
  74.2 2.4 %projection.2 = (f32[4,256,512]{2,1,0:T(8,128)S(1)}, bf16[4,256,1280]{2,1,0:T(8,128)(2,1)S(1)}) custom-call(bf16[256,2560]{1,0:T(8,128)(2,1)S(1)} %copy-done.7, bf16[256,2560]{1,0:T(8,128)(2,1)S(1)} %collective-permute-done.xh_side, bf16[256,2560]{1,0:T(8,128)(2,1)S(1)} %collective-permute-done.1.xl_side, bf16[256,2560]{1,0:T(8,128)(2,1)} %collective-permute-done.2.across, ...), custom_call_target="tpu_custom_call" | custom-call | flops 99999997952 | tf_op jit(solution)/shard_map/projection/pallas_call | solution.py:250
  76.5 0.6 collective-permute-done.3.matrix
  77.1 2.3 %projection.3 = bf16[4,256,512]{2,1,0:T(8,128)(2,1)} custom-call(bf16[4,256,1280]{2,1,0:T(8,128)(2,1)S(1)} %get-tuple-element.13.rows, bf16[1280,512]{1,0:T(8,128)(2,1)S(1)} %collective-permute-done.3.matrix, f32[4,256,512]{2,1,0:T(8,128)S(1)} %get-tuple-element.14.total), custom_call_target="tpu_custom_call" | custom-call | tf_op jit(solution)/shard_map/projection/pallas_call | solution.py:250
  79.4 0.0 copy-start.1
  79.4 0.0 copy-start.2
  79.4 0.0 copy-start.5
  79.4 0.0 copy-start.6
  79.4 0.0 copy-start.4
  79.4 3.8 %all-to-all-start.3 = ((bf16[4,256,512]{2,1,0:T(8,128)(2,1)}), bf16[4,256,512]{2,1,0:T(8,128)(2,1)S(1)}, u32[]{:S(2)}, u32[]{:S(2)}) async-start(bf16[4,256,512]{2,1,0:T(8,128)(2,1)} %projection.3), calls=%async_computation.3 | async-start | bytes 2097152 | tf_op jit(solution)/shard_map/output_exchange/all_to_all | solution.py:350
  83.2 1.9 %momentum.2 = f32[1,10,64,128]{3,2,1,0:T(8,128)} custom-call(f32[1,10,64,128]{3,2,1,0:T(8,128)S(1)} %copy-done.1, bf16[1,10,64,128]{3,2,1,0:T(8,128)(2,1)S(1)} %copy-done.2, s32[20,1,32]{2,1,0:T(1,128)S(1)} %bitcast.3, f32[8,16,128]{2,1,0:T(8,128)S(1)} %copy-done.5, bf16[5,128,128]{2,1,0:T(8,128)(2,1)S(1)} %copy-done), custom_call_target="tpu_custom_call" | custom-call | bytes 1048576 | tf_op jit(solution)/shard_map/momentum/pallas_call | solution.py:250
  85.1 3.3 %new_weight.3 = bf16[10,8,128]{2,1,0:T(8,128)(2,1)} custom-call(f32[8,16,128]{2,1,0:T(8,128)S(1)} %copy-done.4, bf16[5,128,128]{2,1,0:T(8,128)(2,1)S(1)} %copy-done), custom_call_target="tpu_custom_call" | custom-call | bytes 524288 | tf_op jit(solution)/shard_map/new_weight/pallas_call | solution.py:250
  88.4 10.1 %all-to-all-done.3.back = bf16[4,256,512]{2,1,0:T(8,128)(2,1)S(1)} async-done(((bf16[4,256,512]{2,1,0:T(8,128)(2,1)}), bf16[4,256,512]{2,1,0:T(8,128)(2,1)S(1)}, u32[]{:S(2)}, u32[]{:S(2)}) %all-to-all-start.3) | async-done | bytes 1048608 | tf_op jit(solution)/shard_map/output_exchange/all_to_all | solution.py:350
  98.5 0.9 output_exchange.1
  (11 shorter events, 0.0 us)
Async XLA Ops:
  0.6 15.8 %copy-start = (bf16[5,128,128]{2,1,0:T(8,128)(2,1)S(1)}, bf16[5,128,128]{2,1,0:T(8,128)(2,1)}, u32[]{:S(2)}) copy-start(bf16[5,128,128]{2,1,0:T(8,128)(2,1)} %constant.2.clone.table_far.table) | copy-start | bytes 491524
  0.6 15.8 %copy-start.8 = (bf16[10,64,128]{2,1,0:T(8,128)(2,1)S(1)}, bf16[10,64,128]{2,1,0:T(8,128)(2,1)}, u32[]{:S(2)}) copy-start(bf16[10,64,128]{2,1,0:T(8,128)(2,1)} %weight.1) | copy-start | bytes 491524
  4.6 11.8 %all-to-all-start = ((f32[8,16,128]{2,1,0:T(8,128)}), f32[8,16,128]{2,1,0:T(8,128)S(1)}, u32[]{:S(2)}, u32[]{:S(2)}) async-start(f32[8,16,128]{2,1,0:T(8,128)} %get-tuple-element.10.sent), calls=%async_computation | async-start | bytes 131072 | tf_op jit(solution)/shard_map/replica_exchange/all_to_all | solution.py:285
  10.1 43.1 %collective-permute-start = (bf16[256,2560]{1,0:T(8,128)(2,1)}, bf16[256,2560]{1,0:T(8,128)(2,1)S(1)}, u32[]{:S(2)}, u32[]{:S(2)}) collective-permute-start(bf16[256,2560]{1,0:T(8,128)(2,1)} %get-tuple-element.9.mine), channel_id=1, source_target_pairs={{0,32},{32,0},{1,33},{33,1},{2,34},{34,2},{3,35},{35,3},{4,36},{36... | collective-permute-start | bytes 3932168 | tf_op jit(solution)/shard_map/hidden_exchange/ppermute | solution.py:289
  16.4 2.5 %copy-start.3 = (f32[8,16,128]{2,1,0:T(8,128)}, f32[8,16,128]{2,1,0:T(8,128)S(1)}, u32[]{:S(2)}) copy-start(f32[8,16,128]{2,1,0:T(8,128)S(1)} %all-to-all-done.got.after) | copy-start | bytes 196612
  18.9 34.3 %all-to-all-start.1 = ((bf16[16,5,16,128]{3,2,1,0:T(8,128)(2,1)}), bf16[16,5,16,128]{3,2,1,0:T(8,128)(2,1)S(1)}, u32[]{:S(2)}, u32[]{:S(2)}) async-start(bf16[16,5,16,128]{3,2,1,0:T(8,128)(2,1)} %new_weight.2), calls=%async_computation.1 | async-start | bytes 655360 | tf_op jit(solution)/shard_map/weight_exchange/all_to_all | solution.py:322
  36.7 37.5 %collective-permute-start.1 = (bf16[256,2560]{1,0:T(8,128)(2,1)}, bf16[256,2560]{1,0:T(8,128)(2,1)S(1)}, u32[]{:S(2)}, u32[]{:S(2)}) collective-permute-start(bf16[256,2560]{1,0:T(8,128)(2,1)} %hidden_exchange.1), channel_id=1, source_target_pairs={{0,256},{256,0},{1,257},{257,1},{2,258},{258,2},{3,259},{259,3},{4... | collective-permute-start | bytes 3932168 | tf_op jit(solution)/shard_map/hidden_exchange/ppermute | solution.py:300
  39.2 34.9 %collective-permute-start.2 = (bf16[256,2560]{1,0:T(8,128)(2,1)}, bf16[256,2560]{1,0:T(8,128)(2,1)}, u32[]{:S(2)}, u32[]{:S(2)}) collective-permute-start(bf16[256,2560]{1,0:T(8,128)(2,1)} %hidden_exchange.1), channel_id=1, source_target_pairs={{0,288},{32,256},{256,32},{288,0},{1,289},{33,257},{257,33},{289,1... | collective-permute-start | bytes 3932168 | tf_op jit(solution)/shard_map/hidden_exchange/ppermute | solution.py:301
  71.8 2.3 %copy-start.7 = (bf16[256,2560]{1,0:T(8,128)(2,1)S(1)}, bf16[256,2560]{1,0:T(8,128)(2,1)}, u32[]{:S(2)}) copy-start(bf16[256,2560]{1,0:T(8,128)(2,1)} %get-tuple-element.9.mine) | copy-start | bytes 3932164
  72.1 5.1 %collective-permute-start.3 = (bf16[1280,512]{1,0:T(8,128)(2,1)S(1)}, bf16[1280,512]{1,0:T(8,128)(2,1)S(1)}, u32[]{:S(2)}, u32[]{:S(2)}) collective-permute-start(bf16[1280,512]{1,0:T(8,128)(2,1)S(1)} %weight_exchange.1.matrix), channel_id=1, source_target_pairs={{0,1},{1,0},{2,3},{3,2},{4,5},{5,4},{6,7},{7,6},{8,9},{9,8},{10,11... | collective-permute-start | bytes 3932168 | tf_op jit(solution)/shard_map/weight_exchange/ppermute | solution.py:327
  79.4 3.8 %copy-start.1 = (f32[1,10,64,128]{3,2,1,0:T(8,128)S(1)}, f32[1,10,64,128]{3,2,1,0:T(8,128)}, u32[]{:S(2)}) copy-start(f32[1,10,64,128]{3,2,1,0:T(8,128)} %momentum.3) | copy-start | bytes 983044
  79.4 3.8 %copy-start.2 = (bf16[1,10,64,128]{3,2,1,0:T(8,128)(2,1)S(1)}, bf16[1,10,64,128]{3,2,1,0:T(8,128)(2,1)}, u32[]{:S(2)}) copy-start(bf16[1,10,64,128]{3,2,1,0:T(8,128)(2,1)} %gradient.1) | copy-start | bytes 491524
  79.4 3.8 %copy-start.5 = (f32[8,16,128]{2,1,0:T(8,128)S(1)}, f32[8,16,128]{2,1,0:T(8,128)}, u32[]{:S(2)}) copy-start(f32[8,16,128]{2,1,0:T(8,128)} %get-tuple-element.10.sent) | copy-start | bytes 196612
  79.4 3.8 %copy-start.6 = (s32[1,20,32]{2,0,1:T(1,128)S(1)}, s32[1,20,32]{2,0,1:T(1,128)}, u32[]{:S(2)}) copy-start(s32[1,20,32]{2,0,1:T(1,128)} %param.11) | copy-start | bytes 7684
  79.4 5.7 %copy-start.4 = (f32[8,16,128]{2,1,0:T(8,128)S(1)}, f32[8,16,128]{2,1,0:T(8,128)}, u32[]{:S(2)}) copy-start(f32[8,16,128]{2,1,0:T(8,128)} %copy-done.3) | copy-start | bytes 196612
  79.4 19.0 %all-to-all-start.3 = ((bf16[4,256,512]{2,1,0:T(8,128)(2,1)}), bf16[4,256,512]{2,1,0:T(8,128)(2,1)S(1)}, u32[]{:S(2)}, u32[]{:S(2)}) async-start(bf16[4,256,512]{2,1,0:T(8,128)(2,1)} %projection.3), calls=%async_computation.3 | async-start | bytes 2097152 | tf_op jit(solution)/shard_map/output_exchange/all_to_all | solution.py:350

commit v7 on v6

--- a/solution.py
+++ b/solution.py
@@ -120,7 +120,7 @@
     momentum, gradient, indices, counts, table, parts, mine, sems, hidden_sems,
 ):
     copies = fetch(
-        (indices_far, table_far, momentum_far, gradient_far, counts_far), (indices, table, momentum, gradient, counts), sems
+        (indices_far, table_far.at[pl.ds(WIDE_T, 2)], momentum_far, gradient_far, counts_far), (indices, table, momentum, gradient, counts), sems
     )
     half = lax.axis_index("xl")
     hidden_copies = start_hidden(hidden_far, parts, hidden_sems)
@@ -274,7 +274,7 @@
             values_kernel,
             (shape((8, 16, PAIR), f32), shape((256, 2 * HALF), bf16)),
             momentum, gradient, lines, counts[0], table, hidden,
-            scratch=room(momentum, gradient, lines) + [pltpu.SMEM((2 * tiles,), jnp.int32)] + room(table) + packing + [dmas((5,)), dmas((8,))],
+            scratch=room(momentum, gradient, lines) + [pltpu.SMEM((2 * tiles,), jnp.int32), pltpu.VMEM((2, PAIR, PAIR), bf16)] + packing + [dmas((5,)), dmas((8,))],
             moved=2**19,
             limit=MOST,
             in_specs=[far] * 6,

time: 99.9 us -> 99.9 us (level)
  no operation moved by 1% of the time
where the time goes in v7:
time: 99.9 us; the launch traced here: 99.3 us
  starting transfers between devices  38.2 us (38%)
  waiting for transfers between devices  21.7 us (22%)
  Pallas kernels  19.9 us (20%)
  blocking collectives  18.5 us (19%)
    pallas_call x9, Pallas kernels, call(): pl.pallas_call(kernel, out_shape=out_shape, scratch_shapes=list(scratch),...  19.9 us
    all_to_all x1, blocking collectives, shards(): lax.all_to_all(jnp.broadcast_to(along_z, (4,) + along_z.shape), 'y', 0, 0)  18.5 us
    all_to_all x1, starting transfers between devices, shards(): along_z = lax.all_to_all(pieces, 'z', 0, 0)  15.2 us
    all_to_all x1, waiting for transfers between devices, shards(): back = lax.all_to_all(partial, ('xl', 'xh'), 0, 0)  10 us
    all_to_all x1, waiting for transfers between devices, shards(): along_z = lax.all_to_all(pieces, 'z', 0, 0)  9.38 us
    all_to_all x1, starting transfers between devices, shards(): got = lax.all_to_all(sent, ('xl', 'y'), 0, 0)  5.41 us
    ppermute x1, starting transfers between devices, shards(): xh_side = lax.ppermute(mine, 'xh', swap)  4.63 us
    ppermute x1, starting transfers between devices, shards(): across = lax.ppermute(theirs, ('xl', 'xh'), cross)  4.55 us
  transfers between devices with their start and end apart: 7, of which 4 were waited for; matrix products, arithmetic and copies ran while one was open for 0% of the time, Pallas kernels for 13%

profile of v7, /device:TPU:32, one launch (start us, length us, event | category | flops | bytes accessed | tf_op | source)
XLA Modules:
  0.0 99.3 jit_solution(12242320249875945710)
XLA Ops:
  0.6 0.0 copy-start
  0.7 3.9 %own_values.1 = (f32[8,16,128]{2,1,0:T(8,128)}, bf16[256,2560]{1,0:T(8,128)(2,1)}) custom-call(f32[1,10,64,128]{3,2,1,0:T(8,128)} %momentum.3, bf16[1,10,64,128]{3,2,1,0:T(8,128)(2,1)} %gradient.1, s32[20,1,32]{2,1,0:T(1,128)} %bitcast.2, s32[20]{0:T(128)} %bitcast.4, bf16[5,128,128]{2,1,0:T(8,128)(2,1)} %constant.2.clone.table_far.table, ...), custom_call_target="tpu_custom_call" | custom-call | bytes 524288 | tf_op jit(solution)/shard_map/own_values/pallas_call | solution.py:250
  4.6 5.4 %all-to-all-start = ((f32[8,16,128]{2,1,0:T(8,128)}), f32[8,16,128]{2,1,0:T(8,128)S(1)}, u32[]{:S(2)}, u32[]{:S(2)}) async-start(f32[8,16,128]{2,1,0:T(8,128)} %get-tuple-element.10.sent), calls=%async_computation | async-start | bytes 131072 | tf_op jit(solution)/shard_map/replica_exchange/all_to_all | solution.py:285
  10.0 4.6 %collective-permute-start = (bf16[256,2560]{1,0:T(8,128)(2,1)}, bf16[256,2560]{1,0:T(8,128)(2,1)S(1)}, u32[]{:S(2)}, u32[]{:S(2)}) collective-permute-start(bf16[256,2560]{1,0:T(8,128)(2,1)} %get-tuple-element.9.mine), channel_id=1, source_target_pairs={{0,32},{32,0},{1,33},{33,1},{2,34},{34,2},{3,35},{35,3},{4,36},{36... | collective-permute-start | bytes 3932168 | tf_op jit(solution)/shard_map/hidden_exchange/ppermute | solution.py:289
  14.6 1.7 %all-to-all-done.got.after = f32[8,16,128]{2,1,0:T(8,128)S(1)} async-done(((f32[8,16,128]{2,1,0:T(8,128)}), f32[8,16,128]{2,1,0:T(8,128)S(1)}, u32[]{:S(2)}, u32[]{:S(2)}) %all-to-all-start) | async-done | bytes 65568 | tf_op jit(solution)/shard_map/replica_exchange/all_to_all | solution.py:285
  16.4 0.0 copy-done
  16.4 2.5 %new_weight.2 = bf16[16,5,16,128]{3,2,1,0:T(8,128)(2,1)} custom-call(f32[8,16,128]{2,1,0:T(8,128)S(1)} %all-to-all-done.got.after, bf16[10,64,128]{2,1,0:T(8,128)(2,1)S(1)} %copy-done.8, bf16[5,128,128]{2,1,0:T(8,128)(2,1)S(1)} %copy-done), custom_call_target="tpu_custom_call" | custom-call | flops 99999997952 | tf_op jit(solution)/shard_map/new_weight/pallas_call | solution.py:250
  18.8 0.0 copy-done.3
  18.8 15.2 %all-to-all-start.1 = ((bf16[16,5,16,128]{3,2,1,0:T(8,128)(2,1)}), bf16[16,5,16,128]{3,2,1,0:T(8,128)(2,1)S(1)}, u32[]{:S(2)}, u32[]{:S(2)}) async-start(bf16[16,5,16,128]{3,2,1,0:T(8,128)(2,1)} %new_weight.2), calls=%async_computation.1 | async-start | bytes 655360 | tf_op jit(solution)/shard_map/weight_exchange/all_to_all | solution.py:322
  34.0 2.6 %hidden_exchange.1 = bf16[256,2560]{1,0:T(8,128)(2,1)} custom-call(bf16[256,5120]{1,0:T(8,128)(2,1)} %hidden_far.3, f32[8,16,128]{2,1,0:T(8,128)} %copy-done.3), custom_call_target="tpu_custom_call" | custom-call | bytes 4194304 | tf_op jit(solution)/shard_map/hidden_exchange/pallas_call | solution.py:250
  36.6 2.6 %collective-permute-start.1 = (bf16[256,2560]{1,0:T(8,128)(2,1)}, bf16[256,2560]{1,0:T(8,128)(2,1)S(1)}, u32[]{:S(2)}, u32[]{:S(2)}) collective-permute-start(bf16[256,2560]{1,0:T(8,128)(2,1)} %hidden_exchange.1), channel_id=1, source_target_pairs={{0,256},{256,0},{1,257},{257,1},{2,258},{258,2},{3,259},{259,3},{4... | collective-permute-start | bytes 3932168 | tf_op jit(solution)/shard_map/hidden_exchange/ppermute | solution.py:300
  39.2 4.5 %collective-permute-start.2 = (bf16[256,2560]{1,0:T(8,128)(2,1)}, bf16[256,2560]{1,0:T(8,128)(2,1)}, u32[]{:S(2)}, u32[]{:S(2)}) collective-permute-start(bf16[256,2560]{1,0:T(8,128)(2,1)} %hidden_exchange.1), channel_id=1, source_target_pairs={{0,288},{32,256},{256,32},{288,0},{1,289},{33,257},{257,33},{289,1... | collective-permute-start | bytes 3932168 | tf_op jit(solution)/shard_map/hidden_exchange/ppermute | solution.py:301
  43.8 9.4 %all-to-all-done.1 = bf16[16,5,16,128]{3,2,1,0:T(8,128)(2,1)S(1)} async-done(((bf16[16,5,16,128]{3,2,1,0:T(8,128)(2,1)}), bf16[16,5,16,128]{3,2,1,0:T(8,128)(2,1)S(1)}, u32[]{:S(2)}, u32[]{:S(2)}) %all-to-all-start.1) | async-done | bytes 327712 | tf_op jit(solution)/shard_map/weight_exchange/all_to_all | solution.py:322
  53.1 0.0 collective-permute-done.xh_side
  53.1 0.2 broadcast_in_dim.3
  53.3 18.5 %all_to_all.20.source = bf16[4,16,5,16,128]{4,3,2,1,0:T(8,128)(2,1)S(1)} all-to-all(bf16[4,16,5,16,128]{4,3,2,1,0:T(8,128)(2,1)S(1)} %broadcast_in_dim.3), channel_id=1, replica_groups=mesh['xl'=2,'y'=4,'xh'=2,'z'=16,'c'=2] {'y'}, dimensions={0} | all-to-all | bytes 2621440 | tf_op jit(solution)/shard_map/weight_exchange/all_to_all | solution.py:324
  71.8 0.2 weight_exchange.1.matrix
  72.0 2.1 %collective-permute-start.3 = (bf16[1280,512]{1,0:T(8,128)(2,1)S(1)}, bf16[1280,512]{1,0:T(8,128)(2,1)S(1)}, u32[]{:S(2)}, u32[]{:S(2)}) collective-permute-start(bf16[1280,512]{1,0:T(8,128)(2,1)S(1)} %weight_exchange.1.matrix), channel_id=1, source_target_pairs={{0,1},{1,0},{2,3},{3,2},{4,5},{5,4},{6,7},{7,6},{8,9},{9,8},{10,11... | collective-permute-start | bytes 3932168 | tf_op jit(solution)/shard_map/weight_exchange/ppermute | solution.py:327
  74.1 0.0 collective-permute-done.1.xl_side
  74.1 0.0 collective-permute-done.2.across
  74.1 2.4 %projection.2 = (f32[4,256,512]{2,1,0:T(8,128)S(1)}, bf16[4,256,1280]{2,1,0:T(8,128)(2,1)S(1)}) custom-call(bf16[256,2560]{1,0:T(8,128)(2,1)S(1)} %copy-done.7, bf16[256,2560]{1,0:T(8,128)(2,1)S(1)} %collective-permute-done.xh_side, bf16[256,2560]{1,0:T(8,128)(2,1)S(1)} %collective-permute-done.1.xl_side, bf16[256,2560]{1,0:T(8,128)(2,1)} %collective-permute-done.2.across, ...), custom_call_target="tpu_custom_call" | custom-call | flops 99999997952 | tf_op jit(solution)/shard_map/projection/pallas_call | solution.py:250
  76.5 0.6 collective-permute-done.3.matrix
  77.1 2.3 %projection.3 = bf16[4,256,512]{2,1,0:T(8,128)(2,1)} custom-call(bf16[4,256,1280]{2,1,0:T(8,128)(2,1)S(1)} %get-tuple-element.13.rows, bf16[1280,512]{1,0:T(8,128)(2,1)S(1)} %collective-permute-done.3.matrix, f32[4,256,512]{2,1,0:T(8,128)S(1)} %get-tuple-element.14.total), custom_call_target="tpu_custom_call" | custom-call | tf_op jit(solution)/shard_map/projection/pallas_call | solution.py:250
  79.3 0.0 copy-start.1
  79.3 0.0 copy-start.2
  79.4 0.0 copy-start.5
  79.4 0.0 copy-start.6
  79.4 3.8 %all-to-all-start.3 = ((bf16[4,256,512]{2,1,0:T(8,128)(2,1)}), bf16[4,256,512]{2,1,0:T(8,128)(2,1)S(1)}, u32[]{:S(2)}, u32[]{:S(2)}) async-start(bf16[4,256,512]{2,1,0:T(8,128)(2,1)} %projection.3), calls=%async_computation.3 | async-start | bytes 2097152 | tf_op jit(solution)/shard_map/output_exchange/all_to_all | solution.py:350
  83.2 1.9 %momentum.2 = f32[1,10,64,128]{3,2,1,0:T(8,128)} custom-call(f32[1,10,64,128]{3,2,1,0:T(8,128)S(1)} %copy-done.1, bf16[1,10,64,128]{3,2,1,0:T(8,128)(2,1)S(1)} %copy-done.2, s32[20,1,32]{2,1,0:T(1,128)S(1)} %bitcast.3, f32[8,16,128]{2,1,0:T(8,128)S(1)} %copy-done.5, bf16[5,128,128]{2,1,0:T(8,128)(2,1)S(1)} %copy-done), custom_call_target="tpu_custom_call" | custom-call | bytes 1048576 | tf_op jit(solution)/shard_map/momentum/pallas_call | solution.py:250
  85.0 3.3 %new_weight.3 = bf16[10,8,128]{2,1,0:T(8,128)(2,1)} custom-call(f32[8,16,128]{2,1,0:T(8,128)S(1)} %copy-done.4, bf16[5,128,128]{2,1,0:T(8,128)(2,1)S(1)} %copy-done), custom_call_target="tpu_custom_call" | custom-call | bytes 524288 | tf_op jit(solution)/shard_map/new_weight/pallas_call | solution.py:250
  88.4 10.0 %all-to-all-done.3.back = bf16[4,256,512]{2,1,0:T(8,128)(2,1)S(1)} async-done(((bf16[4,256,512]{2,1,0:T(8,128)(2,1)}), bf16[4,256,512]{2,1,0:T(8,128)(2,1)S(1)}, u32[]{:S(2)}, u32[]{:S(2)}) %all-to-all-start.3) | async-done | bytes 1048608 | tf_op jit(solution)/shard_map/output_exchange/all_to_all | solution.py:350
  98.4 0.9 output_exchange.1
  (11 shorter events, 0.0 us)
Async XLA Ops:
  0.6 15.7 %copy-start = (bf16[5,128,128]{2,1,0:T(8,128)(2,1)S(1)}, bf16[5,128,128]{2,1,0:T(8,128)(2,1)}, u32[]{:S(2)}) copy-start(bf16[5,128,128]{2,1,0:T(8,128)(2,1)} %constant.2.clone.table_far.table) | copy-start | bytes 491524
  0.6 15.7 %copy-start.8 = (bf16[10,64,128]{2,1,0:T(8,128)(2,1)S(1)}, bf16[10,64,128]{2,1,0:T(8,128)(2,1)}, u32[]{:S(2)}) copy-start(bf16[10,64,128]{2,1,0:T(8,128)(2,1)} %weight.1) | copy-start | bytes 491524
  4.6 11.8 %all-to-all-start = ((f32[8,16,128]{2,1,0:T(8,128)}), f32[8,16,128]{2,1,0:T(8,128)S(1)}, u32[]{:S(2)}, u32[]{:S(2)}) async-start(f32[8,16,128]{2,1,0:T(8,128)} %get-tuple-element.10.sent), calls=%async_computation | async-start | bytes 131072 | tf_op jit(solution)/shard_map/replica_exchange/all_to_all | solution.py:285
  10.0 43.1 %collective-permute-start = (bf16[256,2560]{1,0:T(8,128)(2,1)}, bf16[256,2560]{1,0:T(8,128)(2,1)S(1)}, u32[]{:S(2)}, u32[]{:S(2)}) collective-permute-start(bf16[256,2560]{1,0:T(8,128)(2,1)} %get-tuple-element.9.mine), channel_id=1, source_target_pairs={{0,32},{32,0},{1,33},{33,1},{2,34},{34,2},{3,35},{35,3},{4,36},{36... | collective-permute-start | bytes 3932168 | tf_op jit(solution)/shard_map/hidden_exchange/ppermute | solution.py:289
  16.4 2.5 %copy-start.3 = (f32[8,16,128]{2,1,0:T(8,128)}, f32[8,16,128]{2,1,0:T(8,128)S(1)}, u32[]{:S(2)}) copy-start(f32[8,16,128]{2,1,0:T(8,128)S(1)} %all-to-all-done.got.after) | copy-start | bytes 196612
  18.8 34.3 %all-to-all-start.1 = ((bf16[16,5,16,128]{3,2,1,0:T(8,128)(2,1)}), bf16[16,5,16,128]{3,2,1,0:T(8,128)(2,1)S(1)}, u32[]{:S(2)}, u32[]{:S(2)}) async-start(bf16[16,5,16,128]{3,2,1,0:T(8,128)(2,1)} %new_weight.2), calls=%async_computation.1 | async-start | bytes 655360 | tf_op jit(solution)/shard_map/weight_exchange/all_to_all | solution.py:322
  36.6 37.4 %collective-permute-start.1 = (bf16[256,2560]{1,0:T(8,128)(2,1)}, bf16[256,2560]{1,0:T(8,128)(2,1)S(1)}, u32[]{:S(2)}, u32[]{:S(2)}) collective-permute-start(bf16[256,2560]{1,0:T(8,128)(2,1)} %hidden_exchange.1), channel_id=1, source_target_pairs={{0,256},{256,0},{1,257},{257,1},{2,258},{258,2},{3,259},{259,3},{4... | collective-permute-start | bytes 3932168 | tf_op jit(solution)/shard_map/hidden_exchange/ppermute | solution.py:300
  39.2 34.9 %collective-permute-start.2 = (bf16[256,2560]{1,0:T(8,128)(2,1)}, bf16[256,2560]{1,0:T(8,128)(2,1)}, u32[]{:S(2)}, u32[]{:S(2)}) collective-permute-start(bf16[256,2560]{1,0:T(8,128)(2,1)} %hidden_exchange.1), channel_id=1, source_target_pairs={{0,288},{32,256},{256,32},{288,0},{1,289},{33,257},{257,33},{289,1... | collective-permute-start | bytes 3932168 | tf_op jit(solution)/shard_map/hidden_exchange/ppermute | solution.py:301
  71.8 2.3 %copy-start.7 = (bf16[256,2560]{1,0:T(8,128)(2,1)S(1)}, bf16[256,2560]{1,0:T(8,128)(2,1)}, u32[]{:S(2)}) copy-start(bf16[256,2560]{1,0:T(8,128)(2,1)} %get-tuple-element.9.mine) | copy-start | bytes 3932164
  72.0 5.1 %collective-permute-start.3 = (bf16[1280,512]{1,0:T(8,128)(2,1)S(1)}, bf16[1280,512]{1,0:T(8,128)(2,1)S(1)}, u32[]{:S(2)}, u32[]{:S(2)}) collective-permute-start(bf16[1280,512]{1,0:T(8,128)(2,1)S(1)} %weight_exchange.1.matrix), channel_id=1, source_target_pairs={{0,1},{1,0},{2,3},{3,2},{4,5},{5,4},{6,7},{7,6},{8,9},{9,8},{10,11... | collective-permute-start | bytes 3932168 | tf_op jit(solution)/shard_map/weight_exchange/ppermute | solution.py:327
  79.3 3.8 %copy-start.1 = (f32[1,10,64,128]{3,2,1,0:T(8,128)S(1)}, f32[1,10,64,128]{3,2,1,0:T(8,128)}, u32[]{:S(2)}) copy-start(f32[1,10,64,128]{3,2,1,0:T(8,128)} %momentum.3) | copy-start | bytes 983044
  79.3 3.8 %copy-start.2 = (bf16[1,10,64,128]{3,2,1,0:T(8,128)(2,1)S(1)}, bf16[1,10,64,128]{3,2,1,0:T(8,128)(2,1)}, u32[]{:S(2)}) copy-start(bf16[1,10,64,128]{3,2,1,0:T(8,128)(2,1)} %gradient.1) | copy-start | bytes 491524
  79.4 3.8 %copy-start.5 = (f32[8,16,128]{2,1,0:T(8,128)S(1)}, f32[8,16,128]{2,1,0:T(8,128)}, u32[]{:S(2)}) copy-start(f32[8,16,128]{2,1,0:T(8,128)} %get-tuple-element.10.sent) | copy-start | bytes 196612
  79.4 3.8 %copy-start.6 = (s32[1,20,32]{2,0,1:T(1,128)S(1)}, s32[1,20,32]{2,0,1:T(1,128)}, u32[]{:S(2)}) copy-start(s32[1,20,32]{2,0,1:T(1,128)} %param.11) | copy-start | bytes 7684
  79.4 5.7 %copy-start.4 = (f32[8,16,128]{2,1,0:T(8,128)S(1)}, f32[8,16,128]{2,1,0:T(8,128)}, u32[]{:S(2)}) copy-start(f32[8,16,128]{2,1,0:T(8,128)} %copy-done.3) | copy-start | bytes 196612
  79.4 19.0 %all-to-all-start.3 = ((bf16[4,256,512]{2,1,0:T(8,128)(2,1)}), bf16[4,256,512]{2,1,0:T(8,128)(2,1)S(1)}, u32[]{:S(2)}, u32[]{:S(2)}) async-start(bf16[4,256,512]{2,1,0:T(8,128)(2,1)} %projection.3), calls=%async_computation.3 | async-start | bytes 2097152 | tf_op jit(solution)/shard_map/output_exchange/all_to_all | solution.py:350
